TPU v7x, 32 devices: a whole 2x2x4 slice. The times are simulated.
32 devices in a mesh: blk: 4 (over y, x), regroup: 4 (over z), hid: 2 (over core).
Axes of the slice: x: 2, y: 2, z: 4, core: 2. Of those that a mesh axis runs over, the one named last changes fastest.
Arguments:
- tokens: bfloat16 [256, 6144], P(('blk', 'regroup')), may hold values from -6 to 6
- kinds: int32 [256], P(('blk', 'regroup')), may hold values from 0 to 7
- slots: int32 [16, 16], P(('blk', 'regroup')), may hold values from 0 to 15, each once within a row
- gains: float32 [8, 6144], replicated, may hold values from 0.1 to 1.9
- gate_weight: bfloat16 [6144, 16384], P(None, ('blk', 'hid')), may hold values from -0.078125 to 0.078125
- up_weight: bfloat16 [6144, 16384], P(None, ('blk', 'hid')), may hold values from -0.078125 to 0.078125
- down_weight: bfloat16 [16384, 6144], P(('blk', 'hid')), may hold values from -0.0625 to 0.0625
Outputs:
- mixed: bfloat16 [256, 6144], P(('blk', 'regroup'), 'hid')
Inputs may be any that keep to these rules, and one draw needn't show every extreme that they name: Each row of slots names every number 0 to 15 once.
All inputs are finite; a program needn't handle non-finite values.
Results may differ from a plain program's by a relative error of at most 0.019.
Values may be sent and summed in bfloat16 or wider, within the bound.
No kernel may reach another device: no remote copies, remote signals or barrier semaphores. Data moves between devices by JAX's collectives and lax.ppermute only.
A program may use at most 128 MiB of HBM per device.

v0:
```python
import jax
import jax.numpy as jnp
from jax import lax
from jax.sharding import PartitionSpec as P

epsilon = 1e-05


def on_device(tokens, kinds, slots, gains, gate_weight, up_weight, down_weight):
    row_count = tokens.shape[0]
    feature_width = tokens.shape[1]
    lane_count = lax.axis_size("regroup")
    float_rows = tokens.astype(jnp.float32)
    row_scale = lax.rsqrt(jnp.mean(float_rows * float_rows, axis=1, keepdims=True) + epsilon)
    choose = (kinds[:, None] == jnp.arange(gains.shape[0], dtype=jnp.int32)[None, :]).astype(
        jnp.float32
    )
    row_gain = jnp.dot(choose, gains, precision=lax.Precision.HIGHEST)
    normed = (float_rows * row_scale * row_gain).astype(jnp.bfloat16)
    placing = (slots[0][None, :] == jnp.arange(row_count, dtype=jnp.int32)[:, None]).astype(
        jnp.bfloat16
    )
    ordered = jnp.dot(placing, normed, preferred_element_type=jnp.float32).astype(jnp.bfloat16)
    by_lane = ordered.reshape(row_count // lane_count, lane_count, feature_width)
    arranged = lax.all_to_all(by_lane, "regroup", split_axis=1, concat_axis=1, tiled=True).reshape(
        row_count, feature_width
    )
    panel = lax.all_gather(arranged, "blk", axis=0, tiled=True)
    gate_proj = jnp.dot(panel, gate_weight, preferred_element_type=jnp.float32)
    up_proj = jnp.dot(panel, up_weight, preferred_element_type=jnp.float32)
    hidden = (jax.nn.silu(gate_proj) * up_proj).astype(jnp.bfloat16)
    block_total = lax.psum_scatter(
        jnp.dot(hidden, down_weight, preferred_element_type=jnp.float32).astype(jnp.bfloat16),
        "blk",
        scatter_dimension=0,
        tiled=True,
    )
    summed = lax.psum_scatter(block_total, "hid", scatter_dimension=1, tiled=True).astype(
        jnp.float32
    )
    return summed.astype(jnp.bfloat16)


def solution(mesh):
    placed = (
        P(("blk", "regroup"), None),
        P(("blk", "regroup")),
        P(("blk", "regroup"), None),
        P(),
        P(None, ("blk", "hid")),
        P(None, ("blk", "hid")),
        P(("blk", "hid"), None),
    )
    return jax.shard_map(
        on_device,
        mesh=mesh,
        in_specs=placed,
        out_specs=P(("blk", "regroup"), "hid"),
        check_vma=False,
    )
```

profile of v0, /device:TPU:0, one launch (start us, length us, event | category | flops | bytes accessed | tf_op | source)
XLA Modules:
  0.0 107.6 jit_solution(6066564869388138009)
XLA Ops:
  6.5 0.0 copy-start
  6.5 0.0 reduce-scatter.3.cloned.1.call-start
  6.5 1.1 %fusion.7 = f32[16]{0:T(128)S(1)} fusion(bf16[16,6144]{1,0:T(8,128)(2,1)} %param.7), kind=kLoop, calls=%fused_computation.13 | loop fusion | flops 294896 | bytes 196672 | tf_op jit(solution)/shard_map/reduce_sum | solution.py:14
  7.7 0.0 copy-done
  7.7 1.3 %fusion = bf16[16,6144]{1,0:T(8,128)(2,1)S(1)} fusion(f32[8,6144]{1,0:T(8,128)S(1)} %copy-done, bf16[16,6144]{1,0:T(8,128)(2,1)} %param.7, f32[16]{0:T(128)S(1)} %add_rsqrt_fusion, s32[16]{0:T(128)} %param.8), kind=kOutput, calls=%fused_computation.2 | convolution fusion | flops 9830528 | bytes 589952 | tf_op jit(solution)/shard_map/dot_general | solution.py:18
  9.0 0.8 convolution_convert_fusion.1
  9.9 0.1 reshape.15
  9.9 0.2 copy.9
  10.1 13.6 %all_to_all.5 = bf16[4,4,6144]{2,0,1:T(4,128)(2,1)S(1)} all-to-all(bf16[4,4,6144]{2,0,1:T(4,128)(2,1)S(1)} %copy.9), channel_id=1, replica_groups=mesh['blk'=4,'regroup'=4,'hid'=2] {'regroup'}, dimensions={1} | all-to-all | bytes 393216 | tf_op jit(solution)/shard_map/all_to_all | solution.py:25
  23.7 0.2 copy.10
  23.9 12.1 %all_gather.3 = bf16[64,6144]{1,0:T(8,128)(2,1)S(1)} all-gather(bf16[16,6144]{1,0:T(8,128)(2,1)S(1)} %reshape.16), channel_id=1, replica_groups=mesh['blk'=4,'regroup'=4,'hid'=2] {'blk'}, dimensions={0}, use_global_device_ids=true | all-gather | bytes 983040 | tf_op jit(solution)/shard_map/all_gather | solution.py:28
  36.0 10.5 %fusion.12 = f32[64,2048]{1,0:T(8,128)S(1)} fusion(bf16[64,6144]{1,0:T(8,128)(2,1)S(1)} %all_gather.3, bf16[6144,2048]{1,0:T(8,128)(2,1)} %param.11), kind=kOutput, calls=%fused_computation.21 | convolution fusion | flops 1610612736 | bytes 26476544 | tf_op jit(solution)/shard_map/dot_general | solution.py:29
  46.5 20.8 %convolution_convert_fusion = bf16[64,6144]{1,0:T(8,128)(2,1)} fusion(bf16[2048,6144]{1,0:T(8,128)(2,1)} %param.13, bf16[64,6144]{1,0:T(8,128)(2,1)S(1)} %all_gather.3, bf16[6144,2048]{1,0:T(8,128)(2,1)} %param.12, f32[64,2048]{1,0:T(8,128)S(1)} %fusion.12), kind=kOutput, calls=%fused_computation | convolution fusion | flops 3222405120 | bytes 52428800 | tf_op jit(solution)/shard_map/dot_general | solution.py:33
  67.3 0.0 reduce-scatter.3.cloned.1.call-update
  67.3 0.0 reduce-scatter.5.cloned.1.call-start
  67.4 23.6 %reduce-scatter.3.cloned.1.call-done = bf16[16,6144]{1,0:T(8,128)(2,1)} async-done(((bf16[64,6144]{1,0:T(8,128)(2,1)}), bf16[16,6144]{1,0:T(8,128)(2,1)}) %reduce-scatter.3.cloned.1.call-update) | async-done | bytes 196624 | tf_op jit(solution)/shard_map/reduce_scatter | solution.py:32
  91.0 0.0 reduce-scatter.5.cloned.1.call-update
  91.0 9.8 %reduce-scatter.5.cloned.1.call-done = bf16[16,3072]{1,0:T(8,128)(2,1)} async-done(((bf16[16,6144]{1,0:T(8,128)(2,1)}), bf16[16,3072]{1,0:T(8,128)(2,1)}) %reduce-scatter.5.cloned.1.call-update) | async-done | bytes 98320 | tf_op jit(solution)/shard_map/reduce_scatter | solution.py:38
  (2 shorter events, 0.1 us)
Async XLA Ops:
  6.5 1.1 %copy-start = (f32[8,6144]{1,0:T(8,128)S(1)}, f32[8,6144]{1,0:T(8,128)}, u32[]{:S(2)}) copy-start(f32[8,6144]{1,0:T(8,128)} %param.10) | copy-start | bytes 589828
  6.5 84.5 %reduce-scatter.3.cloned.1.call-start = ((), (), s32[]{:S(2)}) async-start(), calls=%async_computation.3 | async-start | bytes 983040 | tf_op jit(solution)/shard_map/reduce_scatter | solution.py:32
  67.3 33.4 %reduce-scatter.5.cloned.1.call-start = ((), (), s32[]{:S(2)}) async-start(), calls=%async_computation.4 | async-start | bytes 294912 | tf_op jit(solution)/shard_map/reduce_scatter | solution.py:38
Sparse Core Ops, SparseCore 0:
  67.5 23.4 reduce-scatter.2
  93.2 7.5 reduce-scatter.4
where the time goes:
time: 108 us
  matrix products  33.4 us (31%)
  waiting for transfers between devices  33.4 us (31%)
  blocking collectives  25.7 us (24%)
  between operations  13.5 us (12%)
  other arithmetic  1.14 us (1%)
    reduce_scatter x1, waiting for transfers between devices, on_device(): lax.psum_scatter(jnp.dot(hidden, down_weight, preferred_element_type=jnp....  23.6 us
    dot_general x1, matrix products, on_device(): jnp.dot(hidden, down_weight, preferred_element_type=jnp.float32)  20.8 us
    all_to_all x1, blocking collectives, on_device(): lax.all_to_all(by_lane, 'regroup', split_axis=1, concat_axis=1, tiled=True)  13.6 us
    all_gather x1, blocking collectives, on_device(): panel = lax.all_gather(arranged, 'blk', axis=0, tiled=True)  12.1 us
    dot_general x1, matrix products, on_device(): gate_proj = jnp.dot(panel, gate_weight, preferred_element_type=jnp.float32)  10.5 us
    reduce_scatter x1, waiting for transfers between devices, on_device(): lax.psum_scatter(block_total, 'hid', scatter_dimension=1, tiled=True)  9.78 us
  transfers between devices with their start and end apart: 2, of which 2 were waited for; matrix products, arithmetic and copies ran while one was open for 0% of the time, Pallas kernels for 0%

commit v1 on v0

v1 whole, which is shorter than its diff:
```python
import functools

import jax
import jax.numpy as jnp
from jax import lax
from jax.experimental import pallas as pl
from jax.experimental.pallas import tpu as pltpu
from jax.sharding import PartitionSpec as P

epsilon = 1e-05
MIB = 1 << 20

IN_HBM = pl.BlockSpec(memory_space=pltpu.HBM)
ANYWHERE = pl.BlockSpec(memory_space=pl.ANY)
IN_VMEM = pl.BlockSpec(memory_space=pltpu.VMEM)
IN_SMEM = pl.BlockSpec(memory_space=pltpu.SMEM)


def log2(number):
    bits = number.bit_length() - 1
    assert 1 << bits == number
    return bits


def exchange(array, axis, step):
    count = lax.axis_size(axis)
    log2(count)
    return lax.ppermute(array, axis, [(i, i ^ step) for i in range(count)])


def norm_kernel(lanes, tokens_ref, kinds_ref, slots_ref, gains_ref, out_ref):
    rows = tokens_ref.shape[0]
    rounds = rows // lanes
    x = tokens_ref[...].astype(jnp.float32)
    row_scale = lax.rsqrt(jnp.mean(x * x, axis=1, keepdims=True) + epsilon)
    at = lax.broadcasted_iota(jnp.int32, (rows, 1), 0)
    kind = jnp.zeros((rows, 1), jnp.int32)
    for i in range(rows):
        kind = jnp.where(at == i, kinds_ref[i], kind)
    gain = jnp.broadcast_to(gains_ref[0:1, :], x.shape)
    for c in range(1, gains_ref.shape[0]):
        gain = jnp.where(kind == c, gains_ref[c : c + 1, :], gain)
    normed = (x * row_scale * gain).astype(jnp.bfloat16)
    me = lax.axis_index("regroup")
    target = lax.broadcasted_iota(jnp.int32, (rows, rows), 0)
    lane = jnp.bitwise_xor(lax.shift_right_logical(target, log2(rounds)), me)
    slot = jnp.bitwise_and(target, rounds - 1) * lanes + lane
    placing = (jnp.broadcast_to(slots_ref[0:1, :], slot.shape) == slot).astype(jnp.bfloat16)
    out_ref[...] = jnp.dot(placing, normed, preferred_element_type=jnp.float32).astype(jnp.bfloat16)


def norm(tokens, kinds, slots, gains):
    return pl.pallas_call(
        functools.partial(norm_kernel, lax.axis_size("regroup")),
        out_shape=jax.ShapeDtypeStruct(tokens.shape, jnp.bfloat16),
        in_specs=[IN_VMEM, IN_SMEM, IN_VMEM, IN_VMEM],
        out_specs=IN_VMEM,
        compiler_params=pltpu.CompilerParams(vmem_limit_bytes=8 * MIB),
        name="norm",
    )(tokens, kinds, slots, gains)


def early_kernel(gate_ref, up_ref, gate_out, up_out, sems):
    width = gate_out.shape[1]
    copies = [
        pltpu.make_async_copy(src.at[:, pl.ds(0, width)], dst, sems.at[i])
        for i, (src, dst) in enumerate(((gate_ref, gate_out), (up_ref, up_out)))
    ]
    for copy in copies:
        copy.start()
    for copy in copies:
        copy.wait()


def early(gate_weight, up_weight, width):
    depth = gate_weight.shape[0]
    held = pltpu.VMEM((depth, width), jnp.bfloat16)
    return pl.pallas_call(
        early_kernel,
        out_shape=(held, held),
        in_specs=[IN_HBM, IN_HBM],
        out_specs=(IN_VMEM, IN_VMEM),
        scratch_shapes=[pltpu.SemaphoreType.DMA((2,))],
        compiler_params=pltpu.CompilerParams(vmem_limit_bytes=1 * MIB),
        cost_estimate=pl.CostEstimate(
            flops=0, bytes_accessed=8 * depth * width, transcendentals=0
        ),
        name="early",
    )(gate_weight, up_weight)


def by_steps(rows, blocks, lanes):
    rounds = rows // (blocks * lanes)
    r = lax.broadcasted_iota(jnp.int32, (rows, rows), 0)
    c = lax.broadcasted_iota(jnp.int32, (rows, rows), 1)
    m = jnp.bitwise_and(r, rounds - 1)
    rest = lax.shift_right_logical(r, log2(rounds))
    block = jnp.bitwise_and(rest, blocks - 1)
    lane = lax.shift_right_logical(rest, log2(blocks))
    return (c == (block * lanes + lane) * rounds + m).astype(jnp.bfloat16)


def by_place(rows, blocks, lanes, me):
    rounds = rows // (blocks * lanes)
    r = lax.broadcasted_iota(jnp.int32, (rows, rows), 0)
    c = lax.broadcasted_iota(jnp.int32, (rows, rows), 1)
    step = jnp.bitwise_xor(jnp.bitwise_and(r, lanes - 1), me)
    rest = lax.shift_right_logical(r, log2(lanes))
    m = jnp.bitwise_and(rest, rounds - 1)
    block = lax.shift_right_logical(rest, log2(rounds))
    return (c == (step * blocks + block) * rounds + m).astype(jnp.bfloat16)


def hidden_kernel(blocks, lanes, chunk, held_chunks, parts, slots, *refs):
    panel_refs = refs[:blocks]
    gate_held, up_held, gate_ref, up_ref = refs[blocks : blocks + 4]
    out_refs = refs[blocks + 4 : blocks + 4 + lanes]
    panel, gate_sum, up_sum, ring, sems = refs[blocks + 4 + lanes :]
    rows, depth = panel.shape
    part = depth // parts
    each = rows // blocks
    chunks = gate_ref.shape[1] // chunk
    units = [(c, p) for c in range(held_chunks, chunks) for p in range(parts)]

    def copies(n):
        c, p = units[n]
        return [
            pltpu.make_async_copy(
                src.at[pl.ds(p * part, part), pl.ds(c * chunk, chunk)],
                ring.at[n % slots, i],
                sems.at[n % slots, i],
            )
            for i, src in enumerate((gate_ref, up_ref))
        ]

    for n in range(min(slots, len(units))):
        for copy in copies(n):
            copy.start()
    for step, ref in enumerate(panel_refs):
        panel[step * each : (step + 1) * each, :] = ref[...]
    order = by_steps(rows, blocks, lanes)

    def finish(c, gate, up):
        hidden = (gate / (1.0 + jnp.exp(-gate)) * up).astype(jnp.bfloat16)
        placed = jnp.dot(order, hidden, preferred_element_type=jnp.float32).astype(jnp.bfloat16)
        span = rows // lanes
        for lane, ref in enumerate(out_refs):
            ref[:, c * chunk : (c + 1) * chunk] = placed[lane * span : (lane + 1) * span, :]

    for c in range(held_chunks):
        columns = slice(c * chunk, (c + 1) * chunk)
        x = panel[...]
        gate = jnp.dot(x, gate_held[:, columns], preferred_element_type=jnp.float32)
        up = jnp.dot(x, up_held[:, columns], preferred_element_type=jnp.float32)
        finish(c, gate, up)
    for n, (c, p) in enumerate(units):
        for copy in copies(n):
            copy.wait()
        x = panel[:, p * part : (p + 1) * part]
        gate = jnp.dot(x, ring[n % slots, 0], preferred_element_type=jnp.float32)
        up = jnp.dot(x, ring[n % slots, 1], preferred_element_type=jnp.float32)
        if n + slots < len(units):
            for copy in copies(n + slots):
                copy.start()
        if p > 0:
            gate += gate_sum[...]
            up += up_sum[...]
        if p < parts - 1:
            gate_sum[...] = gate
            up_sum[...] = up
        else:
            finish(c, gate, up)


def hidden_part(panels, gate_held, up_held, gate_weight, up_weight, chunk, parts, slots):
    blocks, lanes = len(panels), lax.axis_size("regroup")
    each, depth = panels[0].shape
    rows = blocks * each
    width = gate_weight.shape[1]
    piece = jax.ShapeDtypeStruct((rows // lanes, width), jnp.bfloat16)
    return pl.pallas_call(
        functools.partial(
            hidden_kernel, blocks, lanes, chunk, gate_held.shape[1] // chunk, parts, slots
        ),
        out_shape=(piece,) * lanes,
        in_specs=[IN_VMEM] * blocks + [IN_VMEM, IN_VMEM, IN_HBM, IN_HBM],
        out_specs=(IN_VMEM,) * lanes,
        scratch_shapes=[
            pltpu.VMEM((rows, depth), jnp.bfloat16),
            pltpu.VMEM((rows, chunk), jnp.float32),
            pltpu.VMEM((rows, chunk), jnp.float32),
            pltpu.VMEM((slots, 2, depth // parts, chunk), jnp.bfloat16),
            pltpu.SemaphoreType.DMA((slots, 2)),
        ],
        compiler_params=pltpu.CompilerParams(vmem_limit_bytes=18 * MIB),
        cost_estimate=pl.CostEstimate(
            flops=4 * rows * depth * width,
            bytes_accessed=4 * depth * width,
            transcendentals=rows * width,
        ),
        name="hidden_part",
    )(*panels, gate_held, up_held, gate_weight, up_weight)


def down_kernel(blocks, lanes, chunk, *refs):
    piece_refs = refs[:lanes]
    down_ref = refs[lanes]
    out_refs = refs[lanes + 1 : -2]
    stack, hidden = refs[-2:]
    rows = hidden.shape[0]
    span = rows // lanes
    for step, ref in enumerate(piece_refs):
        stack[step * span : (step + 1) * span, :] = ref[...]
    order = by_place(rows, blocks, lanes, lax.axis_index("regroup"))
    hidden[...] = jnp.dot(order, stack[...], preferred_element_type=jnp.float32).astype(
        jnp.bfloat16
    )
    me = lax.axis_index("hid")
    for step in reversed(range(len(out_refs))):
        width = out_refs[step].shape[1]
        start = jnp.bitwise_xor(me, step) * width
        for c in range(width // chunk):
            at = pl.multiple_of(start + c * chunk, chunk)
            out_refs[step][:, c * chunk : (c + 1) * chunk] = jnp.dot(
                hidden[...], down_ref[:, pl.ds(at, chunk)], preferred_element_type=jnp.float32
            ).astype(out_refs[step].dtype)


def down_part(pieces, down_weight, blocks, chunk):
    lanes, hids = len(pieces), lax.axis_size("hid")
    rows = lanes * pieces[0].shape[0]
    depth, features = down_weight.shape
    width = features // hids
    outs = [jax.ShapeDtypeStruct((rows, width), jnp.float32)]
    outs += [jax.ShapeDtypeStruct((rows, width), jnp.bfloat16)] * (hids - 1)
    return pl.pallas_call(
        functools.partial(down_kernel, blocks, lanes, chunk),
        out_shape=tuple(outs),
        in_specs=[IN_VMEM] * (lanes + 1),
        out_specs=(IN_VMEM,) * hids,
        scratch_shapes=[
            pltpu.VMEM((rows, depth), jnp.bfloat16),
            pltpu.VMEM((rows, depth), jnp.bfloat16),
        ],
        compiler_params=pltpu.CompilerParams(vmem_limit_bytes=30 * MIB),
        cost_estimate=pl.CostEstimate(
            flops=2 * rows * depth * features,
            bytes_accessed=2 * depth * features,
            transcendentals=0,
        ),
        name="down_part",
    )(*pieces, down_weight)


def hid_sum_kernel(count, *refs):
    total = refs[0][...]
    for ref in refs[1:count]:
        total += ref[...].astype(jnp.float32)
    each = total.shape[0] // len(refs[count:])
    for step, ref in enumerate(refs[count:]):
        ref[...] = total[step * each : (step + 1) * each, :].astype(ref.dtype)


def hid_sum(parts, blocks):
    rows, width = parts[0].shape
    each = rows // blocks
    outs = [jax.ShapeDtypeStruct((each, width), jnp.float32)]
    outs += [jax.ShapeDtypeStruct((each, width), jnp.bfloat16)] * (blocks - 1)
    return pl.pallas_call(
        functools.partial(hid_sum_kernel, len(parts)),
        out_shape=tuple(outs),
        in_specs=[IN_VMEM] * len(parts),
        out_specs=(IN_VMEM,) * blocks,
        compiler_params=pltpu.CompilerParams(vmem_limit_bytes=8 * MIB),
        name="hid_sum",
    )(*parts)


def blk_sum_kernel(*refs):
    total = refs[0][...]
    for ref in refs[1:-1]:
        total += ref[...].astype(jnp.float32)
    refs[-1][...] = total.astype(refs[-1].dtype)


def blk_sum(parts):
    return pl.pallas_call(
        blk_sum_kernel,
        out_shape=jax.ShapeDtypeStruct(parts[0].shape, jnp.bfloat16),
        in_specs=[IN_VMEM] * len(parts),
        out_specs=IN_VMEM,
        compiler_params=pltpu.CompilerParams(vmem_limit_bytes=8 * MIB),
        name="blk_sum",
    )(*parts)


def on_device(tokens, kinds, slots, gains, gate_weight, up_weight, down_weight):
    blocks, lanes, hids = (lax.axis_size(axis) for axis in ("blk", "regroup", "hid"))
    shard = gate_weight.shape[1]
    chunk = min(512, shard)
    rows = norm(tokens, kinds, slots, gains)
    panels = [rows] + [exchange(rows, "blk", step) for step in range(1, blocks)]
    gate_held, up_held = early(gate_weight, up_weight, chunk)
    pieces = hidden_part(panels, gate_held, up_held, gate_weight, up_weight, chunk, 4, 4)
    pieces = [pieces[0]] + [
        exchange(pieces[step], "regroup", step) for step in range(1, lanes)
    ]
    partial = down_part(pieces, down_weight, blocks, min(512, down_weight.shape[1] // hids))
    partial = [partial[0]] + [exchange(partial[step], "hid", step) for step in range(1, hids)]
    own = hid_sum(partial, blocks)
    return blk_sum([own[0]] + [exchange(own[step], "blk", step) for step in range(1, blocks)])


def solution(mesh):
    placed = (
        P(("blk", "regroup"), None),
        P(("blk", "regroup")),
        P(("blk", "regroup"), None),
        P(),
        P(None, ("blk", "hid")),
        P(None, ("blk", "hid")),
        P(("blk", "hid"), None),
    )
    return jax.shard_map(
        on_device,
        mesh=mesh,
        in_specs=placed,
        out_specs=P(("blk", "regroup"), "hid"),
        check_vma=False,
    )
```

time: 108 us -> 69.8 us (0.65)
  matrix products: 33.4 us -> 0 us
  Pallas kernels: 0 us -> 32.5 us
  blocking collectives: 25.7 us -> 0 us
  waiting for transfers between devices: 33.4 us -> 12.8 us
  between operations: 13.5 us -> 0.08 us
  starting transfers between devices: 0.04 us -> 12.9 us
  local copies, waits for them, and re-layouts: 0.45 us -> 11.3 us
  other arithmetic: 1.14 us -> 0 us
    dot_general x4 -> x0, matrix products: 33.4 us -> none  [the longest x1 20.8 us: on_device(): jnp.dot(hidden, down_weight, preferred_element_type=jnp.float32)]
    reduce_scatter x2 -> x0, waiting for transfers between devices: 33.4 us -> none  [the longest x1 23.6 us: on_device(): lax.psum_scatter(jnp.dot(hidden, down_weight, preferred_element_type=jnp....]
    pallas_call x0 -> x6, Pallas kernels: none -> 32.5 us  [the longest x1 14.2 us: hidden_part(): pl.pallas_call(functools.partial(hidden_kernel, blocks, lanes, chunk, gat...]
    all_to_all x1 -> x0, blocking collectives: 13.6 us -> none  [on_device(): lax.all_to_all(by_lane, 'regroup', split_axis=1, concat_axis=1, tiled=True)]
    ppermute x0 -> x10, starting transfers between devices: none -> 12.9 us  [exchange(): return lax.ppermute(array, axis, [(i, i ^ step) for i in range(count)])]
    ppermute x0 -> x10, waiting for transfers between devices: none -> 12.8 us  [exchange(): return lax.ppermute(array, axis, [(i, i ^ step) for i in range(count)])]
    all_gather x1 -> x0, blocking collectives: 12.1 us -> none  [on_device(): panel = lax.all_gather(arranged, 'blk', axis=0, tiled=True)]
    unnamed x2 -> x10, local copies, waits for them, and re-layouts: 0.01 us -> 11.3 us
  transfers between devices with their start and end apart: 2 -> 10, of which waited for: 2 -> 6; matrix products, arithmetic and copies ran while one was open for 0% -> 0% of each run, Pallas kernels for 0% -> 5%
where the time goes in v1:
time: 69.8 us; the launch traced here: 69.6 us
  Pallas kernels  32.5 us (47%)
  starting transfers between devices  12.9 us (18%)
  waiting for transfers between devices  12.8 us (18%)
  local copies, waits for them, and re-layouts  11.3 us (16%)
    pallas_call x1, Pallas kernels, hidden_part(): pl.pallas_call(functools.partial(hidden_kernel, blocks, lanes, chunk, gat...  14.2 us
    ppermute x10, starting transfers between devices, exchange(): return lax.ppermute(array, axis, [(i, i ^ step) for i in range(count)])  12.9 us
    ppermute x10, waiting for transfers between devices, exchange(): return lax.ppermute(array, axis, [(i, i ^ step) for i in range(count)])  12.8 us
    pallas_call x1, Pallas kernels, down_part(): pl.pallas_call(functools.partial(down_kernel, blocks, lanes, chunk), out_...  12.8 us
    unnamed x10, local copies, waits for them, and re-layouts  11.3 us
    pallas_call x1, Pallas kernels, early(): pl.pallas_call(early_kernel, out_shape=(held, held), in_specs=[IN_HBM, IN...  3.81 us
  transfers between devices with their start and end apart: 10, of which 6 were waited for; matrix products, arithmetic and copies ran while one was open for 0% of the time, Pallas kernels for 5%

profile of v1, /device:TPU:0, one launch (start us, length us, event | category | flops | bytes accessed | tf_op | source)
XLA Modules:
  0.0 69.6 jit_solution(15398243259317128802)
XLA Ops:
  0.0 0.0 copy-start.1
  0.0 0.9 %copy-done.1 = bf16[16,6144]{1,0:T(8,128)(2,1)S(1)} copy-done((bf16[16,6144]{1,0:T(8,128)(2,1)S(1)}, bf16[16,6144]{1,0:T(8,128)(2,1)}, u32[]{:S(2)}) %copy-start.1) | copy-done | bytes 196632
  0.9 0.0 copy-start.2
  0.9 0.9 %copy-done.2 = f32[8,6144]{1,0:T(8,128)S(1)} copy-done((f32[8,6144]{1,0:T(8,128)S(1)}, f32[8,6144]{1,0:T(8,128)}, u32[]{:S(2)}) %copy-start.2) | copy-done | bytes 196632
  1.9 0.0 copy-start.3
  1.9 0.7 copy-done.3
  2.5 0.0 copy-start.4
  2.5 0.7 copy-done.4
  3.2 0.9 %norm.1.refs_0_ = bf16[16,6144]{1,0:T(8,128)(2,1)S(1)} custom-call(bf16[16,6144]{1,0:T(8,128)(2,1)S(1)} %copy-done.1, s32[16]{0:T(128)S(1)} %copy-done.3, s32[1,16]{1,0:T(1,128)S(1)} %copy-done.4, f32[8,6144]{1,0:T(8,128)S(1)} %copy-done.2), custom_call_target="tpu_custom_call" | custom-call | tf_op jit(solution)/shard_map/norm/pallas_call | solution.py:53
  4.1 4.0 %collective-permute-start.2 = (bf16[16,6144]{1,0:T(8,128)(2,1)S(1)}, bf16[16,6144]{1,0:T(8,128)(2,1)S(1)}, u32[]{:S(2)}, u32[]{:S(2)}) collective-permute-start(bf16[16,6144]{1,0:T(8,128)(2,1)S(1)} %norm.1.refs_0_), channel_id=1, source_target_pairs={{0,24},{8,16},{16,8},{24,0},{1,25},{9,17},{17,9},{25,1},{2,26},{10... | collective-permute-start | bytes 589832 | tf_op jit(solution)/shard_map/ppermute | solution.py:28
  8.1 0.5 collective-permute-start.1
  8.6 0.1 collective-permute-start
  8.7 0.0 copy-start
  8.7 8.2 %copy-done = bf16[6144,2048]{1,0:T(8,128)(2,1)S(1)} copy-done((bf16[6144,2048]{1,0:T(8,128)(2,1)S(1)}, bf16[6144,2048]{1,0:T(8,128)(2,1)}, u32[]{:S(2)}) %copy-start) | copy-done | bytes 25165848
  16.9 3.8 %early.1 = (bf16[6144,512]{1,0:T(8,128)(2,1)S(1)}, bf16[6144,512]{1,0:T(8,128)(2,1)S(1)}) custom-call(bf16[6144,2048]{1,0:T(8,128)(2,1)S(1)} %copy-done, bf16[6144,2048]{1,0:T(8,128)(2,1)} %refs_7_.1), custom_call_target="tpu_custom_call" | custom-call | bytes 25165824 | tf_op jit(solution)/shard_map/early/pallas_call | solution.py:78
  20.7 0.0 collective-permute-done.2.refs_3_
  20.7 0.0 collective-permute-done.1.refs_2_
  20.7 0.0 collective-permute-done.refs_1_
  20.7 14.2 %hidden_part.1 = (bf16[16,2048]{1,0:T(8,128)(2,1)S(1)}, bf16[16,2048]{1,0:T(8,128)(2,1)S(1)}, bf16[16,2048]{1,0:T(8,128)(2,1)S(1)}, bf16[16,2048]{1,0:T(8,128)(2,1)S(1)}) custom-call(bf16[16,6144]{1,0:T(8,128)(2,1)S(1)} %norm.1.refs_0_, bf16[16,6144]{1,0:T(8,128)(2,1)S(1)} %collective-permute-done.refs_1_, ...), custom_call_target="tpu_custom_call" | custom-call | flops 3221225472 | bytes 50331648 | tf_op jit(solution)/shard_map/hidden_part/pallas_call | solution.py:181
  34.9 2.0 %collective-permute-start.3 = (bf16[16,2048]{1,0:T(8,128)(2,1)S(1)}, bf16[16,2048]{1,0:T(8,128)(2,1)S(1)}, u32[]{:S(2)}, u32[]{:S(2)}) collective-permute-start(bf16[16,2048]{1,0:T(8,128)(2,1)S(1)} %get-tuple-element.20), channel_id=1, source_target_pairs={{0,2},{2,0},{4,6},{6,4},{1,3},{3,1},{5,7},{7,5},{8,10},{10,8},{12,... | collective-permute-start | bytes 196616 | tf_op jit(solution)/shard_map/ppermute | solution.py:28
  37.0 2.6 %collective-permute-start.4 = (bf16[16,2048]{1,0:T(8,128)(2,1)S(1)}, bf16[16,2048]{1,0:T(8,128)(2,1)S(1)}, u32[]{:S(2)}, u32[]{:S(2)}) collective-permute-start(bf16[16,2048]{1,0:T(8,128)(2,1)S(1)} %get-tuple-element.21), channel_id=1, source_target_pairs={{0,4},{2,6},{4,0},{6,2},{1,5},{3,7},{5,1},{7,3},{8,12},{10,14},{12... | collective-permute-start | bytes 196616 | tf_op jit(solution)/shard_map/ppermute | solution.py:28
  39.6 0.0 collective-permute-start.5
  39.6 0.0 collective-permute-done.3.refs_1_
  39.6 4.0 %collective-permute-done.4.refs_2_ = bf16[16,2048]{1,0:T(8,128)(2,1)S(1)} collective-permute-done((bf16[16,2048]{1,0:T(8,128)(2,1)S(1)}, bf16[16,2048]{1,0:T(8,128)(2,1)S(1)}, u32[]{:S(2)}, u32[]{:S(2)}) %collective-permute-start.4) | collective-permute-done | bytes 65568 | tf_op jit(solution)/shard_map/ppermute | solution.py:28
  43.5 2.1 %collective-permute-done.5.refs_3_ = bf16[16,2048]{1,0:T(8,128)(2,1)S(1)} collective-permute-done((bf16[16,2048]{1,0:T(8,128)(2,1)S(1)}, bf16[16,2048]{1,0:T(8,128)(2,1)S(1)}, u32[]{:S(2)}, u32[]{:S(2)}) %collective-permute-start.5) | collective-permute-done | bytes 65568 | tf_op jit(solution)/shard_map/ppermute | solution.py:28
  45.6 12.8 %down_part.1 = (f32[64,3072]{1,0:T(8,128)S(1)}, bf16[64,3072]{1,0:T(8,128)(2,1)S(1)}) custom-call(bf16[16,2048]{1,0:T(8,128)(2,1)S(1)} %get-tuple-element.19.refs_0_, bf16[16,2048]{1,0:T(8,128)(2,1)S(1)} %collective-permute-done.3.refs_1_, bf16[16,2048]{1,0:T(8,128)(2,1)S(1)} %collective-permute-done.4.refs_2_, ...), custom_call_target="tpu_custom_call" | custom-call | flops 1610612736 | bytes 25165824 | tf_op jit(solution)/shard_map/down_part/pallas_call | solution.py:236
  58.4 0.1 collective-permute-start.6
  58.5 1.7 %collective-permute-done.6.refs_1_ = bf16[64,3072]{1,0:T(8,128)(2,1)S(1)} collective-permute-done((bf16[64,3072]{1,0:T(8,128)(2,1)S(1)}, bf16[64,3072]{1,0:T(8,128)(2,1)S(1)}, u32[]{:S(2)}, u32[]{:S(2)}) %collective-permute-start.6) | collective-permute-done | bytes 393248 | tf_op jit(solution)/shard_map/ppermute | solution.py:28
  60.2 0.1 hid_sum.1
  60.3 1.6 %collective-permute-start.7 = (bf16[16,3072]{1,0:T(8,128)(2,1)S(1)}, bf16[16,3072]{1,0:T(8,128)(2,1)S(1)}, u32[]{:S(2)}, u32[]{:S(2)}) collective-permute-start(bf16[16,3072]{1,0:T(8,128)(2,1)S(1)} %get-tuple-element.26), channel_id=1, source_target_pairs={{0,8},{8,0},{16,24},{24,16},{1,9},{9,1},{17,25},{25,17},{2,10},{10... | collective-permute-start | bytes 294920 | tf_op jit(solution)/shard_map/ppermute | solution.py:28
  61.8 1.5 %collective-permute-start.8 = (bf16[16,3072]{1,0:T(8,128)(2,1)S(1)}, bf16[16,3072]{1,0:T(8,128)(2,1)S(1)}, u32[]{:S(2)}, u32[]{:S(2)}) collective-permute-start(bf16[16,3072]{1,0:T(8,128)(2,1)S(1)} %get-tuple-element.27), channel_id=1, source_target_pairs={{0,16},{8,24},{16,0},{24,8},{1,17},{9,25},{17,1},{25,9},{2,18},{10... | collective-permute-start | bytes 294920 | tf_op jit(solution)/shard_map/ppermute | solution.py:28
  63.4 0.5 collective-permute-start.9
  63.8 1.3 %collective-permute-done.7.refs_1_ = bf16[16,3072]{1,0:T(8,128)(2,1)S(1)} collective-permute-done((bf16[16,3072]{1,0:T(8,128)(2,1)S(1)}, bf16[16,3072]{1,0:T(8,128)(2,1)S(1)}, u32[]{:S(2)}, u32[]{:S(2)}) %collective-permute-start.7) | collective-permute-done | bytes 98336 | tf_op jit(solution)/shard_map/ppermute | solution.py:28
  65.2 2.4 %collective-permute-done.8.refs_2_ = bf16[16,3072]{1,0:T(8,128)(2,1)S(1)} collective-permute-done((bf16[16,3072]{1,0:T(8,128)(2,1)S(1)}, bf16[16,3072]{1,0:T(8,128)(2,1)S(1)}, u32[]{:S(2)}, u32[]{:S(2)}) %collective-permute-start.8) | collective-permute-done | bytes 98336 | tf_op jit(solution)/shard_map/ppermute | solution.py:28
  67.6 1.3 %collective-permute-done.9.refs_3_ = bf16[16,3072]{1,0:T(8,128)(2,1)S(1)} collective-permute-done((bf16[16,3072]{1,0:T(8,128)(2,1)S(1)}, bf16[16,3072]{1,0:T(8,128)(2,1)S(1)}, u32[]{:S(2)}, u32[]{:S(2)}) %collective-permute-start.9) | collective-permute-done | bytes 98336 | tf_op jit(solution)/shard_map/ppermute | solution.py:28
  68.9 0.7 blk_sum.1
Async XLA Ops:
  0.0 0.9 %copy-start.1 = (bf16[16,6144]{1,0:T(8,128)(2,1)S(1)}, bf16[16,6144]{1,0:T(8,128)(2,1)}, u32[]{:S(2)}) copy-start(bf16[16,6144]{1,0:T(8,128)(2,1)} %tokens_ref.1) | copy-start | bytes 589828
  0.9 0.9 %copy-start.2 = (f32[8,6144]{1,0:T(8,128)S(1)}, f32[8,6144]{1,0:T(8,128)}, u32[]{:S(2)}) copy-start(f32[8,6144]{1,0:T(8,128)} %gains_ref.1) | copy-start | bytes 589828
  1.9 0.7 copy-start.3
  2.5 0.7 copy-start.4
  4.1 16.6 %collective-permute-start.2 = (bf16[16,6144]{1,0:T(8,128)(2,1)S(1)}, bf16[16,6144]{1,0:T(8,128)(2,1)S(1)}, u32[]{:S(2)}, u32[]{:S(2)}) collective-permute-start(bf16[16,6144]{1,0:T(8,128)(2,1)S(1)} %norm.1.refs_0_), channel_id=1, source_target_pairs={{0,24},{8,16},{16,8},{24,0},{1,25},{9,17},{17,9},{25,1},{2,26},{10... | collective-permute-start | bytes 589832 | tf_op jit(solution)/shard_map/ppermute | solution.py:28
  8.1 12.6 %collective-permute-start.1 = (bf16[16,6144]{1,0:T(8,128)(2,1)S(1)}, bf16[16,6144]{1,0:T(8,128)(2,1)S(1)}, u32[]{:S(2)}, u32[]{:S(2)}) collective-permute-start(bf16[16,6144]{1,0:T(8,128)(2,1)S(1)} %norm.1.refs_0_), channel_id=1, source_target_pairs={{0,16},{8,24},{16,0},{24,8},{1,17},{9,25},{17,1},{25,9},{2,18},{10... | collective-permute-start | bytes 589832 | tf_op jit(solution)/shard_map/ppermute | solution.py:28
  8.6 12.1 %collective-permute-start = (bf16[16,6144]{1,0:T(8,128)(2,1)S(1)}, bf16[16,6144]{1,0:T(8,128)(2,1)S(1)}, u32[]{:S(2)}, u32[]{:S(2)}) collective-permute-start(bf16[16,6144]{1,0:T(8,128)(2,1)S(1)} %norm.1.refs_0_), channel_id=1, source_target_pairs={{0,8},{8,0},{16,24},{24,16},{1,9},{9,1},{17,25},{25,17},{2,10},{10... | collective-permute-start | bytes 589832 | tf_op jit(solution)/shard_map/ppermute | solution.py:28
  8.7 8.2 %copy-start = (bf16[6144,2048]{1,0:T(8,128)(2,1)S(1)}, bf16[6144,2048]{1,0:T(8,128)(2,1)}, u32[]{:S(2)}) copy-start(bf16[6144,2048]{1,0:T(8,128)(2,1)} %refs_6_.1) | copy-start | bytes 75497472
  34.9 4.6 %collective-permute-start.3 = (bf16[16,2048]{1,0:T(8,128)(2,1)S(1)}, bf16[16,2048]{1,0:T(8,128)(2,1)S(1)}, u32[]{:S(2)}, u32[]{:S(2)}) collective-permute-start(bf16[16,2048]{1,0:T(8,128)(2,1)S(1)} %get-tuple-element.20), channel_id=1, source_target_pairs={{0,2},{2,0},{4,6},{6,4},{1,3},{3,1},{5,7},{7,5},{8,10},{10,8},{12,... | collective-permute-start | bytes 196616 | tf_op jit(solution)/shard_map/ppermute | solution.py:28
  37.0 6.6 %collective-permute-start.4 = (bf16[16,2048]{1,0:T(8,128)(2,1)S(1)}, bf16[16,2048]{1,0:T(8,128)(2,1)S(1)}, u32[]{:S(2)}, u32[]{:S(2)}) collective-permute-start(bf16[16,2048]{1,0:T(8,128)(2,1)S(1)} %get-tuple-element.21), channel_id=1, source_target_pairs={{0,4},{2,6},{4,0},{6,2},{1,5},{3,7},{5,1},{7,3},{8,12},{10,14},{12... | collective-permute-start | bytes 196616 | tf_op jit(solution)/shard_map/ppermute | solution.py:28
  39.6 6.1 %collective-permute-start.5 = (bf16[16,2048]{1,0:T(8,128)(2,1)S(1)}, bf16[16,2048]{1,0:T(8,128)(2,1)S(1)}, u32[]{:S(2)}, u32[]{:S(2)}) collective-permute-start(bf16[16,2048]{1,0:T(8,128)(2,1)S(1)} %get-tuple-element.22), channel_id=1, source_target_pairs={{0,6},{2,4},{4,2},{6,0},{1,7},{3,5},{5,3},{7,1},{8,14},{10,12},{12... | collective-permute-start | bytes 196616 | tf_op jit(solution)/shard_map/ppermute | solution.py:28
  58.4 1.8 %collective-permute-start.6 = (bf16[64,3072]{1,0:T(8,128)(2,1)S(1)}, bf16[64,3072]{1,0:T(8,128)(2,1)S(1)}, u32[]{:S(2)}, u32[]{:S(2)}) collective-permute-start(bf16[64,3072]{1,0:T(8,128)(2,1)S(1)} %get-tuple-element.24), channel_id=1, source_target_pairs={{0,1},{1,0},{2,3},{3,2},{4,5},{5,4},{6,7},{7,6},{8,9},{9,8},{10,11... | collective-permute-start | bytes 1179656 | tf_op jit(solution)/shard_map/ppermute | solution.py:28
  60.3 4.9 %collective-permute-start.7 = (bf16[16,3072]{1,0:T(8,128)(2,1)S(1)}, bf16[16,3072]{1,0:T(8,128)(2,1)S(1)}, u32[]{:S(2)}, u32[]{:S(2)}) collective-permute-start(bf16[16,3072]{1,0:T(8,128)(2,1)S(1)} %get-tuple-element.26), channel_id=1, source_target_pairs={{0,8},{8,0},{16,24},{24,16},{1,9},{9,1},{17,25},{25,17},{2,10},{10... | collective-permute-start | bytes 294920 | tf_op jit(solution)/shard_map/ppermute | solution.py:28
  61.8 5.8 %collective-permute-start.8 = (bf16[16,3072]{1,0:T(8,128)(2,1)S(1)}, bf16[16,3072]{1,0:T(8,128)(2,1)S(1)}, u32[]{:S(2)}, u32[]{:S(2)}) collective-permute-start(bf16[16,3072]{1,0:T(8,128)(2,1)S(1)} %get-tuple-element.27), channel_id=1, source_target_pairs={{0,16},{8,24},{16,0},{24,8},{1,17},{9,25},{17,1},{25,9},{2,18},{10... | collective-permute-start | bytes 294920 | tf_op jit(solution)/shard_map/ppermute | solution.py:28
  63.4 5.5 %collective-permute-start.9 = (bf16[16,3072]{1,0:T(8,128)(2,1)S(1)}, bf16[16,3072]{1,0:T(8,128)(2,1)S(1)}, u32[]{:S(2)}, u32[]{:S(2)}) collective-permute-start(bf16[16,3072]{1,0:T(8,128)(2,1)S(1)} %get-tuple-element.28), channel_id=1, source_target_pairs={{0,24},{8,16},{16,8},{24,0},{1,25},{9,17},{17,9},{25,1},{2,26},{10... | collective-permute-start | bytes 294920 | tf_op jit(solution)/shard_map/ppermute | solution.py:28

commit v2 on v0

v2 whole, which is shorter than its diff:
```python
import functools

import jax
import jax.numpy as jnp
from jax import lax
from jax.experimental import pallas as pl
from jax.experimental.pallas import tpu as pltpu
from jax.sharding import PartitionSpec as P

epsilon = 1e-05
MIB = 1 << 20

ANYWHERE = pl.BlockSpec(memory_space=pl.ANY)
IN_VMEM = pl.BlockSpec(memory_space=pltpu.VMEM)


def log2(number):
    bits = number.bit_length() - 1
    assert 1 << bits == number
    return bits


def exchange(array, axis, step):
    count = lax.axis_size(axis)
    log2(count)
    return lax.ppermute(array, axis, [(i, i ^ step) for i in range(count)])


def norm_kernel(lanes, *refs):
    sources, piece_refs = refs[:4], refs[4 : 4 + lanes]
    targets, placed, sems = refs[4 + lanes : 8 + lanes], refs[8 + lanes], refs[9 + lanes]
    copies = [
        pltpu.make_async_copy(src, dst, sems.at[i])
        for i, (src, dst) in enumerate(zip(sources, targets))
    ]
    for copy in copies:
        copy.start()
    for copy in copies:
        copy.wait()
    tokens_ref, kinds_ref, slots_ref, gains_ref = targets
    rows = tokens_ref.shape[0]
    rounds = rows // lanes
    x = tokens_ref[...].astype(jnp.float32)
    row_scale = lax.rsqrt(jnp.mean(x * x, axis=1, keepdims=True) + epsilon)
    width = placed.shape[1]
    columns = pl.ds(pl.multiple_of(lax.axis_index("hid") * width, width), width)
    x = tokens_ref[:, columns].astype(jnp.float32)
    at = lax.broadcasted_iota(jnp.int32, (rows, 1), 0)
    kind = jnp.zeros((rows, 1), jnp.int32)
    for i in range(rows):
        kind = jnp.where(at == i, kinds_ref[i], kind)
    gain = jnp.broadcast_to(gains_ref[0:1, columns], x.shape)
    for c in range(1, gains_ref.shape[0]):
        gain = jnp.where(kind == c, gains_ref[c : c + 1, columns], gain)
    normed = (x * row_scale * gain).astype(jnp.bfloat16)
    me = lax.axis_index("regroup")
    target = lax.broadcasted_iota(jnp.int32, (rows, rows), 0)
    lane = jnp.bitwise_xor(lax.shift_right_logical(target, log2(rounds)), me)
    slot = jnp.bitwise_and(target, rounds - 1) * lanes + lane
    placing = (jnp.broadcast_to(slots_ref[0:1, :], slot.shape) == slot).astype(jnp.bfloat16)
    placed[...] = jnp.dot(placing, normed, preferred_element_type=jnp.float32)
    for step, ref in enumerate(piece_refs):
        ref[...] = placed[step * rounds : (step + 1) * rounds, :].astype(jnp.bfloat16)


def norm(tokens, kinds, slots, gains):
    rows, features = tokens.shape
    lanes = lax.axis_size("regroup")
    width = features // lax.axis_size("hid")
    return pl.pallas_call(
        functools.partial(norm_kernel, lanes),
        out_shape=(jax.ShapeDtypeStruct((rows // lanes, width), jnp.bfloat16),) * lanes,
        in_specs=[ANYWHERE] * 4,
        out_specs=(IN_VMEM,) * lanes,
        scratch_shapes=[
            pltpu.VMEM(tokens.shape, tokens.dtype),
            pltpu.SMEM(kinds.shape, kinds.dtype),
            pltpu.VMEM(slots.shape, slots.dtype),
            pltpu.VMEM(gains.shape, gains.dtype),
            pltpu.VMEM((rows, width), jnp.float32),
            pltpu.SemaphoreType.DMA((4,)),
        ],
        compiler_params=pltpu.CompilerParams(vmem_limit_bytes=4 * MIB),
        cost_estimate=pl.CostEstimate(flops=0, bytes_accessed=48 * MIB, transcendentals=0),
        name="norm",
    )(tokens, kinds, slots, gains)


def arrange_kernel(lanes, *refs):
    out_ref, stack = refs[lanes:]
    rows = out_ref.shape[0]
    rounds = rows // lanes
    for step in range(lanes):
        stack[step * rounds : (step + 1) * rounds, :] = refs[step][...].astype(jnp.float32)
    r = lax.broadcasted_iota(jnp.int32, (rows, rows), 0)
    c = lax.broadcasted_iota(jnp.int32, (rows, rows), 1)
    step = jnp.bitwise_xor(jnp.bitwise_and(r, lanes - 1), lax.axis_index("regroup"))
    order = (c == step * rounds + lax.shift_right_logical(r, log2(lanes))).astype(jnp.bfloat16)
    out_ref[...] = jnp.dot(
        order, stack[...].astype(jnp.bfloat16), preferred_element_type=jnp.float32
    ).astype(jnp.bfloat16)


def arrange(pieces):
    lanes = len(pieces)
    rounds, width = pieces[0].shape
    return pl.pallas_call(
        functools.partial(arrange_kernel, lanes),
        out_shape=jax.ShapeDtypeStruct((lanes * rounds, width), jnp.bfloat16),
        in_specs=[IN_VMEM] * lanes,
        out_specs=IN_VMEM,
        scratch_shapes=[pltpu.VMEM((lanes * rounds, width), jnp.float32)],
        compiler_params=pltpu.CompilerParams(vmem_limit_bytes=4 * MIB),
        name="arrange",
    )(*pieces)


def early_kernel(after_ref, up_ref, out_ref, sem):
    depth = out_ref.shape[0]
    start = pl.multiple_of(lax.axis_index("hid") * depth, depth)
    copy = pltpu.make_async_copy(up_ref.at[pl.ds(start, depth), :], out_ref, sem)
    copy.start()
    copy.wait()


def early(after, up_weight):
    depth = up_weight.shape[0] // lax.axis_size("hid")
    shard = up_weight.shape[1]
    return pl.pallas_call(
        early_kernel,
        out_shape=pltpu.VMEM((depth, shard), jnp.bfloat16),
        in_specs=[ANYWHERE, ANYWHERE],
        out_specs=IN_VMEM,
        scratch_shapes=[pltpu.SemaphoreType.DMA(())],
        compiler_params=pltpu.CompilerParams(vmem_limit_bytes=1 * MIB),
        cost_estimate=pl.CostEstimate(
            flops=0, bytes_accessed=2 * depth * shard, transcendentals=0
        ),
        name="early",
    )(after, up_weight)


def even(total, most):
    return next(size for size in range(min(most, total), 0, -128) if total % size == 0)


def ffn_kernel(blocks, hids, plan, *refs):
    slots, part, up_cols, down_rows, down_cols = plan
    count = blocks * hids
    panel_refs = refs[:count]
    gate_ref, held_ref, up_ref, down_ref = refs[count : count + 4]
    hidden_ref, kept = refs[count + 4 : count + 6]
    out_refs = refs[count + 6 : count + 5 + hids]
    panel, up_sum, ring, ring_sems, kept_sem = refs[count + 5 + hids :]
    rows, depth = panel.shape
    each = rows // blocks
    shard = gate_ref.shape[1]
    width = depth // hids
    me = lax.axis_index("hid")
    inside, across = width // part, shard // up_cols
    deep, wide = shard // down_rows, width // down_cols
    up_count = (hids - 1) * inside * across
    down_count = (hids - 1) * wide * deep

    def side_start(side):
        return jnp.bitwise_xor(me, side) * width

    def up_copy(n):
        side, p, c = n // (inside * across) + 1, n // across % inside, n % across
        return pltpu.make_async_copy(
            up_ref.at[
                pl.ds(pl.multiple_of(side_start(side) + p * part, part), part),
                pl.ds(pl.multiple_of(c * up_cols, up_cols), up_cols),
            ],
            ring.at[n % slots, pl.ds(0, part), pl.ds(0, up_cols)],
            ring_sems.at[n % slots],
        )

    def down_copy(n):
        side, c, k = n // (wide * deep) + 1, n // deep % wide, n % deep
        slot = (n + up_count) % slots
        return pltpu.make_async_copy(
            down_ref.at[
                pl.ds(pl.multiple_of(k * down_rows, down_rows), down_rows),
                pl.ds(pl.multiple_of(side_start(side) + c * down_cols, 128), down_cols),
            ],
            ring.at[slot, pl.ds(0, down_rows), pl.ds(0, down_cols)],
            ring_sems.at[slot],
        )

    kept_copy = pltpu.make_async_copy(
        down_ref.at[:, pl.ds(pl.multiple_of(me * width, 128), kept.shape[1])], kept, kept_sem
    )

    def start_next(n):
        if isinstance(n, int):
            if n < up_count:
                up_copy(n).start()
            elif n < up_count + down_count:
                down_copy(n - up_count).start()
            return

        @pl.when(n < up_count)
        def _():
            up_copy(n).start()

        @pl.when((n >= up_count) & (n < up_count + down_count))
        def _():
            down_copy(n - up_count).start()

    for n in range(slots):
        start_next(n)
    for side in range(hids):
        start = pl.multiple_of(side_start(side), width)
        for step in range(blocks):
            panel[step * each : (step + 1) * each, pl.ds(start, width)] = panel_refs[
                side * blocks + step
            ][...]
    chunk = min(1024, shard)
    own = pl.ds(pl.multiple_of(me * width, width), width)

    @pl.loop(0, shard // chunk)
    def _(c):
        columns = pl.ds(pl.multiple_of(c * chunk, chunk), chunk)
        up_sum[:, columns] = jnp.dot(
            panel[:, own], held_ref[:, columns], preferred_element_type=jnp.float32
        )

    @pl.loop(0, (hids - 1) * inside)
    def _(u):
        side, p = u // inside + 1, u % inside
        x = panel[:, pl.ds(pl.multiple_of(side_start(side) + p * part, part), part)]
        for c in range(across):
            n = u * across + c
            up_copy(n).wait()
            columns = slice(c * up_cols, (c + 1) * up_cols)
            up_sum[:, columns] += jnp.dot(
                x,
                ring[n % slots, 0:part, 0:up_cols],
                preferred_element_type=jnp.float32,
            )
            start_next(n + slots)

    kept_copy.start()

    @pl.loop(0, shard // chunk)
    def _(c):
        columns = pl.ds(pl.multiple_of(c * chunk, chunk), chunk)
        gate = jnp.dot(panel[...], gate_ref[:, columns], preferred_element_type=jnp.float32)
        hidden_ref[:, columns] = (gate / (1.0 + jnp.exp(-gate)) * up_sum[:, columns]).astype(
            jnp.bfloat16
        )

    for side in range(1, hids):

        @pl.loop(0, wide)
        def _(c):
            total = None
            for k in range(deep):
                n = ((side - 1) * wide + c) * deep + k
                down_copy(n).wait()
                value = jnp.dot(
                    hidden_ref[:, k * down_rows : (k + 1) * down_rows],
                    ring[(n + up_count) % slots, 0:down_rows, 0:down_cols],
                    preferred_element_type=jnp.float32,
                )
                total = value if total is None else total + value
                start_next(n + up_count + slots)
            columns = pl.ds(pl.multiple_of(c * down_cols, 128), down_cols)
            out_refs[side - 1][:, columns] = total.astype(jnp.bfloat16)

    kept_copy.wait()


def ffn(panels, gate_weight, up_held, up_weight, down_weight, blocks):
    hids = lax.axis_size("hid")
    each, width = panels[0].shape
    rows, depth = blocks * each, width * hids
    shard = gate_weight.shape[1]
    part, up_cols = even(width, 1024), even(shard, 1024)
    down_rows, down_cols = even(shard, 1024), even(width, 1024)
    slots = 4
    outs = [
        pltpu.VMEM((rows, shard), jnp.bfloat16),
        pltpu.VMEM((shard, (width // down_cols + 1) // 2 * down_cols), jnp.bfloat16),
    ] + [pltpu.VMEM((rows, width), jnp.bfloat16)] * (hids - 1)
    return pl.pallas_call(
        functools.partial(
            ffn_kernel, blocks, hids, (slots, part, up_cols, down_rows, down_cols)
        ),
        out_shape=tuple(outs),
        in_specs=[IN_VMEM] * (len(panels) + 2) + [ANYWHERE, ANYWHERE],
        out_specs=(IN_VMEM,) * (1 + hids),
        scratch_shapes=[
            pltpu.VMEM((rows, depth), jnp.bfloat16),
            pltpu.VMEM((rows, shard), jnp.float32),
            pltpu.VMEM((slots, max(part, down_rows), max(up_cols, down_cols)), jnp.bfloat16),
            pltpu.SemaphoreType.DMA((slots,)),
            pltpu.SemaphoreType.DMA(()),
        ],
        compiler_params=pltpu.CompilerParams(vmem_limit_bytes=13 * MIB),
        cost_estimate=pl.CostEstimate(
            flops=4 * rows * depth * shard + 2 * rows * shard * (depth - width),
            bytes_accessed=4 * depth * shard,
            transcendentals=rows * shard,
        ),
        name="ffn",
    )(*panels, gate_weight, up_held, up_weight, down_weight)


def kept_kernel(hidden_ref, kept_ref, down_ref, out_ref, rest, sems):
    width = out_ref.shape[1]
    have, band = kept_ref.shape[1], rest.shape[2]
    me = lax.axis_index("hid")

    def copy(n):
        start = pl.multiple_of(me * width + have + n * band, 128)
        return pltpu.make_async_copy(
            down_ref.at[:, pl.ds(start, band)], rest.at[n], sems.at[n]
        )

    more = (width - have) // band
    for n in range(more):
        copy(n).start()

    @pl.loop(0, have // band)
    def _(n):
        columns = pl.ds(pl.multiple_of(n * band, 128), band)
        out_ref[:, columns] = jnp.dot(
            hidden_ref[...], kept_ref[:, columns], preferred_element_type=jnp.float32
        )

    @pl.loop(0, more)
    def _(n):
        copy(n).wait()
        columns = pl.ds(pl.multiple_of(have + n * band, 128), band)
        out_ref[:, columns] = jnp.dot(
            hidden_ref[...], rest[n], preferred_element_type=jnp.float32
        )


def kept_part(hidden, kept, down_weight):
    rows, shard = hidden.shape
    width = down_weight.shape[1] // lax.axis_size("hid")
    band = even(kept.shape[1], 512)
    more = max(1, (width - kept.shape[1]) // band)
    return pl.pallas_call(
        kept_kernel,
        out_shape=jax.ShapeDtypeStruct((rows, width), jnp.float32),
        in_specs=[IN_VMEM, IN_VMEM, ANYWHERE],
        out_specs=IN_VMEM,
        scratch_shapes=[
            pltpu.VMEM((more, shard, band), jnp.bfloat16),
            pltpu.SemaphoreType.DMA((more,)),
        ],
        compiler_params=pltpu.CompilerParams(vmem_limit_bytes=6 * MIB),
        cost_estimate=pl.CostEstimate(
            flops=2 * rows * shard * width, bytes_accessed=2 * shard * width, transcendentals=0
        ),
        name="kept_part",
    )(hidden, kept, down_weight)


def hid_sum_kernel(count, *refs):
    total = refs[0][...]
    for ref in refs[1:count]:
        total += ref[...].astype(jnp.float32)
    each = total.shape[0] // len(refs[count:])
    for step, ref in enumerate(refs[count:]):
        ref[...] = total[step * each : (step + 1) * each, :].astype(ref.dtype)


def hid_sum(parts, blocks):
    rows, width = parts[0].shape
    each = rows // blocks
    outs = [jax.ShapeDtypeStruct((each, width), jnp.float32)]
    outs += [jax.ShapeDtypeStruct((each, width), jnp.bfloat16)] * (blocks - 1)
    return pl.pallas_call(
        functools.partial(hid_sum_kernel, len(parts)),
        out_shape=tuple(outs),
        in_specs=[IN_VMEM] * len(parts),
        out_specs=(IN_VMEM,) * blocks,
        compiler_params=pltpu.CompilerParams(vmem_limit_bytes=4 * MIB),
        name="hid_sum",
    )(*parts)


def blk_sum_kernel(*refs):
    total = refs[0][...]
    for ref in refs[1:-1]:
        total += ref[...].astype(jnp.float32)
    refs[-1][...] = total.astype(refs[-1].dtype)


def blk_sum(parts):
    return pl.pallas_call(
        blk_sum_kernel,
        out_shape=jax.ShapeDtypeStruct(parts[0].shape, jnp.bfloat16),
        in_specs=[IN_VMEM] * len(parts),
        out_specs=IN_VMEM,
        compiler_params=pltpu.CompilerParams(vmem_limit_bytes=4 * MIB),
        name="blk_sum",
    )(*parts)


def held(array):
    return pltpu.with_memory_space_constraint(array, pltpu.VMEM)


def on_device(tokens, kinds, slots, gains, gate_weight, up_weight, down_weight):
    blocks, lanes, hids = (lax.axis_size(axis) for axis in ("blk", "regroup", "hid"))
    tokens, kinds, slots, gains, up_weight, down_weight = (
        pltpu.with_memory_space_constraint(array, pltpu.HBM)
        for array in (tokens, kinds, slots, gains, up_weight, down_weight)
    )
    gate_weight = held(gate_weight)
    pieces = norm(tokens, kinds, slots, gains)
    half = arrange(
        [pieces[0]] + [exchange(pieces[step], "regroup", step) for step in range(1, lanes)]
    )
    halves = [half] + [exchange(half, "blk", step) for step in range(1, blocks)]
    up_held = held(early(half, up_weight))
    halves, up_held = lax.optimization_barrier((halves, up_held))
    up_held = held(up_held)
    panels = halves + [exchange(part, "hid", side) for side in range(1, hids) for part in halves]
    panels = [held(part) for part in panels]
    hidden, kept, *sent = ffn(panels, gate_weight, up_held, up_weight, down_weight, blocks)
    hidden, kept = held(hidden), held(kept)
    came = [exchange(part, "hid", step + 1) for step, part in enumerate(sent)]
    parts = hid_sum([kept_part(hidden, kept, down_weight)] + came, blocks)
    return blk_sum(
        [parts[0]] + [exchange(parts[step], "blk", step) for step in range(1, blocks)]
    )


def solution(mesh):
    placed = (
        P(("blk", "regroup"), None),
        P(("blk", "regroup")),
        P(("blk", "regroup"), None),
        P(),
        P(None, ("blk", "hid")),
        P(None, ("blk", "hid")),
        P(("blk", "hid"), None),
    )
    return jax.shard_map(
        on_device,
        mesh=mesh,
        in_specs=placed,
        out_specs=P(("blk", "regroup"), "hid"),
        check_vma=False,
    )
```

time: 108 us -> 49.8 us (0.46)
  matrix products: 33.4 us -> 0 us
  blocking collectives: 25.7 us -> 0 us
  Pallas kernels: 0 us -> 23.6 us
  waiting for transfers between devices: 33.4 us -> 11.6 us
  starting transfers between devices: 0.04 us -> 14.3 us
  between operations: 13.5 us -> 0.1 us
  other arithmetic: 1.14 us -> 0 us
    dot_general x4 -> x0, matrix products: 33.4 us -> none  [the longest x1 20.8 us: on_device(): jnp.dot(hidden, down_weight, preferred_element_type=jnp.float32)]
    reduce_scatter x2 -> x0, waiting for transfers between devices: 33.4 us -> none  [the longest x1 23.6 us: on_device(): lax.psum_scatter(jnp.dot(hidden, down_weight, preferred_element_type=jnp....]
    pallas_call x0 -> x7, Pallas kernels: none -> 23.6 us  [the longest x1 13.6 us: ffn(): pl.pallas_call(functools.partial(ffn_kernel, blocks, hids, (slots, part,...]
    ppermute x0 -> x14, starting transfers between devices: none -> 14.3 us  [exchange(): return lax.ppermute(array, axis, [(i, i ^ step) for i in range(count)])]
    all_to_all x1 -> x0, blocking collectives: 13.6 us -> none  [on_device(): lax.all_to_all(by_lane, 'regroup', split_axis=1, concat_axis=1, tiled=True)]
    all_gather x1 -> x0, blocking collectives: 12.1 us -> none  [on_device(): panel = lax.all_gather(arranged, 'blk', axis=0, tiled=True)]
    ppermute x0 -> x14, waiting for transfers between devices: none -> 11.6 us  [exchange(): return lax.ppermute(array, axis, [(i, i ^ step) for i in range(count)])]
    reduce_sum x1 -> x0, other arithmetic: 1.13 us -> none  [on_device(): jnp.mean(float_rows * float_rows, axis=1, keepdims=True) + epsilon]
  transfers between devices with their start and end apart: 2 -> 14, of which waited for: 2 -> 9; matrix products, arithmetic and copies ran while one was open for 0% -> 0% of each run, Pallas kernels for 0% -> 15%
where the time goes in v2:
time: 49.8 us; the launch traced here: 49.6 us
  Pallas kernels  23.6 us (47%)
  starting transfers between devices  14.3 us (29%)
  waiting for transfers between devices  11.6 us (23%)
    ppermute x14, starting transfers between devices, exchange(): return lax.ppermute(array, axis, [(i, i ^ step) for i in range(count)])  14.3 us
    pallas_call x1, Pallas kernels, ffn(): pl.pallas_call(functools.partial(ffn_kernel, blocks, hids, (slots, part,...  13.6 us
    ppermute x14, waiting for transfers between devices, exchange(): return lax.ppermute(array, axis, [(i, i ^ step) for i in range(count)])  11.6 us
    pallas_call x1, Pallas kernels, early(): pl.pallas_call(early_kernel, out_shape=pltpu.VMEM((depth, shard), jnp.bfl...  4.58 us
    pallas_call x1, Pallas kernels, kept_part(): pl.pallas_call(kept_kernel, out_shape=jax.ShapeDtypeStruct((rows, width),...  2.92 us
    pallas_call x1, Pallas kernels, norm(): pl.pallas_call(functools.partial(norm_kernel, lanes), out_shape=(jax.Shap...  1.55 us
  transfers between devices with their start and end apart: 14, of which 9 were waited for; matrix products, arithmetic and copies ran while one was open for 0% of the time, Pallas kernels for 15%

profile of v2, /device:TPU:0, one launch (start us, length us, event | category | flops | bytes accessed | tf_op | source)
XLA Modules:
  0.0 49.6 jit_solution(13540067845289698142)
XLA Ops:
  0.0 0.0 copy-start
  0.0 1.5 %norm.1 = (bf16[4,3072]{1,0:T(4,128)(2,1)S(1)}, bf16[4,3072]{1,0:T(4,128)(2,1)S(1)}, bf16[4,3072]{1,0:T(4,128)(2,1)S(1)}, bf16[4,3072]{1,0:T(4,128)(2,1)S(1)}) custom-call(bf16[16,6144]{1,0:T(8,128)(2,1)} %refs_0_.1, s32[16]{0:T(128)} %refs_1_.1, s32[1,16]{1,0:T(1,128)} %refs_2_.1, f32[8,6144]{1,0:T(8,128)} %refs_3_.1), custom_call_target="tpu_custom_call" | custom-call | bytes 50331648 | tf_op jit(solution)/shard_map/norm/pallas_call | solution.py:70
  1.6 3.1 %collective-permute-start = (bf16[4,3072]{1,0:T(4,128)(2,1)S(1)}, bf16[4,3072]{1,0:T(4,128)(2,1)S(1)}, u32[]{:S(2)}, u32[]{:S(2)}) collective-permute-start(bf16[4,3072]{1,0:T(4,128)(2,1)S(1)} %get-tuple-element.22), channel_id=1, source_target_pairs={{0,2},{2,0},{4,6},{6,4},{1,3},{3,1},{5,7},{7,5},{8,10},{10,8},{12,... | collective-permute-start | bytes 73736 | tf_op jit(solution)/shard_map/ppermute | solution.py:26
  4.6 2.6 %collective-permute-start.1 = (bf16[4,3072]{1,0:T(4,128)(2,1)S(1)}, bf16[4,3072]{1,0:T(4,128)(2,1)S(1)}, u32[]{:S(2)}, u32[]{:S(2)}) collective-permute-start(bf16[4,3072]{1,0:T(4,128)(2,1)S(1)} %get-tuple-element.23), channel_id=1, source_target_pairs={{0,4},{2,6},{4,0},{6,2},{1,5},{3,7},{5,1},{7,3},{8,12},{10,14},{12... | collective-permute-start | bytes 73736 | tf_op jit(solution)/shard_map/ppermute | solution.py:26
  7.2 0.0 collective-permute-start.2
  7.2 0.0 collective-permute-done.refs_1_
  7.2 2.5 %collective-permute-done.1.refs_2_ = bf16[4,3072]{1,0:T(4,128)(2,1)S(1)} collective-permute-done((bf16[4,3072]{1,0:T(4,128)(2,1)S(1)}, bf16[4,3072]{1,0:T(4,128)(2,1)S(1)}, u32[]{:S(2)}, u32[]{:S(2)}) %collective-permute-start.1) | collective-permute-done | bytes 24608 | tf_op jit(solution)/shard_map/ppermute | solution.py:26
  9.7 3.1 %collective-permute-done.2.refs_3_ = bf16[4,3072]{1,0:T(4,128)(2,1)S(1)} collective-permute-done((bf16[4,3072]{1,0:T(4,128)(2,1)S(1)}, bf16[4,3072]{1,0:T(4,128)(2,1)S(1)}, u32[]{:S(2)}, u32[]{:S(2)}) %collective-permute-start.2) | collective-permute-done | bytes 24608 | tf_op jit(solution)/shard_map/ppermute | solution.py:26
  12.9 0.2 arrange.1.after_ref.refs_0_
  13.0 2.5 %collective-permute-start.5 = (bf16[16,3072]{1,0:T(8,128)(2,1)S(1)}, bf16[16,3072]{1,0:T(8,128)(2,1)S(1)}, u32[]{:S(2)}, u32[]{:S(2)}) collective-permute-start(bf16[16,3072]{1,0:T(8,128)(2,1)S(1)} %arrange.1.after_ref.refs_0_), channel_id=1, source_target_pairs={{0,24},{8,16},{16,8},{24,0},{1,25},{9,17},{17,9},{25,1},{2,26},{10... | collective-permute-start | bytes 294920 | tf_op jit(solution)/shard_map/ppermute | solution.py:26
  15.5 0.5 %collective-permute-start.4 = (bf16[16,3072]{1,0:T(8,128)(2,1)S(1)}, bf16[16,3072]{1,0:T(8,128)(2,1)S(1)}, u32[]{:S(2)}, u32[]{:S(2)}) collective-permute-start(bf16[16,3072]{1,0:T(8,128)(2,1)S(1)} %arrange.1.after_ref.refs_0_), channel_id=1, source_target_pairs={{0,16},{8,24},{16,0},{24,8},{1,17},{9,25},{17,1},{25,9},{2,18},{10... | collective-permute-start | bytes 294920 | tf_op jit(solution)/shard_map/ppermute | solution.py:26
  16.0 0.5 %collective-permute-start.3 = (bf16[16,3072]{1,0:T(8,128)(2,1)S(1)}, bf16[16,3072]{1,0:T(8,128)(2,1)S(1)}, u32[]{:S(2)}, u32[]{:S(2)}) collective-permute-start(bf16[16,3072]{1,0:T(8,128)(2,1)S(1)} %arrange.1.after_ref.refs_0_), channel_id=1, source_target_pairs={{0,8},{8,0},{16,24},{24,16},{1,9},{9,1},{17,25},{25,17},{2,10},{10... | collective-permute-start | bytes 294920 | tf_op jit(solution)/shard_map/ppermute | solution.py:26
  16.6 4.6 %early.1.refs_9_ = bf16[3072,2048]{1,0:T(8,128)(2,1)S(1)} custom-call(bf16[16,3072]{1,0:T(8,128)(2,1)S(1)} %arrange.1.after_ref.refs_0_, bf16[6144,2048]{1,0:T(8,128)(2,1)} %refs_10_.1), custom_call_target="tpu_custom_call" | custom-call | bytes 12582912 | tf_op jit(solution)/shard_map/early/pallas_call | solution.py:129
  21.2 0.0 collective-permute-done.5.refs_3_
  21.2 0.0 collective-permute-done.4.refs_2_
  21.2 0.0 collective-permute-done.3.refs_1_
  21.2 0.1 collective-permute-start.6
  21.3 0.5 %collective-permute-start.7 = (bf16[16,3072]{1,0:T(8,128)(2,1)S(1)}, bf16[16,3072]{1,0:T(8,128)(2,1)S(1)}, u32[]{:S(2)}, u32[]{:S(2)}) collective-permute-start(bf16[16,3072]{1,0:T(8,128)(2,1)S(1)} %collective-permute-done.3.refs_1_), channel_id=1, source_target_pairs={{0,1},{1,0},{2,3},{3,2},{4,5},{5,4},{6,7},{7,6},{8,9},{9,8},{10,11... | collective-permute-start | bytes 294920 | tf_op jit(solution)/shard_map/ppermute | solution.py:26
  21.8 0.1 collective-permute-start.8
  21.9 0.4 collective-permute-start.9
  22.3 0.3 collective-permute-done.6.refs_4_
  22.6 0.2 collective-permute-done.7.refs_5_
  22.7 0.4 collective-permute-done.8.refs_6_
  23.1 0.2 collective-permute-done.9.refs_7_
  23.2 0.0 copy-done
  23.2 13.6 %ffn.1 = (bf16[64,2048]{1,0:T(8,128)(2,1)S(1)}, bf16[2048,2048]{1,0:T(8,128)(2,1)S(1)}, bf16[64,3072]{1,0:T(8,128)(2,1)S(1)}) custom-call(bf16[16,3072]{1,0:T(8,128)(2,1)S(1)} %arrange.1.after_ref.refs_0_, bf16[16,3072]{1,0:T(8,128)(2,1)S(1)} %collective-permute-done.3.refs_1_, bf16[16,3072]{1,0:T(8,128)(2,1)S(1)} %collective-permute-done.4.refs_2_, ...), custom_call_target="tpu_custom_call" | custom-call | flops 4026531840 | bytes 50331648 | tf_op jit(solution)/shard_map/ffn/pallas_call | solution.py:287
  36.9 0.4 collective-permute-start.10
  37.3 2.9 %kept_part.1.refs_0_ = f32[64,3072]{1,0:T(8,128)S(1)} custom-call(bf16[64,2048]{1,0:T(8,128)(2,1)S(1)} %get-tuple-element.30.hidden_ref, bf16[2048,2048]{1,0:T(8,128)(2,1)S(1)} %get-tuple-element.31.kept_ref, bf16[2048,6144]{1,0:T(8,128)(2,1)} %down_ref.1), custom_call_target="tpu_custom_call" | custom-call | flops 805306368 | bytes 12582912 | tf_op jit(solution)/shard_map/kept_part/pallas_call | solution.py:347
  40.2 0.0 collective-permute-done.10.refs_1_
  40.3 0.1 hid_sum.1
  40.3 1.6 %collective-permute-start.11 = (bf16[16,3072]{1,0:T(8,128)(2,1)S(1)}, bf16[16,3072]{1,0:T(8,128)(2,1)S(1)}, u32[]{:S(2)}, u32[]{:S(2)}) collective-permute-start(bf16[16,3072]{1,0:T(8,128)(2,1)S(1)} %get-tuple-element.34), channel_id=1, source_target_pairs={{0,8},{8,0},{16,24},{24,16},{1,9},{9,1},{17,25},{25,17},{2,10},{10... | collective-permute-start | bytes 294920 | tf_op jit(solution)/shard_map/ppermute | solution.py:26
  41.9 1.5 %collective-permute-start.12 = (bf16[16,3072]{1,0:T(8,128)(2,1)S(1)}, bf16[16,3072]{1,0:T(8,128)(2,1)S(1)}, u32[]{:S(2)}, u32[]{:S(2)}) collective-permute-start(bf16[16,3072]{1,0:T(8,128)(2,1)S(1)} %get-tuple-element.35), channel_id=1, source_target_pairs={{0,16},{8,24},{16,0},{24,8},{1,17},{9,25},{17,1},{25,9},{2,18},{10... | collective-permute-start | bytes 294920 | tf_op jit(solution)/shard_map/ppermute | solution.py:26
  43.4 0.5 collective-permute-start.13
  43.9 1.4 %collective-permute-done.11.refs_1_ = bf16[16,3072]{1,0:T(8,128)(2,1)S(1)} collective-permute-done((bf16[16,3072]{1,0:T(8,128)(2,1)S(1)}, bf16[16,3072]{1,0:T(8,128)(2,1)S(1)}, u32[]{:S(2)}, u32[]{:S(2)}) %collective-permute-start.11) | collective-permute-done | bytes 98336 | tf_op jit(solution)/shard_map/ppermute | solution.py:26
  45.2 2.4 %collective-permute-done.12.refs_2_ = bf16[16,3072]{1,0:T(8,128)(2,1)S(1)} collective-permute-done((bf16[16,3072]{1,0:T(8,128)(2,1)S(1)}, bf16[16,3072]{1,0:T(8,128)(2,1)S(1)}, u32[]{:S(2)}, u32[]{:S(2)}) %collective-permute-start.12) | collective-permute-done | bytes 98336 | tf_op jit(solution)/shard_map/ppermute | solution.py:26
  47.7 1.3 %collective-permute-done.13.refs_3_ = bf16[16,3072]{1,0:T(8,128)(2,1)S(1)} collective-permute-done((bf16[16,3072]{1,0:T(8,128)(2,1)S(1)}, bf16[16,3072]{1,0:T(8,128)(2,1)S(1)}, u32[]{:S(2)}, u32[]{:S(2)}) %collective-permute-start.13) | collective-permute-done | bytes 98336 | tf_op jit(solution)/shard_map/ppermute | solution.py:26
  48.9 0.7 %blk_sum.1 = bf16[16,3072]{1,0:T(8,128)(2,1)} custom-call(f32[16,3072]{1,0:T(8,128)S(1)} %get-tuple-element.33.refs_0_, bf16[16,3072]{1,0:T(8,128)(2,1)S(1)} %collective-permute-done.11.refs_1_, bf16[16,3072]{1,0:T(8,128)(2,1)S(1)} %collective-permute-done.12.refs_2_, bf16[16,3072]{1,0:T(8,128)(2,1)S(1)} %collective-permute-done.13.refs_3_), custom_call_target="tpu_custom_call" | custom-call | tf_op jit(solution)/shard_map/blk_sum/pallas_call | solution.py:396
Async XLA Ops:
  0.0 23.2 %copy-start = (bf16[6144,2048]{1,0:T(8,128)(2,1)S(1)}, bf16[6144,2048]{1,0:T(8,128)(2,1)}, u32[]{:S(2)}) copy-start(bf16[6144,2048]{1,0:T(8,128)(2,1)} %refs_8_.1) | copy-start | bytes 75497472
  1.6 5.7 %collective-permute-start = (bf16[4,3072]{1,0:T(4,128)(2,1)S(1)}, bf16[4,3072]{1,0:T(4,128)(2,1)S(1)}, u32[]{:S(2)}, u32[]{:S(2)}) collective-permute-start(bf16[4,3072]{1,0:T(4,128)(2,1)S(1)} %get-tuple-element.22), channel_id=1, source_target_pairs={{0,2},{2,0},{4,6},{6,4},{1,3},{3,1},{5,7},{7,5},{8,10},{10,8},{12,... | collective-permute-start | bytes 73736 | tf_op jit(solution)/shard_map/ppermute | solution.py:26
  4.6 5.1 %collective-permute-start.1 = (bf16[4,3072]{1,0:T(4,128)(2,1)S(1)}, bf16[4,3072]{1,0:T(4,128)(2,1)S(1)}, u32[]{:S(2)}, u32[]{:S(2)}) collective-permute-start(bf16[4,3072]{1,0:T(4,128)(2,1)S(1)} %get-tuple-element.23), channel_id=1, source_target_pairs={{0,4},{2,6},{4,0},{6,2},{1,5},{3,7},{5,1},{7,3},{8,12},{10,14},{12... | collective-permute-start | bytes 73736 | tf_op jit(solution)/shard_map/ppermute | solution.py:26
  7.2 5.6 %collective-permute-start.2 = (bf16[4,3072]{1,0:T(4,128)(2,1)S(1)}, bf16[4,3072]{1,0:T(4,128)(2,1)S(1)}, u32[]{:S(2)}, u32[]{:S(2)}) collective-permute-start(bf16[4,3072]{1,0:T(4,128)(2,1)S(1)} %get-tuple-element.24), channel_id=1, source_target_pairs={{0,6},{2,4},{4,2},{6,0},{1,7},{3,5},{5,3},{7,1},{8,14},{10,12},{12... | collective-permute-start | bytes 73736 | tf_op jit(solution)/shard_map/ppermute | solution.py:26
  13.0 8.1 %collective-permute-start.5 = (bf16[16,3072]{1,0:T(8,128)(2,1)S(1)}, bf16[16,3072]{1,0:T(8,128)(2,1)S(1)}, u32[]{:S(2)}, u32[]{:S(2)}) collective-permute-start(bf16[16,3072]{1,0:T(8,128)(2,1)S(1)} %arrange.1.after_ref.refs_0_), channel_id=1, source_target_pairs={{0,24},{8,16},{16,8},{24,0},{1,25},{9,17},{17,9},{25,1},{2,26},{10... | collective-permute-start | bytes 294920 | tf_op jit(solution)/shard_map/ppermute | solution.py:26
  15.5 5.6 %collective-permute-start.4 = (bf16[16,3072]{1,0:T(8,128)(2,1)S(1)}, bf16[16,3072]{1,0:T(8,128)(2,1)S(1)}, u32[]{:S(2)}, u32[]{:S(2)}) collective-permute-start(bf16[16,3072]{1,0:T(8,128)(2,1)S(1)} %arrange.1.after_ref.refs_0_), channel_id=1, source_target_pairs={{0,16},{8,24},{16,0},{24,8},{1,17},{9,25},{17,1},{25,9},{2,18},{10... | collective-permute-start | bytes 294920 | tf_op jit(solution)/shard_map/ppermute | solution.py:26
  16.0 5.2 %collective-permute-start.3 = (bf16[16,3072]{1,0:T(8,128)(2,1)S(1)}, bf16[16,3072]{1,0:T(8,128)(2,1)S(1)}, u32[]{:S(2)}, u32[]{:S(2)}) collective-permute-start(bf16[16,3072]{1,0:T(8,128)(2,1)S(1)} %arrange.1.after_ref.refs_0_), channel_id=1, source_target_pairs={{0,8},{8,0},{16,24},{24,16},{1,9},{9,1},{17,25},{25,17},{2,10},{10... | collective-permute-start | bytes 294920 | tf_op jit(solution)/shard_map/ppermute | solution.py:26
  21.2 1.4 %collective-permute-start.6 = (bf16[16,3072]{1,0:T(8,128)(2,1)S(1)}, bf16[16,3072]{1,0:T(8,128)(2,1)S(1)}, u32[]{:S(2)}, u32[]{:S(2)}) collective-permute-start(bf16[16,3072]{1,0:T(8,128)(2,1)S(1)} %arrange.1.after_ref.refs_0_), channel_id=1, source_target_pairs={{0,1},{1,0},{2,3},{3,2},{4,5},{5,4},{6,7},{7,6},{8,9},{9,8},{10,11... | collective-permute-start | bytes 294920 | tf_op jit(solution)/shard_map/ppermute | solution.py:26
  21.3 1.4 %collective-permute-start.7 = (bf16[16,3072]{1,0:T(8,128)(2,1)S(1)}, bf16[16,3072]{1,0:T(8,128)(2,1)S(1)}, u32[]{:S(2)}, u32[]{:S(2)}) collective-permute-start(bf16[16,3072]{1,0:T(8,128)(2,1)S(1)} %collective-permute-done.3.refs_1_), channel_id=1, source_target_pairs={{0,1},{1,0},{2,3},{3,2},{4,5},{5,4},{6,7},{7,6},{8,9},{9,8},{10,11... | collective-permute-start | bytes 294920 | tf_op jit(solution)/shard_map/ppermute | solution.py:26
  21.8 1.3 %collective-permute-start.8 = (bf16[16,3072]{1,0:T(8,128)(2,1)S(1)}, bf16[16,3072]{1,0:T(8,128)(2,1)S(1)}, u32[]{:S(2)}, u32[]{:S(2)}) collective-permute-start(bf16[16,3072]{1,0:T(8,128)(2,1)S(1)} %collective-permute-done.4.refs_2_), channel_id=1, source_target_pairs={{0,1},{1,0},{2,3},{3,2},{4,5},{5,4},{6,7},{7,6},{8,9},{9,8},{10,11... | collective-permute-start | bytes 294920 | tf_op jit(solution)/shard_map/ppermute | solution.py:26
  21.9 1.4 %collective-permute-start.9 = (bf16[16,3072]{1,0:T(8,128)(2,1)S(1)}, bf16[16,3072]{1,0:T(8,128)(2,1)S(1)}, u32[]{:S(2)}, u32[]{:S(2)}) collective-permute-start(bf16[16,3072]{1,0:T(8,128)(2,1)S(1)} %collective-permute-done.5.refs_3_), channel_id=1, source_target_pairs={{0,1},{1,0},{2,3},{3,2},{4,5},{5,4},{6,7},{7,6},{8,9},{9,8},{10,11... | collective-permute-start | bytes 294920 | tf_op jit(solution)/shard_map/ppermute | solution.py:26
  36.9 3.4 %collective-permute-start.10 = (bf16[64,3072]{1,0:T(8,128)(2,1)S(1)}, bf16[64,3072]{1,0:T(8,128)(2,1)S(1)}, u32[]{:S(2)}, u32[]{:S(2)}) collective-permute-start(bf16[64,3072]{1,0:T(8,128)(2,1)S(1)} %get-tuple-element.32), channel_id=1, source_target_pairs={{0,1},{1,0},{2,3},{3,2},{4,5},{5,4},{6,7},{7,6},{8,9},{9,8},{10,11... | collective-permute-start | bytes 1179656 | tf_op jit(solution)/shard_map/ppermute | solution.py:26
  40.3 4.9 %collective-permute-start.11 = (bf16[16,3072]{1,0:T(8,128)(2,1)S(1)}, bf16[16,3072]{1,0:T(8,128)(2,1)S(1)}, u32[]{:S(2)}, u32[]{:S(2)}) collective-permute-start(bf16[16,3072]{1,0:T(8,128)(2,1)S(1)} %get-tuple-element.34), channel_id=1, source_target_pairs={{0,8},{8,0},{16,24},{24,16},{1,9},{9,1},{17,25},{25,17},{2,10},{10... | collective-permute-start | bytes 294920 | tf_op jit(solution)/shard_map/ppermute | solution.py:26
  41.9 5.8 %collective-permute-start.12 = (bf16[16,3072]{1,0:T(8,128)(2,1)S(1)}, bf16[16,3072]{1,0:T(8,128)(2,1)S(1)}, u32[]{:S(2)}, u32[]{:S(2)}) collective-permute-start(bf16[16,3072]{1,0:T(8,128)(2,1)S(1)} %get-tuple-element.35), channel_id=1, source_target_pairs={{0,16},{8,24},{16,0},{24,8},{1,17},{9,25},{17,1},{25,9},{2,18},{10... | collective-permute-start | bytes 294920 | tf_op jit(solution)/shard_map/ppermute | solution.py:26
  43.4 5.5 %collective-permute-start.13 = (bf16[16,3072]{1,0:T(8,128)(2,1)S(1)}, bf16[16,3072]{1,0:T(8,128)(2,1)S(1)}, u32[]{:S(2)}, u32[]{:S(2)}) collective-permute-start(bf16[16,3072]{1,0:T(8,128)(2,1)S(1)} %get-tuple-element.36), channel_id=1, source_target_pairs={{0,24},{8,16},{16,8},{24,0},{1,25},{9,17},{17,9},{25,1},{2,26},{10... | collective-permute-start | bytes 294920 | tf_op jit(solution)/shard_map/ppermute | solution.py:26

commit v3 on v2

--- a/solution.py
+++ b/solution.py
@@ -115,19 +115,23 @@
     )(*pieces)
 
 
-def early_kernel(after_ref, up_ref, out_ref, sem):
-    depth = out_ref.shape[0]
-    start = pl.multiple_of(lax.axis_index("hid") * depth, depth)
-    copy = pltpu.make_async_copy(up_ref.at[pl.ds(start, depth), :], out_ref, sem)
+def even(total, most):
+    return next(size for size in range(min(most, total), 0, -128) if total % size == 0)
+
+
+def early_kernel(width, after_ref, up_ref, out_ref, sem):
+    start = pl.multiple_of(lax.axis_index("hid") * width, width)
+    copy = pltpu.make_async_copy(up_ref.at[pl.ds(start, out_ref.shape[0]), :], out_ref, sem)
     copy.start()
     copy.wait()
 
 
 def early(after, up_weight):
-    depth = up_weight.shape[0] // lax.axis_size("hid")
+    width = up_weight.shape[0] // lax.axis_size("hid")
+    depth = width - even(width, 1024)
     shard = up_weight.shape[1]
     return pl.pallas_call(
-        early_kernel,
+        functools.partial(early_kernel, width),
         out_shape=pltpu.VMEM((depth, shard), jnp.bfloat16),
         in_specs=[ANYWHERE, ANYWHERE],
         out_specs=IN_VMEM,
@@ -140,10 +144,6 @@
     )(after, up_weight)
 
 
-def even(total, most):
-    return next(size for size in range(min(most, total), 0, -128) if total % size == 0)
-
-
 def ffn_kernel(blocks, hids, plan, *refs):
     slots, part, up_cols, down_rows, down_cols = plan
     count = blocks * hids
@@ -151,7 +151,7 @@
     gate_ref, held_ref, up_ref, down_ref = refs[count : count + 4]
     hidden_ref, kept = refs[count + 4 : count + 6]
     out_refs = refs[count + 6 : count + 5 + hids]
-    panel, up_sum, ring, ring_sems, kept_sem = refs[count + 5 + hids :]
+    panel, up_sum, act, ring, ring_sems, kept_sems = refs[count + 5 + hids :]
     rows, depth = panel.shape
     each = rows // blocks
     shard = gate_ref.shape[1]
@@ -159,14 +159,16 @@
     me = lax.axis_index("hid")
     inside, across = width // part, shard // up_cols
     deep, wide = shard // down_rows, width // down_cols
-    up_count = (hids - 1) * inside * across
+    skip = held_ref.shape[0] // part
+    up_count = (hids * inside - skip) * across
     down_count = (hids - 1) * wide * deep
 
     def side_start(side):
         return jnp.bitwise_xor(me, side) * width
 
     def up_copy(n):
-        side, p, c = n // (inside * across) + 1, n // across % inside, n % across
+        u, c = n // across + skip, n % across
+        side, p = u // inside, u % inside
         return pltpu.make_async_copy(
             up_ref.at[
                 pl.ds(pl.multiple_of(side_start(side) + p * part, part), part),
@@ -188,9 +190,14 @@
             ring_sems.at[slot],
         )
 
-    kept_copy = pltpu.make_async_copy(
-        down_ref.at[:, pl.ds(pl.multiple_of(me * width, 128), kept.shape[1])], kept, kept_sem
-    )
+    def kept_copy(n):
+        size = kept.shape[1] // 2
+        start = pl.multiple_of(me * width + n * size, 128)
+        return pltpu.make_async_copy(
+            down_ref.at[:, pl.ds(start, size)],
+            kept.at[:, n * size : (n + 1) * size],
+            kept_sems.at[n],
+        )
 
     def start_next(n):
         if isinstance(n, int):
@@ -210,14 +217,15 @@
 
     for n in range(slots):
         start_next(n)
+    kept_copy(0).start()
     for side in range(hids):
         start = pl.multiple_of(side_start(side), width)
         for step in range(blocks):
             panel[step * each : (step + 1) * each, pl.ds(start, width)] = panel_refs[
                 side * blocks + step
             ][...]
-    chunk = min(1024, shard)
-    own = pl.ds(pl.multiple_of(me * width, width), width)
+    chunk = even(shard, 1024)
+    own = pl.ds(pl.multiple_of(me * width, width), skip * part)
 
     @pl.loop(0, shard // chunk)
     def _(c):
@@ -226,12 +234,23 @@
             panel[:, own], held_ref[:, columns], preferred_element_type=jnp.float32
         )
 
-    @pl.loop(0, (hids - 1) * inside)
+    def gate_act(columns):
+        gate = jnp.dot(panel[...], gate_ref[:, columns], preferred_element_type=jnp.float32)
+        return gate / (1.0 + jnp.exp(-gate))
+
+    before = shard // chunk // 2
+
+    @pl.loop(0, before)
+    def _(c):
+        columns = pl.ds(pl.multiple_of(c * chunk, chunk), chunk)
+        act[:, columns] = gate_act(columns)
+
+    @pl.loop(skip, hids * inside)
     def _(u):
-        side, p = u // inside + 1, u % inside
+        side, p = u // inside, u % inside
         x = panel[:, pl.ds(pl.multiple_of(side_start(side) + p * part, part), part)]
         for c in range(across):
-            n = u * across + c
+            n = (u - skip) * across + c
             up_copy(n).wait()
             columns = slice(c * up_cols, (c + 1) * up_cols)
             up_sum[:, columns] += jnp.dot(
@@ -241,15 +260,16 @@
             )
             start_next(n + slots)
 
-    kept_copy.start()
-
-    @pl.loop(0, shard // chunk)
+    kept_copy(1).start()
+
+    @pl.loop(before, shard // chunk)
     def _(c):
         columns = pl.ds(pl.multiple_of(c * chunk, chunk), chunk)
-        gate = jnp.dot(panel[...], gate_ref[:, columns], preferred_element_type=jnp.float32)
-        hidden_ref[:, columns] = (gate / (1.0 + jnp.exp(-gate)) * up_sum[:, columns]).astype(
-            jnp.bfloat16
-        )
+        hidden_ref[:, columns] = (gate_act(columns) * up_sum[:, columns]).astype(jnp.bfloat16)
+
+    done = slice(0, before * chunk)
+    if before:
+        hidden_ref[:, done] = (act[:, done] * up_sum[:, done]).astype(jnp.bfloat16)
 
     for side in range(1, hids):
 
@@ -269,7 +289,8 @@
             columns = pl.ds(pl.multiple_of(c * down_cols, 128), down_cols)
             out_refs[side - 1][:, columns] = total.astype(jnp.bfloat16)
 
-    kept_copy.wait()
+    for n in range(2):
+        kept_copy(n).wait()
 
 
 def ffn(panels, gate_weight, up_held, up_weight, down_weight, blocks):
@@ -279,7 +300,7 @@
     shard = gate_weight.shape[1]
     part, up_cols = even(width, 1024), even(shard, 1024)
     down_rows, down_cols = even(shard, 1024), even(width, 1024)
-    slots = 4
+    slots = 6
     outs = [
         pltpu.VMEM((rows, shard), jnp.bfloat16),
         pltpu.VMEM((shard, (width // down_cols + 1) // 2 * down_cols), jnp.bfloat16),
@@ -294,11 +315,12 @@
         scratch_shapes=[
             pltpu.VMEM((rows, depth), jnp.bfloat16),
             pltpu.VMEM((rows, shard), jnp.float32),
+            pltpu.VMEM((rows, max(128, shard // 2)), jnp.float32),
             pltpu.VMEM((slots, max(part, down_rows), max(up_cols, down_cols)), jnp.bfloat16),
             pltpu.SemaphoreType.DMA((slots,)),
-            pltpu.SemaphoreType.DMA(()),
+            pltpu.SemaphoreType.DMA((2,)),
         ],
-        compiler_params=pltpu.CompilerParams(vmem_limit_bytes=13 * MIB),
+        compiler_params=pltpu.CompilerParams(vmem_limit_bytes=17 * MIB),
         cost_estimate=pl.CostEstimate(
             flops=4 * rows * depth * shard + 2 * rows * shard * (depth - width),
             bytes_accessed=4 * depth * shard,
@@ -419,11 +441,12 @@
         [pieces[0]] + [exchange(pieces[step], "regroup", step) for step in range(1, lanes)]
     )
     halves = [half] + [exchange(half, "blk", step) for step in range(1, blocks)]
-    up_held = held(early(half, up_weight))
-    halves, up_held = lax.optimization_barrier((halves, up_held))
-    up_held = held(up_held)
+    up_held = early(half, up_weight)
+    for step in range(1, blocks):
+        halves[step], up_held = lax.optimization_barrier((halves[step], up_held))
     panels = halves + [exchange(part, "hid", side) for side in range(1, hids) for part in halves]
     panels = [held(part) for part in panels]
+    up_held = held(up_held)
     hidden, kept, *sent = ffn(panels, gate_weight, up_held, up_weight, down_weight, blocks)
     hidden, kept = held(hidden), held(kept)
     came = [exchange(part, "hid", step + 1) for step, part in enumerate(sent)]

time: 49.8 us -> 48.3 us (0.970)
  Pallas kernels: 23.6 us -> 22.1 us
  waiting for transfers between devices: 11.6 us -> 12.5 us
  starting transfers between devices: 14.3 us -> 13.5 us
    pallas_call x1, Pallas kernels: 4.58 us -> 3.39 us  [early(): pl.pallas_call(functools.partial(early_kernel, width), out_shape=pltpu.VM...]
    ppermute x14, waiting for transfers between devices: 11.6 us -> 12.5 us  [exchange(): return lax.ppermute(array, axis, [(i, i ^ step) for i in range(count)])]
    ppermute x14, starting transfers between devices: 14.3 us -> 13.5 us  [exchange(): return lax.ppermute(array, axis, [(i, i ^ step) for i in range(count)])]
  transfers between devices with their start and end apart: 14 -> 14, of which waited for: 9 -> 8; matrix products, arithmetic and copies ran while one was open for 0% -> 0% of each run, Pallas kernels for 15% -> 13%
where the time goes in v3:
time: 48.3 us; the launch traced here: 48.2 us
  Pallas kernels  22.1 us (46%)
  starting transfers between devices  13.5 us (28%)
  waiting for transfers between devices  12.5 us (26%)
    ppermute x14, starting transfers between devices, exchange(): return lax.ppermute(array, axis, [(i, i ^ step) for i in range(count)])  13.5 us
    pallas_call x1, Pallas kernels, ffn(): pl.pallas_call(functools.partial(ffn_kernel, blocks, hids, (slots, part,...  13.3 us
    ppermute x14, waiting for transfers between devices, exchange(): return lax.ppermute(array, axis, [(i, i ^ step) for i in range(count)])  12.5 us
    pallas_call x1, Pallas kernels, early(): pl.pallas_call(functools.partial(early_kernel, width), out_shape=pltpu.VM...  3.39 us
    pallas_call x1, Pallas kernels, kept_part(): pl.pallas_call(kept_kernel, out_shape=jax.ShapeDtypeStruct((rows, width),...  2.92 us
    pallas_call x1, Pallas kernels, norm(): pl.pallas_call(functools.partial(norm_kernel, lanes), out_shape=(jax.Shap...  1.55 us
  transfers between devices with their start and end apart: 14, of which 8 were waited for; matrix products, arithmetic and copies ran while one was open for 0% of the time, Pallas kernels for 13%

profile of v3, /device:TPU:0, one launch (start us, length us, event | category | flops | bytes accessed | tf_op | source)
XLA Modules:
  0.0 48.2 jit_solution(12831240556069607340)
XLA Ops:
  0.0 0.0 copy-start
  0.0 1.5 %norm.1 = (bf16[4,3072]{1,0:T(4,128)(2,1)S(1)}, bf16[4,3072]{1,0:T(4,128)(2,1)S(1)}, bf16[4,3072]{1,0:T(4,128)(2,1)S(1)}, bf16[4,3072]{1,0:T(4,128)(2,1)S(1)}) custom-call(bf16[16,6144]{1,0:T(8,128)(2,1)} %refs_0_.1, s32[16]{0:T(128)} %refs_1_.1, s32[1,16]{1,0:T(1,128)} %refs_2_.1, f32[8,6144]{1,0:T(8,128)} %refs_3_.1), custom_call_target="tpu_custom_call" | custom-call | bytes 50331648 | tf_op jit(solution)/shard_map/norm/pallas_call | solution.py:70
  1.6 3.1 %collective-permute-start = (bf16[4,3072]{1,0:T(4,128)(2,1)S(1)}, bf16[4,3072]{1,0:T(4,128)(2,1)S(1)}, u32[]{:S(2)}, u32[]{:S(2)}) collective-permute-start(bf16[4,3072]{1,0:T(4,128)(2,1)S(1)} %get-tuple-element.23), channel_id=1, source_target_pairs={{0,2},{2,0},{4,6},{6,4},{1,3},{3,1},{5,7},{7,5},{8,10},{10,8},{12,... | collective-permute-start | bytes 73736 | tf_op jit(solution)/shard_map/ppermute | solution.py:26
  4.6 2.6 %collective-permute-start.1 = (bf16[4,3072]{1,0:T(4,128)(2,1)S(1)}, bf16[4,3072]{1,0:T(4,128)(2,1)S(1)}, u32[]{:S(2)}, u32[]{:S(2)}) collective-permute-start(bf16[4,3072]{1,0:T(4,128)(2,1)S(1)} %get-tuple-element.24), channel_id=1, source_target_pairs={{0,4},{2,6},{4,0},{6,2},{1,5},{3,7},{5,1},{7,3},{8,12},{10,14},{12... | collective-permute-start | bytes 73736 | tf_op jit(solution)/shard_map/ppermute | solution.py:26
  7.2 0.0 collective-permute-start.2
  7.2 0.0 collective-permute-done.refs_1_
  7.2 2.5 %collective-permute-done.1.refs_2_ = bf16[4,3072]{1,0:T(4,128)(2,1)S(1)} collective-permute-done((bf16[4,3072]{1,0:T(4,128)(2,1)S(1)}, bf16[4,3072]{1,0:T(4,128)(2,1)S(1)}, u32[]{:S(2)}, u32[]{:S(2)}) %collective-permute-start.1) | collective-permute-done | bytes 24608 | tf_op jit(solution)/shard_map/ppermute | solution.py:26
  9.7 3.1 %collective-permute-done.2.refs_3_ = bf16[4,3072]{1,0:T(4,128)(2,1)S(1)} collective-permute-done((bf16[4,3072]{1,0:T(4,128)(2,1)S(1)}, bf16[4,3072]{1,0:T(4,128)(2,1)S(1)}, u32[]{:S(2)}, u32[]{:S(2)}) %collective-permute-start.2) | collective-permute-done | bytes 24608 | tf_op jit(solution)/shard_map/ppermute | solution.py:26
  12.9 0.2 arrange.1.after_ref.refs_0_
  13.0 1.6 %collective-permute-start.3 = (bf16[16,3072]{1,0:T(8,128)(2,1)S(1)}, bf16[16,3072]{1,0:T(8,128)(2,1)S(1)}, u32[]{:S(2)}, u32[]{:S(2)}) collective-permute-start(bf16[16,3072]{1,0:T(8,128)(2,1)S(1)} %arrange.1.after_ref.refs_0_), channel_id=1, source_target_pairs={{0,8},{8,0},{16,24},{24,16},{1,9},{9,1},{17,25},{25,17},{2,10},{10... | collective-permute-start | bytes 294920 | tf_op jit(solution)/shard_map/ppermute | solution.py:26
  14.6 1.5 %collective-permute-start.4 = (bf16[16,3072]{1,0:T(8,128)(2,1)S(1)}, bf16[16,3072]{1,0:T(8,128)(2,1)S(1)}, u32[]{:S(2)}, u32[]{:S(2)}) collective-permute-start(bf16[16,3072]{1,0:T(8,128)(2,1)S(1)} %arrange.1.after_ref.refs_0_), channel_id=1, source_target_pairs={{0,16},{8,24},{16,0},{24,8},{1,17},{9,25},{17,1},{25,9},{2,18},{10... | collective-permute-start | bytes 294920 | tf_op jit(solution)/shard_map/ppermute | solution.py:26
  16.1 0.5 collective-permute-start.5
  16.6 0.0 collective-permute-start.6
  16.6 3.4 %early.1.refs_9_ = bf16[2048,2048]{1,0:T(8,128)(2,1)S(1)} custom-call(bf16[16,3072]{1,0:T(8,128)(2,1)S(1)} %arrange.1.after_ref.refs_0_, bf16[6144,2048]{1,0:T(8,128)(2,1)} %refs_10_.1), custom_call_target="tpu_custom_call" | custom-call | bytes 8388608 | tf_op jit(solution)/shard_map/early/pallas_call | solution.py:133
  20.0 0.0 collective-permute-done.3.refs_1_
  20.0 0.0 collective-permute-done.4.refs_2_
  20.0 1.6 %collective-permute-done.5.refs_3_ = bf16[16,3072]{1,0:T(8,128)(2,1)S(1)} collective-permute-done((bf16[16,3072]{1,0:T(8,128)(2,1)S(1)}, bf16[16,3072]{1,0:T(8,128)(2,1)S(1)}, u32[]{:S(2)}, u32[]{:S(2)}) %collective-permute-start.5) | collective-permute-done | bytes 98336 | tf_op jit(solution)/shard_map/ppermute | solution.py:26
  21.6 0.0 collective-permute-start.9
  21.6 0.5 %collective-permute-start.8 = (bf16[16,3072]{1,0:T(8,128)(2,1)S(1)}, bf16[16,3072]{1,0:T(8,128)(2,1)S(1)}, u32[]{:S(2)}, u32[]{:S(2)}) collective-permute-start(bf16[16,3072]{1,0:T(8,128)(2,1)S(1)} %collective-permute-done.4.refs_2_), channel_id=1, source_target_pairs={{0,1},{1,0},{2,3},{3,2},{4,5},{5,4},{6,7},{7,6},{8,9},{9,8},{10,11... | collective-permute-start | bytes 294920 | tf_op jit(solution)/shard_map/ppermute | solution.py:26
  22.1 0.0 collective-permute-start.7
  22.1 0.0 collective-permute-done.6.refs_4_
  22.1 0.8 %collective-permute-done.9.refs_7_ = bf16[16,3072]{1,0:T(8,128)(2,1)S(1)} collective-permute-done((bf16[16,3072]{1,0:T(8,128)(2,1)S(1)}, bf16[16,3072]{1,0:T(8,128)(2,1)S(1)}, u32[]{:S(2)}, u32[]{:S(2)}) %collective-permute-start.9) | collective-permute-done | bytes 98336 | tf_op jit(solution)/shard_map/ppermute | solution.py:26
  22.9 0.2 collective-permute-done.8.refs_6_
  23.1 0.4 collective-permute-done.7.refs_5_
  23.4 0.0 copy-done
  23.4 13.3 %ffn.1 = (bf16[64,2048]{1,0:T(8,128)(2,1)S(1)}, bf16[2048,2048]{1,0:T(8,128)(2,1)S(1)}, bf16[64,3072]{1,0:T(8,128)(2,1)S(1)}) custom-call(bf16[16,3072]{1,0:T(8,128)(2,1)S(1)} %arrange.1.after_ref.refs_0_, bf16[16,3072]{1,0:T(8,128)(2,1)S(1)} %collective-permute-done.3.refs_1_, bf16[16,3072]{1,0:T(8,128)(2,1)S(1)} %collective-permute-done.4.refs_2_, ...), custom_call_target="tpu_custom_call" | custom-call | flops 4026531840 | bytes 50331648 | tf_op jit(solution)/shard_map/ffn/pallas_call | solution.py:308
  36.8 0.2 collective-permute-start.10
  37.0 2.9 %kept_part.1.refs_0_ = f32[64,3072]{1,0:T(8,128)S(1)} custom-call(bf16[64,2048]{1,0:T(8,128)(2,1)S(1)} %get-tuple-element.32.hidden_ref, bf16[2048,2048]{1,0:T(8,128)(2,1)S(1)} %get-tuple-element.33.kept_ref, bf16[2048,6144]{1,0:T(8,128)(2,1)} %down_ref.1), custom_call_target="tpu_custom_call" | custom-call | flops 805306368 | bytes 12582912 | tf_op jit(solution)/shard_map/kept_part/pallas_call | solution.py:369
  39.9 0.0 collective-permute-done.10.refs_1_
  39.9 0.1 hid_sum.1
  40.0 0.6 %collective-permute-start.11 = (bf16[16,3072]{1,0:T(8,128)(2,1)S(1)}, bf16[16,3072]{1,0:T(8,128)(2,1)S(1)}, u32[]{:S(2)}, u32[]{:S(2)}) collective-permute-start(bf16[16,3072]{1,0:T(8,128)(2,1)S(1)} %get-tuple-element.36), channel_id=1, source_target_pairs={{0,8},{8,0},{16,24},{24,16},{1,9},{9,1},{17,25},{25,17},{2,10},{10... | collective-permute-start | bytes 294920 | tf_op jit(solution)/shard_map/ppermute | solution.py:26
  40.6 1.3 %collective-permute-start.12 = (bf16[16,3072]{1,0:T(8,128)(2,1)S(1)}, bf16[16,3072]{1,0:T(8,128)(2,1)S(1)}, u32[]{:S(2)}, u32[]{:S(2)}) collective-permute-start(bf16[16,3072]{1,0:T(8,128)(2,1)S(1)} %get-tuple-element.37), channel_id=1, source_target_pairs={{0,16},{8,24},{16,0},{24,8},{1,17},{9,25},{17,1},{25,9},{2,18},{10... | collective-permute-start | bytes 294920 | tf_op jit(solution)/shard_map/ppermute | solution.py:26
  41.9 1.7 %collective-permute-start.13 = (bf16[16,3072]{1,0:T(8,128)(2,1)S(1)}, bf16[16,3072]{1,0:T(8,128)(2,1)S(1)}, u32[]{:S(2)}, u32[]{:S(2)}) collective-permute-start(bf16[16,3072]{1,0:T(8,128)(2,1)S(1)} %get-tuple-element.38), channel_id=1, source_target_pairs={{0,24},{8,16},{16,8},{24,0},{1,25},{9,17},{17,9},{25,1},{2,26},{10... | collective-permute-start | bytes 294920 | tf_op jit(solution)/shard_map/ppermute | solution.py:26
  43.6 2.1 %collective-permute-done.11.refs_1_ = bf16[16,3072]{1,0:T(8,128)(2,1)S(1)} collective-permute-done((bf16[16,3072]{1,0:T(8,128)(2,1)S(1)}, bf16[16,3072]{1,0:T(8,128)(2,1)S(1)}, u32[]{:S(2)}, u32[]{:S(2)}) %collective-permute-start.11) | collective-permute-done | bytes 98336 | tf_op jit(solution)/shard_map/ppermute | solution.py:26
  45.7 1.8 %collective-permute-done.12.refs_2_ = bf16[16,3072]{1,0:T(8,128)(2,1)S(1)} collective-permute-done((bf16[16,3072]{1,0:T(8,128)(2,1)S(1)}, bf16[16,3072]{1,0:T(8,128)(2,1)S(1)}, u32[]{:S(2)}, u32[]{:S(2)}) %collective-permute-start.12) | collective-permute-done | bytes 98336 | tf_op jit(solution)/shard_map/ppermute | solution.py:26
  47.5 0.0 collective-permute-done.13.refs_3_
  47.5 0.7 %blk_sum.1 = bf16[16,3072]{1,0:T(8,128)(2,1)} custom-call(f32[16,3072]{1,0:T(8,128)S(1)} %get-tuple-element.35.refs_0_, bf16[16,3072]{1,0:T(8,128)(2,1)S(1)} %collective-permute-done.11.refs_1_, bf16[16,3072]{1,0:T(8,128)(2,1)S(1)} %collective-permute-done.12.refs_2_, bf16[16,3072]{1,0:T(8,128)(2,1)S(1)} %collective-permute-done.13.refs_3_), custom_call_target="tpu_custom_call" | custom-call | tf_op jit(solution)/shard_map/blk_sum/pallas_call | solution.py:418
Async XLA Ops:
  0.0 23.4 %copy-start = (bf16[6144,2048]{1,0:T(8,128)(2,1)S(1)}, bf16[6144,2048]{1,0:T(8,128)(2,1)}, u32[]{:S(2)}) copy-start(bf16[6144,2048]{1,0:T(8,128)(2,1)} %refs_8_.1) | copy-start | bytes 75497472
  1.6 5.7 %collective-permute-start = (bf16[4,3072]{1,0:T(4,128)(2,1)S(1)}, bf16[4,3072]{1,0:T(4,128)(2,1)S(1)}, u32[]{:S(2)}, u32[]{:S(2)}) collective-permute-start(bf16[4,3072]{1,0:T(4,128)(2,1)S(1)} %get-tuple-element.23), channel_id=1, source_target_pairs={{0,2},{2,0},{4,6},{6,4},{1,3},{3,1},{5,7},{7,5},{8,10},{10,8},{12,... | collective-permute-start | bytes 73736 | tf_op jit(solution)/shard_map/ppermute | solution.py:26
  4.6 5.1 %collective-permute-start.1 = (bf16[4,3072]{1,0:T(4,128)(2,1)S(1)}, bf16[4,3072]{1,0:T(4,128)(2,1)S(1)}, u32[]{:S(2)}, u32[]{:S(2)}) collective-permute-start(bf16[4,3072]{1,0:T(4,128)(2,1)S(1)} %get-tuple-element.24), channel_id=1, source_target_pairs={{0,4},{2,6},{4,0},{6,2},{1,5},{3,7},{5,1},{7,3},{8,12},{10,14},{12... | collective-permute-start | bytes 73736 | tf_op jit(solution)/shard_map/ppermute | solution.py:26
  7.2 5.6 %collective-permute-start.2 = (bf16[4,3072]{1,0:T(4,128)(2,1)S(1)}, bf16[4,3072]{1,0:T(4,128)(2,1)S(1)}, u32[]{:S(2)}, u32[]{:S(2)}) collective-permute-start(bf16[4,3072]{1,0:T(4,128)(2,1)S(1)} %get-tuple-element.25), channel_id=1, source_target_pairs={{0,6},{2,4},{4,2},{6,0},{1,7},{3,5},{5,3},{7,1},{8,14},{10,12},{12... | collective-permute-start | bytes 73736 | tf_op jit(solution)/shard_map/ppermute | solution.py:26
  13.0 7.0 %collective-permute-start.3 = (bf16[16,3072]{1,0:T(8,128)(2,1)S(1)}, bf16[16,3072]{1,0:T(8,128)(2,1)S(1)}, u32[]{:S(2)}, u32[]{:S(2)}) collective-permute-start(bf16[16,3072]{1,0:T(8,128)(2,1)S(1)} %arrange.1.after_ref.refs_0_), channel_id=1, source_target_pairs={{0,8},{8,0},{16,24},{24,16},{1,9},{9,1},{17,25},{25,17},{2,10},{10... | collective-permute-start | bytes 294920 | tf_op jit(solution)/shard_map/ppermute | solution.py:26
  14.6 5.4 %collective-permute-start.4 = (bf16[16,3072]{1,0:T(8,128)(2,1)S(1)}, bf16[16,3072]{1,0:T(8,128)(2,1)S(1)}, u32[]{:S(2)}, u32[]{:S(2)}) collective-permute-start(bf16[16,3072]{1,0:T(8,128)(2,1)S(1)} %arrange.1.after_ref.refs_0_), channel_id=1, source_target_pairs={{0,16},{8,24},{16,0},{24,8},{1,17},{9,25},{17,1},{25,9},{2,18},{10... | collective-permute-start | bytes 294920 | tf_op jit(solution)/shard_map/ppermute | solution.py:26
  16.1 5.5 %collective-permute-start.5 = (bf16[16,3072]{1,0:T(8,128)(2,1)S(1)}, bf16[16,3072]{1,0:T(8,128)(2,1)S(1)}, u32[]{:S(2)}, u32[]{:S(2)}) collective-permute-start(bf16[16,3072]{1,0:T(8,128)(2,1)S(1)} %arrange.1.after_ref.refs_0_), channel_id=1, source_target_pairs={{0,24},{8,16},{16,8},{24,0},{1,25},{9,17},{17,9},{25,1},{2,26},{10... | collective-permute-start | bytes 294920 | tf_op jit(solution)/shard_map/ppermute | solution.py:26
  16.6 5.6 %collective-permute-start.6 = (bf16[16,3072]{1,0:T(8,128)(2,1)S(1)}, bf16[16,3072]{1,0:T(8,128)(2,1)S(1)}, u32[]{:S(2)}, u32[]{:S(2)}) collective-permute-start(bf16[16,3072]{1,0:T(8,128)(2,1)S(1)} %arrange.1.after_ref.refs_0_), channel_id=1, source_target_pairs={{0,1},{1,0},{2,3},{3,2},{4,5},{5,4},{6,7},{7,6},{8,9},{9,8},{10,11... | collective-permute-start | bytes 294920 | tf_op jit(solution)/shard_map/ppermute | solution.py:26
  21.6 1.3 %collective-permute-start.9 = (bf16[16,3072]{1,0:T(8,128)(2,1)S(1)}, bf16[16,3072]{1,0:T(8,128)(2,1)S(1)}, u32[]{:S(2)}, u32[]{:S(2)}) collective-permute-start(bf16[16,3072]{1,0:T(8,128)(2,1)S(1)} %collective-permute-done.5.refs_3_), channel_id=1, source_target_pairs={{0,1},{1,0},{2,3},{3,2},{4,5},{5,4},{6,7},{7,6},{8,9},{9,8},{10,11... | collective-permute-start | bytes 294920 | tf_op jit(solution)/shard_map/ppermute | solution.py:26
  21.6 1.5 %collective-permute-start.8 = (bf16[16,3072]{1,0:T(8,128)(2,1)S(1)}, bf16[16,3072]{1,0:T(8,128)(2,1)S(1)}, u32[]{:S(2)}, u32[]{:S(2)}) collective-permute-start(bf16[16,3072]{1,0:T(8,128)(2,1)S(1)} %collective-permute-done.4.refs_2_), channel_id=1, source_target_pairs={{0,1},{1,0},{2,3},{3,2},{4,5},{5,4},{6,7},{7,6},{8,9},{9,8},{10,11... | collective-permute-start | bytes 294920 | tf_op jit(solution)/shard_map/ppermute | solution.py:26
  22.1 1.3 %collective-permute-start.7 = (bf16[16,3072]{1,0:T(8,128)(2,1)S(1)}, bf16[16,3072]{1,0:T(8,128)(2,1)S(1)}, u32[]{:S(2)}, u32[]{:S(2)}) collective-permute-start(bf16[16,3072]{1,0:T(8,128)(2,1)S(1)} %collective-permute-done.3.refs_1_), channel_id=1, source_target_pairs={{0,1},{1,0},{2,3},{3,2},{4,5},{5,4},{6,7},{7,6},{8,9},{9,8},{10,11... | collective-permute-start | bytes 294920 | tf_op jit(solution)/shard_map/ppermute | solution.py:26
  36.8 3.1 %collective-permute-start.10 = (bf16[64,3072]{1,0:T(8,128)(2,1)S(1)}, bf16[64,3072]{1,0:T(8,128)(2,1)S(1)}, u32[]{:S(2)}, u32[]{:S(2)}) collective-permute-start(bf16[64,3072]{1,0:T(8,128)(2,1)S(1)} %get-tuple-element.34), channel_id=1, source_target_pairs={{0,1},{1,0},{2,3},{3,2},{4,5},{5,4},{6,7},{7,6},{8,9},{9,8},{10,11... | collective-permute-start | bytes 1179656 | tf_op jit(solution)/shard_map/ppermute | solution.py:26
  40.0 5.7 %collective-permute-start.11 = (bf16[16,3072]{1,0:T(8,128)(2,1)S(1)}, bf16[16,3072]{1,0:T(8,128)(2,1)S(1)}, u32[]{:S(2)}, u32[]{:S(2)}) collective-permute-start(bf16[16,3072]{1,0:T(8,128)(2,1)S(1)} %get-tuple-element.36), channel_id=1, source_target_pairs={{0,8},{8,0},{16,24},{24,16},{1,9},{9,1},{17,25},{25,17},{2,10},{10... | collective-permute-start | bytes 294920 | tf_op jit(solution)/shard_map/ppermute | solution.py:26
  40.6 6.9 %collective-permute-start.12 = (bf16[16,3072]{1,0:T(8,128)(2,1)S(1)}, bf16[16,3072]{1,0:T(8,128)(2,1)S(1)}, u32[]{:S(2)}, u32[]{:S(2)}) collective-permute-start(bf16[16,3072]{1,0:T(8,128)(2,1)S(1)} %get-tuple-element.37), channel_id=1, source_target_pairs={{0,16},{8,24},{16,0},{24,8},{1,17},{9,25},{17,1},{25,9},{2,18},{10... | collective-permute-start | bytes 294920 | tf_op jit(solution)/shard_map/ppermute | solution.py:26
  41.9 5.6 %collective-permute-start.13 = (bf16[16,3072]{1,0:T(8,128)(2,1)S(1)}, bf16[16,3072]{1,0:T(8,128)(2,1)S(1)}, u32[]{:S(2)}, u32[]{:S(2)}) collective-permute-start(bf16[16,3072]{1,0:T(8,128)(2,1)S(1)} %get-tuple-element.38), channel_id=1, source_target_pairs={{0,24},{8,16},{16,8},{24,0},{1,25},{9,17},{17,9},{25,1},{2,26},{10... | collective-permute-start | bytes 294920 | tf_op jit(solution)/shard_map/ppermute | solution.py:26

commit v4 on v3

--- a/solution.py
+++ b/solution.py
@@ -26,9 +26,10 @@
     return lax.ppermute(array, axis, [(i, i ^ step) for i in range(count)])
 
 
-def norm_kernel(lanes, *refs):
-    sources, piece_refs = refs[:4], refs[4 : 4 + lanes]
-    targets, placed, sems = refs[4 + lanes : 8 + lanes], refs[8 + lanes], refs[9 + lanes]
+def norm_kernel(lanes, hids, *refs):
+    count = lanes // hids
+    sources, piece_refs = refs[:4], refs[4 : 4 + count]
+    targets, placed, sems = refs[4 + count : 8 + count], refs[8 + count], refs[9 + count]
     copies = [
         pltpu.make_async_copy(src, dst, sems.at[i])
         for i, (src, dst) in enumerate(zip(sources, targets))
@@ -42,42 +43,39 @@
     rounds = rows // lanes
     x = tokens_ref[...].astype(jnp.float32)
     row_scale = lax.rsqrt(jnp.mean(x * x, axis=1, keepdims=True) + epsilon)
-    width = placed.shape[1]
-    columns = pl.ds(pl.multiple_of(lax.axis_index("hid") * width, width), width)
-    x = tokens_ref[:, columns].astype(jnp.float32)
     at = lax.broadcasted_iota(jnp.int32, (rows, 1), 0)
     kind = jnp.zeros((rows, 1), jnp.int32)
     for i in range(rows):
         kind = jnp.where(at == i, kinds_ref[i], kind)
-    gain = jnp.broadcast_to(gains_ref[0:1, columns], x.shape)
+    gain = jnp.broadcast_to(gains_ref[0:1, :], x.shape)
     for c in range(1, gains_ref.shape[0]):
-        gain = jnp.where(kind == c, gains_ref[c : c + 1, columns], gain)
+        gain = jnp.where(kind == c, gains_ref[c : c + 1, :], gain)
     normed = (x * row_scale * gain).astype(jnp.bfloat16)
-    me = lax.axis_index("regroup")
-    target = lax.broadcasted_iota(jnp.int32, (rows, rows), 0)
-    lane = jnp.bitwise_xor(lax.shift_right_logical(target, log2(rounds)), me)
+    target = lax.broadcasted_iota(jnp.int32, (count * rounds, rows), 0)
+    step = lax.axis_index("hid") * count + lax.shift_right_logical(target, log2(rounds))
+    lane = jnp.bitwise_xor(step, lax.axis_index("regroup"))
     slot = jnp.bitwise_and(target, rounds - 1) * lanes + lane
     placing = (jnp.broadcast_to(slots_ref[0:1, :], slot.shape) == slot).astype(jnp.bfloat16)
     placed[...] = jnp.dot(placing, normed, preferred_element_type=jnp.float32)
-    for step, ref in enumerate(piece_refs):
-        ref[...] = placed[step * rounds : (step + 1) * rounds, :].astype(jnp.bfloat16)
+    for t, ref in enumerate(piece_refs):
+        ref[...] = placed[t * rounds : (t + 1) * rounds, :].astype(jnp.bfloat16)
 
 
 def norm(tokens, kinds, slots, gains):
     rows, features = tokens.shape
-    lanes = lax.axis_size("regroup")
-    width = features // lax.axis_size("hid")
-    return pl.pallas_call(
-        functools.partial(norm_kernel, lanes),
-        out_shape=(jax.ShapeDtypeStruct((rows // lanes, width), jnp.bfloat16),) * lanes,
+    lanes, hids = lax.axis_size("regroup"), lax.axis_size("hid")
+    count, rounds = lanes // hids, rows // lanes
+    return pl.pallas_call(
+        functools.partial(norm_kernel, lanes, hids),
+        out_shape=(jax.ShapeDtypeStruct((rounds, features), jnp.bfloat16),) * count,
         in_specs=[ANYWHERE] * 4,
-        out_specs=(IN_VMEM,) * lanes,
+        out_specs=(IN_VMEM,) * count,
         scratch_shapes=[
             pltpu.VMEM(tokens.shape, tokens.dtype),
             pltpu.SMEM(kinds.shape, kinds.dtype),
             pltpu.VMEM(slots.shape, slots.dtype),
             pltpu.VMEM(gains.shape, gains.dtype),
-            pltpu.VMEM((rows, width), jnp.float32),
+            pltpu.VMEM((count * rounds, features), jnp.float32),
             pltpu.SemaphoreType.DMA((4,)),
         ],
         compiler_params=pltpu.CompilerParams(vmem_limit_bytes=4 * MIB),
@@ -86,32 +84,38 @@
     )(tokens, kinds, slots, gains)
 
 
-def arrange_kernel(lanes, *refs):
-    out_ref, stack = refs[lanes:]
-    rows = out_ref.shape[0]
-    rounds = rows // lanes
-    for step in range(lanes):
-        stack[step * rounds : (step + 1) * rounds, :] = refs[step][...].astype(jnp.float32)
-    r = lax.broadcasted_iota(jnp.int32, (rows, rows), 0)
-    c = lax.broadcasted_iota(jnp.int32, (rows, rows), 1)
-    step = jnp.bitwise_xor(jnp.bitwise_and(r, lanes - 1), lax.axis_index("regroup"))
-    order = (c == step * rounds + lax.shift_right_logical(r, log2(lanes))).astype(jnp.bfloat16)
-    out_ref[...] = jnp.dot(
-        order, stack[...].astype(jnp.bfloat16), preferred_element_type=jnp.float32
-    ).astype(jnp.bfloat16)
-
-
-def arrange(pieces):
-    lanes = len(pieces)
+def to_lanes(pieces):
+    lanes, hids = lax.axis_size("regroup"), lax.axis_size("hid")
+    count = len(pieces)
+    assert count * hids == lanes
+
+    def pairs(t):
+        for lane in range(lanes):
+            for core in range(hids):
+                yield lane * hids + core, (lane ^ (core * count + t)) * hids + core
+
+    return [lax.ppermute(piece, ("regroup", "hid"), list(pairs(t))) for t, piece in enumerate(pieces)]
+
+
+def stack_kernel(*refs):
+    *piece_refs, out_ref, stack = refs
+    rounds = piece_refs[0].shape[0]
+    for t, ref in enumerate(piece_refs):
+        stack[t * rounds : (t + 1) * rounds, :] = ref[...].astype(jnp.float32)
+    out_ref[...] = stack[...].astype(jnp.bfloat16)
+
+
+def stacked(pieces):
     rounds, width = pieces[0].shape
-    return pl.pallas_call(
-        functools.partial(arrange_kernel, lanes),
-        out_shape=jax.ShapeDtypeStruct((lanes * rounds, width), jnp.bfloat16),
-        in_specs=[IN_VMEM] * lanes,
+    rows = len(pieces) * rounds
+    return pl.pallas_call(
+        stack_kernel,
+        out_shape=jax.ShapeDtypeStruct((rows, width), jnp.bfloat16),
+        in_specs=[IN_VMEM] * len(pieces),
         out_specs=IN_VMEM,
-        scratch_shapes=[pltpu.VMEM((lanes * rounds, width), jnp.float32)],
+        scratch_shapes=[pltpu.VMEM((rows, width), jnp.float32)],
         compiler_params=pltpu.CompilerParams(vmem_limit_bytes=4 * MIB),
-        name="arrange",
+        name="stacked",
     )(*pieces)
 
 
@@ -218,12 +222,20 @@
     for n in range(slots):
         start_next(n)
     kept_copy(0).start()
-    for side in range(hids):
-        start = pl.multiple_of(side_start(side), width)
-        for step in range(blocks):
-            panel[step * each : (step + 1) * each, pl.ds(start, width)] = panel_refs[
-                side * blocks + step
-            ][...]
+    cores = lax.broadcasted_iota(jnp.int32, (each // hids, 1), 0) * 0 + me
+    for step in range(blocks):
+        sides = [
+            panel_refs[side * blocks + step][...].astype(jnp.float32) for side in range(hids)
+        ]
+        lined = []
+        for core in range(hids):
+            rows_of = sides[core]
+            for mine in range(1, hids):
+                rows_of = jnp.where(cores == mine, sides[core ^ mine], rows_of)
+            lined.append(rows_of)
+        panel[step * each : (step + 1) * each, :] = jnp.concatenate(lined, axis=0).astype(
+            jnp.bfloat16
+        )
     chunk = even(shard, 1024)
     own = pl.ds(pl.multiple_of(me * width, width), skip * part)
 
@@ -277,15 +289,17 @@
         def _(c):
             total = None
             for k in range(deep):
+                down_copy(((side - 1) * wide + c) * deep + k).wait()
+            for k in range(deep):
                 n = ((side - 1) * wide + c) * deep + k
-                down_copy(n).wait()
                 value = jnp.dot(
                     hidden_ref[:, k * down_rows : (k + 1) * down_rows],
                     ring[(n + up_count) % slots, 0:down_rows, 0:down_cols],
                     preferred_element_type=jnp.float32,
                 )
                 total = value if total is None else total + value
-                start_next(n + up_count + slots)
+            for k in range(deep):
+                start_next(((side - 1) * wide + c) * deep + k + up_count + slots)
             columns = pl.ds(pl.multiple_of(c * down_cols, 128), down_cols)
             out_refs[side - 1][:, columns] = total.astype(jnp.bfloat16)
 
@@ -295,8 +309,8 @@
 
 def ffn(panels, gate_weight, up_held, up_weight, down_weight, blocks):
     hids = lax.axis_size("hid")
-    each, width = panels[0].shape
-    rows, depth = blocks * each, width * hids
+    each, depth = panels[0].shape
+    rows, width = blocks * hids * each, depth // hids
     shard = gate_weight.shape[1]
     part, up_cols = even(width, 1024), even(shard, 1024)
     down_rows, down_cols = even(shard, 1024), even(width, 1024)
@@ -407,16 +421,25 @@
     )(*parts)
 
 
-def blk_sum_kernel(*refs):
-    total = refs[0][...]
-    for ref in refs[1:-1]:
+def blk_sum_kernel(lanes, *refs):
+    *part_refs, out_ref = refs
+    total = part_refs[0][...]
+    for ref in part_refs[1:]:
         total += ref[...].astype(jnp.float32)
-    refs[-1][...] = total.astype(refs[-1].dtype)
+    rows = out_ref.shape[0]
+    rounds = rows // lanes
+    r = lax.broadcasted_iota(jnp.int32, (rows, rows), 0)
+    c = lax.broadcasted_iota(jnp.int32, (rows, rows), 1)
+    step = jnp.bitwise_xor(jnp.bitwise_and(r, lanes - 1), lax.axis_index("regroup"))
+    order = (c == step * rounds + lax.shift_right_logical(r, log2(lanes))).astype(jnp.bfloat16)
+    out_ref[...] = jnp.dot(
+        order, total.astype(jnp.bfloat16), preferred_element_type=jnp.float32
+    ).astype(jnp.bfloat16)
 
 
 def blk_sum(parts):
     return pl.pallas_call(
-        blk_sum_kernel,
+        functools.partial(blk_sum_kernel, lax.axis_size("regroup")),
         out_shape=jax.ShapeDtypeStruct(parts[0].shape, jnp.bfloat16),
         in_specs=[IN_VMEM] * len(parts),
         out_specs=IN_VMEM,
@@ -436,10 +459,7 @@
         for array in (tokens, kinds, slots, gains, up_weight, down_weight)
     )
     gate_weight = held(gate_weight)
-    pieces = norm(tokens, kinds, slots, gains)
-    half = arrange(
-        [pieces[0]] + [exchange(pieces[step], "regroup", step) for step in range(1, lanes)]
-    )
+    half = stacked(to_lanes(norm(tokens, kinds, slots, gains)))
     halves = [half] + [exchange(half, "blk", step) for step in range(1, blocks)]
     up_held = early(half, up_weight)
     for step in range(1, blocks):

time: 48.3 us -> 46.3 us (0.959)
  waiting for transfers between devices: 12.5 us -> 7.55 us
  starting transfers between devices: 13.5 us -> 16.6 us
    ppermute x14 -> x11, waiting for transfers between devices: 12.5 us -> 5.48 us  [exchange(): return lax.ppermute(array, axis, [(i, i ^ step) for i in range(count)])]
    ppermute x0 -> x2, starting transfers between devices: none -> 3.88 us  [to_lanes(): lax.ppermute(piece, ('regroup', 'hid'), list(pairs(t)))]
    ppermute x0 -> x2, waiting for transfers between devices: none -> 2.07 us  [to_lanes(): lax.ppermute(piece, ('regroup', 'hid'), list(pairs(t)))]
    ppermute x14 -> x11, starting transfers between devices: 13.5 us -> 12.7 us  [exchange(): return lax.ppermute(array, axis, [(i, i ^ step) for i in range(count)])]
  transfers between devices with their start and end apart: 14 -> 13, of which waited for: 8 -> 7; matrix products, arithmetic and copies ran while one was open for 0% -> 0% of each run, Pallas kernels for 13% -> 14%
where the time goes in v4:
time: 46.3 us; the launch traced here: 46.2 us
  Pallas kernels  21.9 us (47%)
  starting transfers between devices  16.6 us (36%)
  waiting for transfers between devices  7.55 us (16%)
    pallas_call x1, Pallas kernels, ffn(): pl.pallas_call(functools.partial(ffn_kernel, blocks, hids, (slots, part,...  13.1 us
    ppermute x11, starting transfers between devices, exchange(): return lax.ppermute(array, axis, [(i, i ^ step) for i in range(count)])  12.7 us
    ppermute x11, waiting for transfers between devices, exchange(): return lax.ppermute(array, axis, [(i, i ^ step) for i in range(count)])  5.48 us
    ppermute x2, starting transfers between devices, to_lanes(): lax.ppermute(piece, ('regroup', 'hid'), list(pairs(t)))  3.88 us
    pallas_call x1, Pallas kernels, early(): pl.pallas_call(functools.partial(early_kernel, width), out_shape=pltpu.VM...  3.39 us
    pallas_call x1, Pallas kernels, kept_part(): pl.pallas_call(kept_kernel, out_shape=jax.ShapeDtypeStruct((rows, width),...  2.92 us
    ppermute x2, waiting for transfers between devices, to_lanes(): lax.ppermute(piece, ('regroup', 'hid'), list(pairs(t)))  2.07 us
    pallas_call x1, Pallas kernels, norm(): pl.pallas_call(functools.partial(norm_kernel, lanes, hids), out_shape=(ja...  1.63 us
  transfers between devices with their start and end apart: 13, of which 7 were waited for; matrix products, arithmetic and copies ran while one was open for 0% of the time, Pallas kernels for 14%

profile of v4, /device:TPU:0, one launch (start us, length us, event | category | flops | bytes accessed | tf_op | source)
XLA Modules:
  0.0 46.2 jit_solution(16013427371718884535)
XLA Ops:
  0.0 0.0 copy-start
  0.0 1.6 %norm.1 = (bf16[4,6144]{1,0:T(4,128)(2,1)S(1)}, bf16[4,6144]{1,0:T(4,128)(2,1)S(1)}) custom-call(bf16[16,6144]{1,0:T(8,128)(2,1)} %refs_0_.1, s32[16]{0:T(128)} %refs_1_.1, s32[1,16]{1,0:T(1,128)} %refs_2_.1, f32[8,6144]{1,0:T(8,128)} %refs_3_.1), custom_call_target="tpu_custom_call" | custom-call | bytes 50331648 | tf_op jit(solution)/shard_map/norm/pallas_call | solution.py:68
  1.6 0.8 %collective-permute-start = (bf16[4,6144]{1,0:T(4,128)(2,1)S(1)}, bf16[4,6144]{1,0:T(4,128)(2,1)S(1)}, u32[]{:S(2)}, u32[]{:S(2)}) collective-permute-start(bf16[4,6144]{1,0:T(4,128)(2,1)S(1)} %get-tuple-element.20), channel_id=1, source_target_pairs={{0,0},{1,5},{2,2},{3,7},{4,4},{5,1},{6,6},{7,3},{8,8},{9,13},{10,1... | collective-permute-start | bytes 147464 | tf_op jit(solution)/shard_map/ppermute | solution.py:97
  2.4 3.1 %collective-permute-start.1 = (bf16[4,6144]{1,0:T(4,128)(2,1)S(1)}, bf16[4,6144]{1,0:T(4,128)(2,1)S(1)}, u32[]{:S(2)}, u32[]{:S(2)}) collective-permute-start(bf16[4,6144]{1,0:T(4,128)(2,1)S(1)} %get-tuple-element.21), channel_id=1, source_target_pairs={{0,2},{1,7},{2,0},{3,5},{4,6},{5,3},{6,4},{7,1},{8,10},{9,15},{10,... | collective-permute-start | bytes 147464 | tf_op jit(solution)/shard_map/ppermute | solution.py:97
  5.5 0.0 collective-permute-done.refs_0_
  5.5 2.1 %collective-permute-done.1.refs_1_ = bf16[4,6144]{1,0:T(4,128)(2,1)S(1)} collective-permute-done((bf16[4,6144]{1,0:T(4,128)(2,1)S(1)}, bf16[4,6144]{1,0:T(4,128)(2,1)S(1)}, u32[]{:S(2)}, u32[]{:S(2)}) %collective-permute-start.1) | collective-permute-done | bytes 49184 | tf_op jit(solution)/shard_map/ppermute | solution.py:97
  7.6 2.0 %collective-permute-start.2 = (bf16[8,6144]{1,0:T(8,128)(2,1)S(1)}, bf16[8,6144]{1,0:T(8,128)(2,1)S(1)}, u32[]{:S(2)}, u32[]{:S(2)}) collective-permute-start(bf16[8,6144]{1,0:T(8,128)(2,1)S(1)} %stacked.1.after_ref.refs_0_), channel_id=1, source_target_pairs={{0,8},{8,0},{16,24},{24,16},{1,9},{9,1},{17,25},{25,17},{2,10},{10... | collective-permute-start | bytes 294920 | tf_op jit(solution)/shard_map/ppermute | solution.py:26
  9.6 1.5 %collective-permute-start.3 = (bf16[8,6144]{1,0:T(8,128)(2,1)S(1)}, bf16[8,6144]{1,0:T(8,128)(2,1)S(1)}, u32[]{:S(2)}, u32[]{:S(2)}) collective-permute-start(bf16[8,6144]{1,0:T(8,128)(2,1)S(1)} %stacked.1.after_ref.refs_0_), channel_id=1, source_target_pairs={{0,16},{8,24},{16,0},{24,8},{1,17},{9,25},{17,1},{25,9},{2,18},{10... | collective-permute-start | bytes 294920 | tf_op jit(solution)/shard_map/ppermute | solution.py:26
  11.2 0.0 collective-permute-start.4
  11.2 3.9 %collective-permute-start.5 = (bf16[8,6144]{1,0:T(8,128)(2,1)S(1)}, bf16[8,6144]{1,0:T(8,128)(2,1)S(1)}, u32[]{:S(2)}, u32[]{:S(2)}) collective-permute-start(bf16[8,6144]{1,0:T(8,128)(2,1)S(1)} %stacked.1.after_ref.refs_0_), channel_id=1, source_target_pairs={{0,1},{1,0},{2,3},{3,2},{4,5},{5,4},{6,7},{7,6},{8,9},{9,8},{10,11... | collective-permute-start | bytes 294920 | tf_op jit(solution)/shard_map/ppermute | solution.py:26
  15.1 3.4 %early.1.refs_9_ = bf16[2048,2048]{1,0:T(8,128)(2,1)S(1)} custom-call(bf16[8,6144]{1,0:T(8,128)(2,1)S(1)} %stacked.1.after_ref.refs_0_, bf16[6144,2048]{1,0:T(8,128)(2,1)} %refs_10_.1), custom_call_target="tpu_custom_call" | custom-call | bytes 8388608 | tf_op jit(solution)/shard_map/early/pallas_call | solution.py:137
  18.5 0.0 collective-permute-done.2.refs_1_
  18.5 0.0 collective-permute-done.3.refs_2_
  18.5 0.0 collective-permute-done.4.refs_3_
  18.5 0.7 %collective-permute-start.8 = (bf16[8,6144]{1,0:T(8,128)(2,1)S(1)}, bf16[8,6144]{1,0:T(8,128)(2,1)S(1)}, u32[]{:S(2)}, u32[]{:S(2)}) collective-permute-start(bf16[8,6144]{1,0:T(8,128)(2,1)S(1)} %collective-permute-done.4.refs_3_), channel_id=1, source_target_pairs={{0,1},{1,0},{2,3},{3,2},{4,5},{5,4},{6,7},{7,6},{8,9},{9,8},{10,11... | collective-permute-start | bytes 294920 | tf_op jit(solution)/shard_map/ppermute | solution.py:26
  19.3 0.0 collective-permute-start.7
  19.3 0.5 %collective-permute-start.6 = (bf16[8,6144]{1,0:T(8,128)(2,1)S(1)}, bf16[8,6144]{1,0:T(8,128)(2,1)S(1)}, u32[]{:S(2)}, u32[]{:S(2)}) collective-permute-start(bf16[8,6144]{1,0:T(8,128)(2,1)S(1)} %collective-permute-done.2.refs_1_), channel_id=1, source_target_pairs={{0,1},{1,0},{2,3},{3,2},{4,5},{5,4},{6,7},{7,6},{8,9},{9,8},{10,11... | collective-permute-start | bytes 294920 | tf_op jit(solution)/shard_map/ppermute | solution.py:26
  19.8 0.0 collective-permute-done.5.refs_4_
  19.8 0.4 collective-permute-done.8.refs_7_
  20.2 0.4 collective-permute-done.7.refs_6_
  20.6 0.2 collective-permute-done.6.refs_5_
  20.7 0.0 copy-done
  20.7 13.1 %ffn.1 = (bf16[64,2048]{1,0:T(8,128)(2,1)S(1)}, bf16[2048,2048]{1,0:T(8,128)(2,1)S(1)}, bf16[64,3072]{1,0:T(8,128)(2,1)S(1)}) custom-call(bf16[8,6144]{1,0:T(8,128)(2,1)S(1)} %stacked.1.after_ref.refs_0_, bf16[8,6144]{1,0:T(8,128)(2,1)S(1)} %collective-permute-done.2.refs_1_, bf16[8,6144]{1,0:T(8,128)(2,1)S(1)} %collective-permute-done.3.refs_2_, ...), custom_call_target="tpu_custom_call" | custom-call | flops 4026531840 | bytes 50331648 | tf_op jit(solution)/shard_map/ffn/pallas_call | solution.py:322
  33.8 0.4 collective-permute-start.9
  34.2 2.9 %kept_part.1.refs_0_ = f32[64,3072]{1,0:T(8,128)S(1)} custom-call(bf16[64,2048]{1,0:T(8,128)(2,1)S(1)} %get-tuple-element.28.hidden_ref, bf16[2048,2048]{1,0:T(8,128)(2,1)S(1)} %get-tuple-element.29.kept_ref, bf16[2048,6144]{1,0:T(8,128)(2,1)} %down_ref.1), custom_call_target="tpu_custom_call" | custom-call | flops 805306368 | bytes 12582912 | tf_op jit(solution)/shard_map/kept_part/pallas_call | solution.py:383
  37.2 0.0 collective-permute-done.9.refs_1_
  37.2 0.1 hid_sum.1
  37.3 1.0 %collective-permute-start.10 = (bf16[16,3072]{1,0:T(8,128)(2,1)S(1)}, bf16[16,3072]{1,0:T(8,128)(2,1)S(1)}, u32[]{:S(2)}, u32[]{:S(2)}) collective-permute-start(bf16[16,3072]{1,0:T(8,128)(2,1)S(1)} %get-tuple-element.32), channel_id=1, source_target_pairs={{0,8},{8,0},{16,24},{24,16},{1,9},{9,1},{17,25},{25,17},{2,10},{10... | collective-permute-start | bytes 294920 | tf_op jit(solution)/shard_map/ppermute | solution.py:26
  38.3 1.5 %collective-permute-start.11 = (bf16[16,3072]{1,0:T(8,128)(2,1)S(1)}, bf16[16,3072]{1,0:T(8,128)(2,1)S(1)}, u32[]{:S(2)}, u32[]{:S(2)}) collective-permute-start(bf16[16,3072]{1,0:T(8,128)(2,1)S(1)} %get-tuple-element.33), channel_id=1, source_target_pairs={{0,16},{8,24},{16,0},{24,8},{1,17},{9,25},{17,1},{25,9},{2,18},{10... | collective-permute-start | bytes 294920 | tf_op jit(solution)/shard_map/ppermute | solution.py:26
  39.8 1.0 %collective-permute-start.12 = (bf16[16,3072]{1,0:T(8,128)(2,1)S(1)}, bf16[16,3072]{1,0:T(8,128)(2,1)S(1)}, u32[]{:S(2)}, u32[]{:S(2)}) collective-permute-start(bf16[16,3072]{1,0:T(8,128)(2,1)S(1)} %get-tuple-element.34), channel_id=1, source_target_pairs={{0,24},{8,16},{16,8},{24,0},{1,25},{9,17},{17,9},{25,1},{2,26},{10... | collective-permute-start | bytes 294920 | tf_op jit(solution)/shard_map/ppermute | solution.py:26
  40.8 1.4 %collective-permute-done.10.refs_1_ = bf16[16,3072]{1,0:T(8,128)(2,1)S(1)} collective-permute-done((bf16[16,3072]{1,0:T(8,128)(2,1)S(1)}, bf16[16,3072]{1,0:T(8,128)(2,1)S(1)}, u32[]{:S(2)}, u32[]{:S(2)}) %collective-permute-start.10) | collective-permute-done | bytes 98336 | tf_op jit(solution)/shard_map/ppermute | solution.py:26
  42.2 2.0 %collective-permute-done.11.refs_2_ = bf16[16,3072]{1,0:T(8,128)(2,1)S(1)} collective-permute-done((bf16[16,3072]{1,0:T(8,128)(2,1)S(1)}, bf16[16,3072]{1,0:T(8,128)(2,1)S(1)}, u32[]{:S(2)}, u32[]{:S(2)}) %collective-permute-start.11) | collective-permute-done | bytes 98336 | tf_op jit(solution)/shard_map/ppermute | solution.py:26
  44.2 1.1 %collective-permute-done.12.refs_3_ = bf16[16,3072]{1,0:T(8,128)(2,1)S(1)} collective-permute-done((bf16[16,3072]{1,0:T(8,128)(2,1)S(1)}, bf16[16,3072]{1,0:T(8,128)(2,1)S(1)}, u32[]{:S(2)}, u32[]{:S(2)}) %collective-permute-start.12) | collective-permute-done | bytes 98336 | tf_op jit(solution)/shard_map/ppermute | solution.py:26
  45.3 0.8 %blk_sum.1 = bf16[16,3072]{1,0:T(8,128)(2,1)} custom-call(f32[16,3072]{1,0:T(8,128)S(1)} %get-tuple-element.31.refs_0_, bf16[16,3072]{1,0:T(8,128)(2,1)S(1)} %collective-permute-done.10.refs_1_, bf16[16,3072]{1,0:T(8,128)(2,1)S(1)} %collective-permute-done.11.refs_2_, bf16[16,3072]{1,0:T(8,128)(2,1)S(1)} %collective-permute-done.12.refs_3_), custom_call_target="tpu_custom_call" | custom-call | tf_op jit(solution)/shard_map/blk_sum/pallas_call | solution.py:441
  (1 shorter events, 0.0 us)
Async XLA Ops:
  0.0 20.7 %copy-start = (bf16[6144,2048]{1,0:T(8,128)(2,1)S(1)}, bf16[6144,2048]{1,0:T(8,128)(2,1)}, u32[]{:S(2)}) copy-start(bf16[6144,2048]{1,0:T(8,128)(2,1)} %refs_8_.1) | copy-start | bytes 75497472
  1.6 3.9 %collective-permute-start = (bf16[4,6144]{1,0:T(4,128)(2,1)S(1)}, bf16[4,6144]{1,0:T(4,128)(2,1)S(1)}, u32[]{:S(2)}, u32[]{:S(2)}) collective-permute-start(bf16[4,6144]{1,0:T(4,128)(2,1)S(1)} %get-tuple-element.20), channel_id=1, source_target_pairs={{0,0},{1,5},{2,2},{3,7},{4,4},{5,1},{6,6},{7,3},{8,8},{9,13},{10,1... | collective-permute-start | bytes 147464 | tf_op jit(solution)/shard_map/ppermute | solution.py:97
  2.4 5.2 %collective-permute-start.1 = (bf16[4,6144]{1,0:T(4,128)(2,1)S(1)}, bf16[4,6144]{1,0:T(4,128)(2,1)S(1)}, u32[]{:S(2)}, u32[]{:S(2)}) collective-permute-start(bf16[4,6144]{1,0:T(4,128)(2,1)S(1)} %get-tuple-element.21), channel_id=1, source_target_pairs={{0,2},{1,7},{2,0},{3,5},{4,6},{5,3},{6,4},{7,1},{8,10},{9,15},{10,... | collective-permute-start | bytes 147464 | tf_op jit(solution)/shard_map/ppermute | solution.py:97
  7.6 10.9 %collective-permute-start.2 = (bf16[8,6144]{1,0:T(8,128)(2,1)S(1)}, bf16[8,6144]{1,0:T(8,128)(2,1)S(1)}, u32[]{:S(2)}, u32[]{:S(2)}) collective-permute-start(bf16[8,6144]{1,0:T(8,128)(2,1)S(1)} %stacked.1.after_ref.refs_0_), channel_id=1, source_target_pairs={{0,8},{8,0},{16,24},{24,16},{1,9},{9,1},{17,25},{25,17},{2,10},{10... | collective-permute-start | bytes 294920 | tf_op jit(solution)/shard_map/ppermute | solution.py:26
  9.6 8.9 %collective-permute-start.3 = (bf16[8,6144]{1,0:T(8,128)(2,1)S(1)}, bf16[8,6144]{1,0:T(8,128)(2,1)S(1)}, u32[]{:S(2)}, u32[]{:S(2)}) collective-permute-start(bf16[8,6144]{1,0:T(8,128)(2,1)S(1)} %stacked.1.after_ref.refs_0_), channel_id=1, source_target_pairs={{0,16},{8,24},{16,0},{24,8},{1,17},{9,25},{17,1},{25,9},{2,18},{10... | collective-permute-start | bytes 294920 | tf_op jit(solution)/shard_map/ppermute | solution.py:26
  11.2 7.4 %collective-permute-start.4 = (bf16[8,6144]{1,0:T(8,128)(2,1)S(1)}, bf16[8,6144]{1,0:T(8,128)(2,1)S(1)}, u32[]{:S(2)}, u32[]{:S(2)}) collective-permute-start(bf16[8,6144]{1,0:T(8,128)(2,1)S(1)} %stacked.1.after_ref.refs_0_), channel_id=1, source_target_pairs={{0,24},{8,16},{16,8},{24,0},{1,25},{9,17},{17,9},{25,1},{2,26},{10... | collective-permute-start | bytes 294920 | tf_op jit(solution)/shard_map/ppermute | solution.py:26
  11.2 8.6 %collective-permute-start.5 = (bf16[8,6144]{1,0:T(8,128)(2,1)S(1)}, bf16[8,6144]{1,0:T(8,128)(2,1)S(1)}, u32[]{:S(2)}, u32[]{:S(2)}) collective-permute-start(bf16[8,6144]{1,0:T(8,128)(2,1)S(1)} %stacked.1.after_ref.refs_0_), channel_id=1, source_target_pairs={{0,1},{1,0},{2,3},{3,2},{4,5},{5,4},{6,7},{7,6},{8,9},{9,8},{10,11... | collective-permute-start | bytes 294920 | tf_op jit(solution)/shard_map/ppermute | solution.py:26
  18.5 1.7 %collective-permute-start.8 = (bf16[8,6144]{1,0:T(8,128)(2,1)S(1)}, bf16[8,6144]{1,0:T(8,128)(2,1)S(1)}, u32[]{:S(2)}, u32[]{:S(2)}) collective-permute-start(bf16[8,6144]{1,0:T(8,128)(2,1)S(1)} %collective-permute-done.4.refs_3_), channel_id=1, source_target_pairs={{0,1},{1,0},{2,3},{3,2},{4,5},{5,4},{6,7},{7,6},{8,9},{9,8},{10,11... | collective-permute-start | bytes 294920 | tf_op jit(solution)/shard_map/ppermute | solution.py:26
  19.3 1.3 %collective-permute-start.7 = (bf16[8,6144]{1,0:T(8,128)(2,1)S(1)}, bf16[8,6144]{1,0:T(8,128)(2,1)S(1)}, u32[]{:S(2)}, u32[]{:S(2)}) collective-permute-start(bf16[8,6144]{1,0:T(8,128)(2,1)S(1)} %collective-permute-done.3.refs_2_), channel_id=1, source_target_pairs={{0,1},{1,0},{2,3},{3,2},{4,5},{5,4},{6,7},{7,6},{8,9},{9,8},{10,11... | collective-permute-start | bytes 294920 | tf_op jit(solution)/shard_map/ppermute | solution.py:26
  19.3 1.5 %collective-permute-start.6 = (bf16[8,6144]{1,0:T(8,128)(2,1)S(1)}, bf16[8,6144]{1,0:T(8,128)(2,1)S(1)}, u32[]{:S(2)}, u32[]{:S(2)}) collective-permute-start(bf16[8,6144]{1,0:T(8,128)(2,1)S(1)} %collective-permute-done.2.refs_1_), channel_id=1, source_target_pairs={{0,1},{1,0},{2,3},{3,2},{4,5},{5,4},{6,7},{7,6},{8,9},{9,8},{10,11... | collective-permute-start | bytes 294920 | tf_op jit(solution)/shard_map/ppermute | solution.py:26
  33.8 3.4 %collective-permute-start.9 = (bf16[64,3072]{1,0:T(8,128)(2,1)S(1)}, bf16[64,3072]{1,0:T(8,128)(2,1)S(1)}, u32[]{:S(2)}, u32[]{:S(2)}) collective-permute-start(bf16[64,3072]{1,0:T(8,128)(2,1)S(1)} %get-tuple-element.30), channel_id=1, source_target_pairs={{0,1},{1,0},{2,3},{3,2},{4,5},{5,4},{6,7},{7,6},{8,9},{9,8},{10,11... | collective-permute-start | bytes 1179656 | tf_op jit(solution)/shard_map/ppermute | solution.py:26
  37.3 4.9 %collective-permute-start.10 = (bf16[16,3072]{1,0:T(8,128)(2,1)S(1)}, bf16[16,3072]{1,0:T(8,128)(2,1)S(1)}, u32[]{:S(2)}, u32[]{:S(2)}) collective-permute-start(bf16[16,3072]{1,0:T(8,128)(2,1)S(1)} %get-tuple-element.32), channel_id=1, source_target_pairs={{0,8},{8,0},{16,24},{24,16},{1,9},{9,1},{17,25},{25,17},{2,10},{10... | collective-permute-start | bytes 294920 | tf_op jit(solution)/shard_map/ppermute | solution.py:26
  38.3 5.9 %collective-permute-start.11 = (bf16[16,3072]{1,0:T(8,128)(2,1)S(1)}, bf16[16,3072]{1,0:T(8,128)(2,1)S(1)}, u32[]{:S(2)}, u32[]{:S(2)}) collective-permute-start(bf16[16,3072]{1,0:T(8,128)(2,1)S(1)} %get-tuple-element.33), channel_id=1, source_target_pairs={{0,16},{8,24},{16,0},{24,8},{1,17},{9,25},{17,1},{25,9},{2,18},{10... | collective-permute-start | bytes 294920 | tf_op jit(solution)/shard_map/ppermute | solution.py:26
  39.8 5.5 %collective-permute-start.12 = (bf16[16,3072]{1,0:T(8,128)(2,1)S(1)}, bf16[16,3072]{1,0:T(8,128)(2,1)S(1)}, u32[]{:S(2)}, u32[]{:S(2)}) collective-permute-start(bf16[16,3072]{1,0:T(8,128)(2,1)S(1)} %get-tuple-element.34), channel_id=1, source_target_pairs={{0,24},{8,16},{16,8},{24,0},{1,25},{9,17},{17,9},{25,1},{2,26},{10... | collective-permute-start | bytes 294920 | tf_op jit(solution)/shard_map/ppermute | solution.py:26

commit v5 on v4

--- a/solution.py
+++ b/solution.py
@@ -52,7 +52,8 @@
         gain = jnp.where(kind == c, gains_ref[c : c + 1, :], gain)
     normed = (x * row_scale * gain).astype(jnp.bfloat16)
     target = lax.broadcasted_iota(jnp.int32, (count * rounds, rows), 0)
-    step = lax.axis_index("hid") * count + lax.shift_right_logical(target, log2(rounds))
+    turn = lax.shift_right_logical(target, log2(rounds))
+    step = turn * hids + lax.axis_index("hid")
     lane = jnp.bitwise_xor(step, lax.axis_index("regroup"))
     slot = jnp.bitwise_and(target, rounds - 1) * lanes + lane
     placing = (jnp.broadcast_to(slots_ref[0:1, :], slot.shape) == slot).astype(jnp.bfloat16)
@@ -92,7 +93,7 @@
     def pairs(t):
         for lane in range(lanes):
             for core in range(hids):
-                yield lane * hids + core, (lane ^ (core * count + t)) * hids + core
+                yield lane * hids + core, (lane ^ (t * hids + core)) * hids + core
 
     return [lax.ppermute(piece, ("regroup", "hid"), list(pairs(t))) for t, piece in enumerate(pieces)]
 
@@ -421,7 +422,7 @@
     )(*parts)
 
 
-def blk_sum_kernel(lanes, *refs):
+def blk_sum_kernel(lanes, hids, *refs):
     *part_refs, out_ref = refs
     total = part_refs[0][...]
     for ref in part_refs[1:]:
@@ -431,7 +432,10 @@
     r = lax.broadcasted_iota(jnp.int32, (rows, rows), 0)
     c = lax.broadcasted_iota(jnp.int32, (rows, rows), 1)
     step = jnp.bitwise_xor(jnp.bitwise_and(r, lanes - 1), lax.axis_index("regroup"))
-    order = (c == step * rounds + lax.shift_right_logical(r, log2(lanes))).astype(jnp.bfloat16)
+    turn = lax.shift_right_logical(step, log2(hids))
+    core = jnp.bitwise_and(step, hids - 1)
+    place = core * (lanes // hids) + turn
+    order = (c == place * rounds + lax.shift_right_logical(r, log2(lanes))).astype(jnp.bfloat16)
     out_ref[...] = jnp.dot(
         order, total.astype(jnp.bfloat16), preferred_element_type=jnp.float32
     ).astype(jnp.bfloat16)
@@ -439,7 +443,7 @@
 
 def blk_sum(parts):
     return pl.pallas_call(
-        functools.partial(blk_sum_kernel, lax.axis_size("regroup")),
+        functools.partial(blk_sum_kernel, lax.axis_size("regroup"), lax.axis_size("hid")),
         out_shape=jax.ShapeDtypeStruct(parts[0].shape, jnp.bfloat16),
         in_specs=[IN_VMEM] * len(parts),
         out_specs=IN_VMEM,

time: 46.3 us -> 45.3 us (0.978)
  starting transfers between devices: 16.6 us -> 15.4 us
    ppermute x11, starting transfers between devices: 12.7 us -> 10.5 us  [exchange(): return lax.ppermute(array, axis, [(i, i ^ step) for i in range(count)])]
    ppermute x2, starting transfers between devices: 3.88 us -> 4.9 us  [to_lanes(): lax.ppermute(piece, ('regroup', 'hid'), list(pairs(t)))]
  transfers between devices with their start and end apart: 13 -> 13, of which waited for: 7 -> 8; matrix products, arithmetic and copies ran while one was open for 0% -> 0% of each run, Pallas kernels for 14% -> 14%
where the time goes in v5:
time: 45.3 us; the launch traced here: 45.1 us
  Pallas kernels  21.9 us (48%)
  starting transfers between devices  15.4 us (34%)
  waiting for transfers between devices  7.71 us (17%)
    pallas_call x1, Pallas kernels, ffn(): pl.pallas_call(functools.partial(ffn_kernel, blocks, hids, (slots, part,...  13.1 us
    ppermute x11, starting transfers between devices, exchange(): return lax.ppermute(array, axis, [(i, i ^ step) for i in range(count)])  10.5 us
    ppermute x11, waiting for transfers between devices, exchange(): return lax.ppermute(array, axis, [(i, i ^ step) for i in range(count)])  5.56 us
    ppermute x2, starting transfers between devices, to_lanes(): lax.ppermute(piece, ('regroup', 'hid'), list(pairs(t)))  4.9 us
    pallas_call x1, Pallas kernels, early(): pl.pallas_call(functools.partial(early_kernel, width), out_shape=pltpu.VM...  3.39 us
    pallas_call x1, Pallas kernels, kept_part(): pl.pallas_call(kept_kernel, out_shape=jax.ShapeDtypeStruct((rows, width),...  2.92 us
    ppermute x2, waiting for transfers between devices, to_lanes(): lax.ppermute(piece, ('regroup', 'hid'), list(pairs(t)))  2.15 us
    pallas_call x1, Pallas kernels, norm(): pl.pallas_call(functools.partial(norm_kernel, lanes, hids), out_shape=(ja...  1.64 us
  transfers between devices with their start and end apart: 13, of which 8 were waited for; matrix products, arithmetic and copies ran while one was open for 0% of the time, Pallas kernels for 14%

profile of v5, /device:TPU:0, one launch (start us, length us, event | category | flops | bytes accessed | tf_op | source)
XLA Modules:
  0.0 45.1 jit_solution(17981644549206004937)
XLA Ops:
  0.0 0.0 copy-start
  0.0 1.6 %norm.1 = (bf16[4,6144]{1,0:T(4,128)(2,1)S(1)}, bf16[4,6144]{1,0:T(4,128)(2,1)S(1)}) custom-call(bf16[16,6144]{1,0:T(8,128)(2,1)} %refs_0_.1, s32[16]{0:T(128)} %refs_1_.1, s32[1,16]{1,0:T(1,128)} %refs_2_.1, f32[8,6144]{1,0:T(8,128)} %refs_3_.1), custom_call_target="tpu_custom_call" | custom-call | bytes 50331648 | tf_op jit(solution)/shard_map/norm/pallas_call | solution.py:69
  1.6 0.8 %collective-permute-start = (bf16[4,6144]{1,0:T(4,128)(2,1)S(1)}, bf16[4,6144]{1,0:T(4,128)(2,1)S(1)}, u32[]{:S(2)}, u32[]{:S(2)}) collective-permute-start(bf16[4,6144]{1,0:T(4,128)(2,1)S(1)} %get-tuple-element.20), channel_id=1, source_target_pairs={{0,0},{1,3},{2,2},{3,1},{4,4},{5,7},{6,6},{7,5},{8,8},{9,11},{10,1... | collective-permute-start | bytes 147464 | tf_op jit(solution)/shard_map/ppermute | solution.py:98
  2.4 4.1 %collective-permute-start.1 = (bf16[4,6144]{1,0:T(4,128)(2,1)S(1)}, bf16[4,6144]{1,0:T(4,128)(2,1)S(1)}, u32[]{:S(2)}, u32[]{:S(2)}) collective-permute-start(bf16[4,6144]{1,0:T(4,128)(2,1)S(1)} %get-tuple-element.21), channel_id=1, source_target_pairs={{0,4},{1,7},{2,6},{3,5},{4,0},{5,3},{6,2},{7,1},{8,12},{9,15},{10,... | collective-permute-start | bytes 147464 | tf_op jit(solution)/shard_map/ppermute | solution.py:98
  6.5 0.0 collective-permute-done.refs_0_
  6.6 2.2 %collective-permute-done.1.refs_1_ = bf16[4,6144]{1,0:T(4,128)(2,1)S(1)} collective-permute-done((bf16[4,6144]{1,0:T(4,128)(2,1)S(1)}, bf16[4,6144]{1,0:T(4,128)(2,1)S(1)}, u32[]{:S(2)}, u32[]{:S(2)}) %collective-permute-start.1) | collective-permute-done | bytes 49184 | tf_op jit(solution)/shard_map/ppermute | solution.py:98
  8.7 1.8 %collective-permute-start.2 = (bf16[8,6144]{1,0:T(8,128)(2,1)S(1)}, bf16[8,6144]{1,0:T(8,128)(2,1)S(1)}, u32[]{:S(2)}, u32[]{:S(2)}) collective-permute-start(bf16[8,6144]{1,0:T(8,128)(2,1)S(1)} %stacked.1.after_ref.refs_0_), channel_id=1, source_target_pairs={{0,8},{8,0},{16,24},{24,16},{1,9},{9,1},{17,25},{25,17},{2,10},{10... | collective-permute-start | bytes 294920 | tf_op jit(solution)/shard_map/ppermute | solution.py:26
  10.5 1.5 %collective-permute-start.3 = (bf16[8,6144]{1,0:T(8,128)(2,1)S(1)}, bf16[8,6144]{1,0:T(8,128)(2,1)S(1)}, u32[]{:S(2)}, u32[]{:S(2)}) collective-permute-start(bf16[8,6144]{1,0:T(8,128)(2,1)S(1)} %stacked.1.after_ref.refs_0_), channel_id=1, source_target_pairs={{0,16},{8,24},{16,0},{24,8},{1,17},{9,25},{17,1},{25,9},{2,18},{10... | collective-permute-start | bytes 294920 | tf_op jit(solution)/shard_map/ppermute | solution.py:26
  12.1 0.2 collective-permute-start.4
  12.3 1.8 %collective-permute-start.5 = (bf16[8,6144]{1,0:T(8,128)(2,1)S(1)}, bf16[8,6144]{1,0:T(8,128)(2,1)S(1)}, u32[]{:S(2)}, u32[]{:S(2)}) collective-permute-start(bf16[8,6144]{1,0:T(8,128)(2,1)S(1)} %stacked.1.after_ref.refs_0_), channel_id=1, source_target_pairs={{0,1},{1,0},{2,3},{3,2},{4,5},{5,4},{6,7},{7,6},{8,9},{9,8},{10,11... | collective-permute-start | bytes 294920 | tf_op jit(solution)/shard_map/ppermute | solution.py:26
  14.1 3.4 %early.1.refs_9_ = bf16[2048,2048]{1,0:T(8,128)(2,1)S(1)} custom-call(bf16[8,6144]{1,0:T(8,128)(2,1)S(1)} %stacked.1.after_ref.refs_0_, bf16[6144,2048]{1,0:T(8,128)(2,1)} %refs_10_.1), custom_call_target="tpu_custom_call" | custom-call | bytes 8388608 | tf_op jit(solution)/shard_map/early/pallas_call | solution.py:138
  17.5 0.0 collective-permute-done.2.refs_1_
  17.5 0.0 collective-permute-done.3.refs_2_
  17.5 0.3 collective-permute-done.4.refs_3_
  17.8 0.7 %collective-permute-start.8 = (bf16[8,6144]{1,0:T(8,128)(2,1)S(1)}, bf16[8,6144]{1,0:T(8,128)(2,1)S(1)}, u32[]{:S(2)}, u32[]{:S(2)}) collective-permute-start(bf16[8,6144]{1,0:T(8,128)(2,1)S(1)} %collective-permute-done.4.refs_3_), channel_id=1, source_target_pairs={{0,1},{1,0},{2,3},{3,2},{4,5},{5,4},{6,7},{7,6},{8,9},{9,8},{10,11... | collective-permute-start | bytes 294920 | tf_op jit(solution)/shard_map/ppermute | solution.py:26
  18.5 0.0 collective-permute-start.7
  18.5 0.5 %collective-permute-start.6 = (bf16[8,6144]{1,0:T(8,128)(2,1)S(1)}, bf16[8,6144]{1,0:T(8,128)(2,1)S(1)}, u32[]{:S(2)}, u32[]{:S(2)}) collective-permute-start(bf16[8,6144]{1,0:T(8,128)(2,1)S(1)} %collective-permute-done.2.refs_1_), channel_id=1, source_target_pairs={{0,1},{1,0},{2,3},{3,2},{4,5},{5,4},{6,7},{7,6},{8,9},{9,8},{10,11... | collective-permute-start | bytes 294920 | tf_op jit(solution)/shard_map/ppermute | solution.py:26
  19.0 0.0 collective-permute-done.5.refs_4_
  19.0 0.4 collective-permute-done.8.refs_7_
  19.4 0.4 collective-permute-done.7.refs_6_
  19.8 0.2 collective-permute-done.6.refs_5_
  19.9 0.0 copy-done
  19.9 13.1 %ffn.1 = (bf16[64,2048]{1,0:T(8,128)(2,1)S(1)}, bf16[2048,2048]{1,0:T(8,128)(2,1)S(1)}, bf16[64,3072]{1,0:T(8,128)(2,1)S(1)}) custom-call(bf16[8,6144]{1,0:T(8,128)(2,1)S(1)} %stacked.1.after_ref.refs_0_, bf16[8,6144]{1,0:T(8,128)(2,1)S(1)} %collective-permute-done.2.refs_1_, bf16[8,6144]{1,0:T(8,128)(2,1)S(1)} %collective-permute-done.3.refs_2_, ...), custom_call_target="tpu_custom_call" | custom-call | flops 4026531840 | bytes 50331648 | tf_op jit(solution)/shard_map/ffn/pallas_call | solution.py:323
  33.0 0.4 collective-permute-start.9
  33.4 2.9 %kept_part.1.refs_0_ = f32[64,3072]{1,0:T(8,128)S(1)} custom-call(bf16[64,2048]{1,0:T(8,128)(2,1)S(1)} %get-tuple-element.28.hidden_ref, bf16[2048,2048]{1,0:T(8,128)(2,1)S(1)} %get-tuple-element.29.kept_ref, bf16[2048,6144]{1,0:T(8,128)(2,1)} %down_ref.1), custom_call_target="tpu_custom_call" | custom-call | flops 805306368 | bytes 12582912 | tf_op jit(solution)/shard_map/kept_part/pallas_call | solution.py:384
  36.3 0.0 collective-permute-done.9.refs_1_
  36.4 0.1 hid_sum.1
  36.4 1.1 %collective-permute-start.10 = (bf16[16,3072]{1,0:T(8,128)(2,1)S(1)}, bf16[16,3072]{1,0:T(8,128)(2,1)S(1)}, u32[]{:S(2)}, u32[]{:S(2)}) collective-permute-start(bf16[16,3072]{1,0:T(8,128)(2,1)S(1)} %get-tuple-element.32), channel_id=1, source_target_pairs={{0,8},{8,0},{16,24},{24,16},{1,9},{9,1},{17,25},{25,17},{2,10},{10... | collective-permute-start | bytes 294920 | tf_op jit(solution)/shard_map/ppermute | solution.py:26
  37.5 1.3 %collective-permute-start.11 = (bf16[16,3072]{1,0:T(8,128)(2,1)S(1)}, bf16[16,3072]{1,0:T(8,128)(2,1)S(1)}, u32[]{:S(2)}, u32[]{:S(2)}) collective-permute-start(bf16[16,3072]{1,0:T(8,128)(2,1)S(1)} %get-tuple-element.33), channel_id=1, source_target_pairs={{0,16},{8,24},{16,0},{24,8},{1,17},{9,25},{17,1},{25,9},{2,18},{10... | collective-permute-start | bytes 294920 | tf_op jit(solution)/shard_map/ppermute | solution.py:26
  38.8 1.2 %collective-permute-start.12 = (bf16[16,3072]{1,0:T(8,128)(2,1)S(1)}, bf16[16,3072]{1,0:T(8,128)(2,1)S(1)}, u32[]{:S(2)}, u32[]{:S(2)}) collective-permute-start(bf16[16,3072]{1,0:T(8,128)(2,1)S(1)} %get-tuple-element.34), channel_id=1, source_target_pairs={{0,24},{8,16},{16,8},{24,0},{1,25},{9,17},{17,9},{25,1},{2,26},{10... | collective-permute-start | bytes 294920 | tf_op jit(solution)/shard_map/ppermute | solution.py:26
  40.0 1.5 %collective-permute-done.10.refs_1_ = bf16[16,3072]{1,0:T(8,128)(2,1)S(1)} collective-permute-done((bf16[16,3072]{1,0:T(8,128)(2,1)S(1)}, bf16[16,3072]{1,0:T(8,128)(2,1)S(1)}, u32[]{:S(2)}, u32[]{:S(2)}) %collective-permute-start.10) | collective-permute-done | bytes 98336 | tf_op jit(solution)/shard_map/ppermute | solution.py:26
  41.5 1.7 %collective-permute-done.11.refs_2_ = bf16[16,3072]{1,0:T(8,128)(2,1)S(1)} collective-permute-done((bf16[16,3072]{1,0:T(8,128)(2,1)S(1)}, bf16[16,3072]{1,0:T(8,128)(2,1)S(1)}, u32[]{:S(2)}, u32[]{:S(2)}) %collective-permute-start.11) | collective-permute-done | bytes 98336 | tf_op jit(solution)/shard_map/ppermute | solution.py:26
  43.2 1.1 %collective-permute-done.12.refs_3_ = bf16[16,3072]{1,0:T(8,128)(2,1)S(1)} collective-permute-done((bf16[16,3072]{1,0:T(8,128)(2,1)S(1)}, bf16[16,3072]{1,0:T(8,128)(2,1)S(1)}, u32[]{:S(2)}, u32[]{:S(2)}) %collective-permute-start.12) | collective-permute-done | bytes 98336 | tf_op jit(solution)/shard_map/ppermute | solution.py:26
  44.3 0.8 %blk_sum.1 = bf16[16,3072]{1,0:T(8,128)(2,1)} custom-call(f32[16,3072]{1,0:T(8,128)S(1)} %get-tuple-element.31.refs_0_, bf16[16,3072]{1,0:T(8,128)(2,1)S(1)} %collective-permute-done.10.refs_1_, bf16[16,3072]{1,0:T(8,128)(2,1)S(1)} %collective-permute-done.11.refs_2_, bf16[16,3072]{1,0:T(8,128)(2,1)S(1)} %collective-permute-done.12.refs_3_), custom_call_target="tpu_custom_call" | custom-call | tf_op jit(solution)/shard_map/blk_sum/pallas_call | solution.py:445
  (1 shorter events, 0.0 us)
Async XLA Ops:
  0.0 19.9 %copy-start = (bf16[6144,2048]{1,0:T(8,128)(2,1)S(1)}, bf16[6144,2048]{1,0:T(8,128)(2,1)}, u32[]{:S(2)}) copy-start(bf16[6144,2048]{1,0:T(8,128)(2,1)} %refs_8_.1) | copy-start | bytes 75497472
  1.6 4.9 %collective-permute-start = (bf16[4,6144]{1,0:T(4,128)(2,1)S(1)}, bf16[4,6144]{1,0:T(4,128)(2,1)S(1)}, u32[]{:S(2)}, u32[]{:S(2)}) collective-permute-start(bf16[4,6144]{1,0:T(4,128)(2,1)S(1)} %get-tuple-element.20), channel_id=1, source_target_pairs={{0,0},{1,3},{2,2},{3,1},{4,4},{5,7},{6,6},{7,5},{8,8},{9,11},{10,1... | collective-permute-start | bytes 147464 | tf_op jit(solution)/shard_map/ppermute | solution.py:98
  2.4 6.3 %collective-permute-start.1 = (bf16[4,6144]{1,0:T(4,128)(2,1)S(1)}, bf16[4,6144]{1,0:T(4,128)(2,1)S(1)}, u32[]{:S(2)}, u32[]{:S(2)}) collective-permute-start(bf16[4,6144]{1,0:T(4,128)(2,1)S(1)} %get-tuple-element.21), channel_id=1, source_target_pairs={{0,4},{1,7},{2,6},{3,5},{4,0},{5,3},{6,2},{7,1},{8,12},{9,15},{10,... | collective-permute-start | bytes 147464 | tf_op jit(solution)/shard_map/ppermute | solution.py:98
  8.7 8.7 %collective-permute-start.2 = (bf16[8,6144]{1,0:T(8,128)(2,1)S(1)}, bf16[8,6144]{1,0:T(8,128)(2,1)S(1)}, u32[]{:S(2)}, u32[]{:S(2)}) collective-permute-start(bf16[8,6144]{1,0:T(8,128)(2,1)S(1)} %stacked.1.after_ref.refs_0_), channel_id=1, source_target_pairs={{0,8},{8,0},{16,24},{24,16},{1,9},{9,1},{17,25},{25,17},{2,10},{10... | collective-permute-start | bytes 294920 | tf_op jit(solution)/shard_map/ppermute | solution.py:26
  10.5 7.0 %collective-permute-start.3 = (bf16[8,6144]{1,0:T(8,128)(2,1)S(1)}, bf16[8,6144]{1,0:T(8,128)(2,1)S(1)}, u32[]{:S(2)}, u32[]{:S(2)}) collective-permute-start(bf16[8,6144]{1,0:T(8,128)(2,1)S(1)} %stacked.1.after_ref.refs_0_), channel_id=1, source_target_pairs={{0,16},{8,24},{16,0},{24,8},{1,17},{9,25},{17,1},{25,9},{2,18},{10... | collective-permute-start | bytes 294920 | tf_op jit(solution)/shard_map/ppermute | solution.py:26
  12.1 5.7 %collective-permute-start.4 = (bf16[8,6144]{1,0:T(8,128)(2,1)S(1)}, bf16[8,6144]{1,0:T(8,128)(2,1)S(1)}, u32[]{:S(2)}, u32[]{:S(2)}) collective-permute-start(bf16[8,6144]{1,0:T(8,128)(2,1)S(1)} %stacked.1.after_ref.refs_0_), channel_id=1, source_target_pairs={{0,24},{8,16},{16,8},{24,0},{1,25},{9,17},{17,9},{25,1},{2,26},{10... | collective-permute-start | bytes 294920 | tf_op jit(solution)/shard_map/ppermute | solution.py:26
  12.3 6.7 %collective-permute-start.5 = (bf16[8,6144]{1,0:T(8,128)(2,1)S(1)}, bf16[8,6144]{1,0:T(8,128)(2,1)S(1)}, u32[]{:S(2)}, u32[]{:S(2)}) collective-permute-start(bf16[8,6144]{1,0:T(8,128)(2,1)S(1)} %stacked.1.after_ref.refs_0_), channel_id=1, source_target_pairs={{0,1},{1,0},{2,3},{3,2},{4,5},{5,4},{6,7},{7,6},{8,9},{9,8},{10,11... | collective-permute-start | bytes 294920 | tf_op jit(solution)/shard_map/ppermute | solution.py:26
  17.8 1.6 %collective-permute-start.8 = (bf16[8,6144]{1,0:T(8,128)(2,1)S(1)}, bf16[8,6144]{1,0:T(8,128)(2,1)S(1)}, u32[]{:S(2)}, u32[]{:S(2)}) collective-permute-start(bf16[8,6144]{1,0:T(8,128)(2,1)S(1)} %collective-permute-done.4.refs_3_), channel_id=1, source_target_pairs={{0,1},{1,0},{2,3},{3,2},{4,5},{5,4},{6,7},{7,6},{8,9},{9,8},{10,11... | collective-permute-start | bytes 294920 | tf_op jit(solution)/shard_map/ppermute | solution.py:26
  18.5 1.3 %collective-permute-start.7 = (bf16[8,6144]{1,0:T(8,128)(2,1)S(1)}, bf16[8,6144]{1,0:T(8,128)(2,1)S(1)}, u32[]{:S(2)}, u32[]{:S(2)}) collective-permute-start(bf16[8,6144]{1,0:T(8,128)(2,1)S(1)} %collective-permute-done.3.refs_2_), channel_id=1, source_target_pairs={{0,1},{1,0},{2,3},{3,2},{4,5},{5,4},{6,7},{7,6},{8,9},{9,8},{10,11... | collective-permute-start | bytes 294920 | tf_op jit(solution)/shard_map/ppermute | solution.py:26
  18.5 1.5 %collective-permute-start.6 = (bf16[8,6144]{1,0:T(8,128)(2,1)S(1)}, bf16[8,6144]{1,0:T(8,128)(2,1)S(1)}, u32[]{:S(2)}, u32[]{:S(2)}) collective-permute-start(bf16[8,6144]{1,0:T(8,128)(2,1)S(1)} %collective-permute-done.2.refs_1_), channel_id=1, source_target_pairs={{0,1},{1,0},{2,3},{3,2},{4,5},{5,4},{6,7},{7,6},{8,9},{9,8},{10,11... | collective-permute-start | bytes 294920 | tf_op jit(solution)/shard_map/ppermute | solution.py:26
  33.0 3.4 %collective-permute-start.9 = (bf16[64,3072]{1,0:T(8,128)(2,1)S(1)}, bf16[64,3072]{1,0:T(8,128)(2,1)S(1)}, u32[]{:S(2)}, u32[]{:S(2)}) collective-permute-start(bf16[64,3072]{1,0:T(8,128)(2,1)S(1)} %get-tuple-element.30), channel_id=1, source_target_pairs={{0,1},{1,0},{2,3},{3,2},{4,5},{5,4},{6,7},{7,6},{8,9},{9,8},{10,11... | collective-permute-start | bytes 1179656 | tf_op jit(solution)/shard_map/ppermute | solution.py:26
  36.4 5.1 %collective-permute-start.10 = (bf16[16,3072]{1,0:T(8,128)(2,1)S(1)}, bf16[16,3072]{1,0:T(8,128)(2,1)S(1)}, u32[]{:S(2)}, u32[]{:S(2)}) collective-permute-start(bf16[16,3072]{1,0:T(8,128)(2,1)S(1)} %get-tuple-element.32), channel_id=1, source_target_pairs={{0,8},{8,0},{16,24},{24,16},{1,9},{9,1},{17,25},{25,17},{2,10},{10... | collective-permute-start | bytes 294920 | tf_op jit(solution)/shard_map/ppermute | solution.py:26
  37.5 5.7 %collective-permute-start.11 = (bf16[16,3072]{1,0:T(8,128)(2,1)S(1)}, bf16[16,3072]{1,0:T(8,128)(2,1)S(1)}, u32[]{:S(2)}, u32[]{:S(2)}) collective-permute-start(bf16[16,3072]{1,0:T(8,128)(2,1)S(1)} %get-tuple-element.33), channel_id=1, source_target_pairs={{0,16},{8,24},{16,0},{24,8},{1,17},{9,25},{17,1},{25,9},{2,18},{10... | collective-permute-start | bytes 294920 | tf_op jit(solution)/shard_map/ppermute | solution.py:26
  38.8 5.5 %collective-permute-start.12 = (bf16[16,3072]{1,0:T(8,128)(2,1)S(1)}, bf16[16,3072]{1,0:T(8,128)(2,1)S(1)}, u32[]{:S(2)}, u32[]{:S(2)}) collective-permute-start(bf16[16,3072]{1,0:T(8,128)(2,1)S(1)} %get-tuple-element.34), channel_id=1, source_target_pairs={{0,24},{8,16},{16,8},{24,0},{1,25},{9,17},{17,9},{25,1},{2,26},{10... | collective-permute-start | bytes 294920 | tf_op jit(solution)/shard_map/ppermute | solution.py:26

commit v6 on v5

--- a/solution.py
+++ b/solution.py
@@ -120,6 +120,10 @@
     )(*pieces)
 
 
+def twice(count):
+    return 1 if count % 2 else 2
+
+
 def even(total, most):
     return next(size for size in range(min(most, total), 0, -128) if total % size == 0)
 
@@ -223,18 +227,11 @@
     for n in range(slots):
         start_next(n)
     kept_copy(0).start()
-    cores = lax.broadcasted_iota(jnp.int32, (each // hids, 1), 0) * 0 + me
     for step in range(blocks):
         sides = [
             panel_refs[side * blocks + step][...].astype(jnp.float32) for side in range(hids)
         ]
-        lined = []
-        for core in range(hids):
-            rows_of = sides[core]
-            for mine in range(1, hids):
-                rows_of = jnp.where(cores == mine, sides[core ^ mine], rows_of)
-            lined.append(rows_of)
-        panel[step * each : (step + 1) * each, :] = jnp.concatenate(lined, axis=0).astype(
+        panel[step * each : (step + 1) * each, :] = jnp.concatenate(sides, axis=0).astype(
             jnp.bfloat16
         )
     chunk = even(shard, 1024)
@@ -258,7 +255,7 @@
         columns = pl.ds(pl.multiple_of(c * chunk, chunk), chunk)
         act[:, columns] = gate_act(columns)
 
-    @pl.loop(skip, hids * inside)
+    @pl.loop(skip, hids * inside, unroll=twice(hids * inside - skip))
     def _(u):
         side, p = u // inside, u % inside
         x = panel[:, pl.ds(pl.multiple_of(side_start(side) + p * part, part), part)]
@@ -360,7 +357,7 @@
     for n in range(more):
         copy(n).start()
 
-    @pl.loop(0, have // band)
+    @pl.loop(0, have // band, unroll=twice(have // band))
     def _(n):
         columns = pl.ds(pl.multiple_of(n * band, 128), band)
         out_ref[:, columns] = jnp.dot(
@@ -398,13 +395,20 @@
     )(hidden, kept, down_weight)
 
 
-def hid_sum_kernel(count, *refs):
-    total = refs[0][...]
-    for ref in refs[1:count]:
-        total += ref[...].astype(jnp.float32)
-    each = total.shape[0] // len(refs[count:])
-    for step, ref in enumerate(refs[count:]):
-        ref[...] = total[step * each : (step + 1) * each, :].astype(ref.dtype)
+def hid_sum_kernel(hids, *refs):
+    parts = [ref[...].astype(jnp.float32) for ref in refs[:hids]]
+    each = parts[0].shape[0] // len(refs[hids:])
+    size = each // hids
+    for step, ref in enumerate(refs[hids:]):
+        lined = []
+        for side in range(hids):
+            total = None
+            for q, part in enumerate(parts):
+                start = step * each + (side ^ q) * size
+                value = part[start : start + size, :]
+                total = value if total is None else total + value
+            lined.append(total)
+        ref[...] = jnp.concatenate(lined, axis=0).astype(ref.dtype)
 
 
 def hid_sum(parts, blocks):
@@ -433,8 +437,8 @@
     c = lax.broadcasted_iota(jnp.int32, (rows, rows), 1)
     step = jnp.bitwise_xor(jnp.bitwise_and(r, lanes - 1), lax.axis_index("regroup"))
     turn = lax.shift_right_logical(step, log2(hids))
-    core = jnp.bitwise_and(step, hids - 1)
-    place = core * (lanes // hids) + turn
+    side = jnp.bitwise_xor(jnp.bitwise_and(step, hids - 1), lax.axis_index("hid"))
+    place = side * (lanes // hids) + turn
     order = (c == place * rounds + lax.shift_right_logical(r, log2(lanes))).astype(jnp.bfloat16)
     out_ref[...] = jnp.dot(
         order, total.astype(jnp.bfloat16), preferred_element_type=jnp.float32

time: 45.3 us -> 44.8 us (0.989)
  no operation moved by 1% of the time
where the time goes in v6:
time: 44.8 us; the launch traced here: 44.7 us
  Pallas kernels  21.5 us (48%)
  starting transfers between devices  15.4 us (34%)
  waiting for transfers between devices  7.73 us (17%)
    pallas_call x1, Pallas kernels, ffn(): pl.pallas_call(functools.partial(ffn_kernel, blocks, hids, (slots, part,...  12.8 us
    ppermute x11, starting transfers between devices, exchange(): return lax.ppermute(array, axis, [(i, i ^ step) for i in range(count)])  10.5 us
    ppermute x11, waiting for transfers between devices, exchange(): return lax.ppermute(array, axis, [(i, i ^ step) for i in range(count)])  5.57 us
    ppermute x2, starting transfers between devices, to_lanes(): lax.ppermute(piece, ('regroup', 'hid'), list(pairs(t)))  4.9 us
    pallas_call x1, Pallas kernels, early(): pl.pallas_call(functools.partial(early_kernel, width), out_shape=pltpu.VM...  3.39 us
    pallas_call x1, Pallas kernels, kept_part(): pl.pallas_call(kept_kernel, out_shape=jax.ShapeDtypeStruct((rows, width),...  2.73 us
    ppermute x2, waiting for transfers between devices, to_lanes(): lax.ppermute(piece, ('regroup', 'hid'), list(pairs(t)))  2.15 us
    pallas_call x1, Pallas kernels, norm(): pl.pallas_call(functools.partial(norm_kernel, lanes, hids), out_shape=(ja...  1.64 us
  transfers between devices with their start and end apart: 13, of which 8 were waited for; matrix products, arithmetic and copies ran while one was open for 0% of the time, Pallas kernels for 14%

profile of v6, /device:TPU:0, one launch (start us, length us, event | category | flops | bytes accessed | tf_op | source)
XLA Modules:
  0.0 44.7 jit_solution(16167209038123988398)
XLA Ops:
  0.0 0.0 copy-start
  0.0 1.6 %norm.1 = (bf16[4,6144]{1,0:T(4,128)(2,1)S(1)}, bf16[4,6144]{1,0:T(4,128)(2,1)S(1)}) custom-call(bf16[16,6144]{1,0:T(8,128)(2,1)} %refs_0_.1, s32[16]{0:T(128)} %refs_1_.1, s32[1,16]{1,0:T(1,128)} %refs_2_.1, f32[8,6144]{1,0:T(8,128)} %refs_3_.1), custom_call_target="tpu_custom_call" | custom-call | bytes 50331648 | tf_op jit(solution)/shard_map/norm/pallas_call | solution.py:69
  1.6 0.8 %collective-permute-start = (bf16[4,6144]{1,0:T(4,128)(2,1)S(1)}, bf16[4,6144]{1,0:T(4,128)(2,1)S(1)}, u32[]{:S(2)}, u32[]{:S(2)}) collective-permute-start(bf16[4,6144]{1,0:T(4,128)(2,1)S(1)} %get-tuple-element.20), channel_id=1, source_target_pairs={{0,0},{1,3},{2,2},{3,1},{4,4},{5,7},{6,6},{7,5},{8,8},{9,11},{10,1... | collective-permute-start | bytes 147464 | tf_op jit(solution)/shard_map/ppermute | solution.py:98
  2.4 4.1 %collective-permute-start.1 = (bf16[4,6144]{1,0:T(4,128)(2,1)S(1)}, bf16[4,6144]{1,0:T(4,128)(2,1)S(1)}, u32[]{:S(2)}, u32[]{:S(2)}) collective-permute-start(bf16[4,6144]{1,0:T(4,128)(2,1)S(1)} %get-tuple-element.21), channel_id=1, source_target_pairs={{0,4},{1,7},{2,6},{3,5},{4,0},{5,3},{6,2},{7,1},{8,12},{9,15},{10,... | collective-permute-start | bytes 147464 | tf_op jit(solution)/shard_map/ppermute | solution.py:98
  6.5 0.0 collective-permute-done.refs_0_
  6.6 2.2 %collective-permute-done.1.refs_1_ = bf16[4,6144]{1,0:T(4,128)(2,1)S(1)} collective-permute-done((bf16[4,6144]{1,0:T(4,128)(2,1)S(1)}, bf16[4,6144]{1,0:T(4,128)(2,1)S(1)}, u32[]{:S(2)}, u32[]{:S(2)}) %collective-permute-start.1) | collective-permute-done | bytes 49184 | tf_op jit(solution)/shard_map/ppermute | solution.py:98
  8.7 1.8 %collective-permute-start.2 = (bf16[8,6144]{1,0:T(8,128)(2,1)S(1)}, bf16[8,6144]{1,0:T(8,128)(2,1)S(1)}, u32[]{:S(2)}, u32[]{:S(2)}) collective-permute-start(bf16[8,6144]{1,0:T(8,128)(2,1)S(1)} %stacked.1.after_ref.refs_0_), channel_id=1, source_target_pairs={{0,8},{8,0},{16,24},{24,16},{1,9},{9,1},{17,25},{25,17},{2,10},{10... | collective-permute-start | bytes 294920 | tf_op jit(solution)/shard_map/ppermute | solution.py:26
  10.5 1.5 %collective-permute-start.3 = (bf16[8,6144]{1,0:T(8,128)(2,1)S(1)}, bf16[8,6144]{1,0:T(8,128)(2,1)S(1)}, u32[]{:S(2)}, u32[]{:S(2)}) collective-permute-start(bf16[8,6144]{1,0:T(8,128)(2,1)S(1)} %stacked.1.after_ref.refs_0_), channel_id=1, source_target_pairs={{0,16},{8,24},{16,0},{24,8},{1,17},{9,25},{17,1},{25,9},{2,18},{10... | collective-permute-start | bytes 294920 | tf_op jit(solution)/shard_map/ppermute | solution.py:26
  12.1 0.2 collective-permute-start.4
  12.3 1.8 %collective-permute-start.5 = (bf16[8,6144]{1,0:T(8,128)(2,1)S(1)}, bf16[8,6144]{1,0:T(8,128)(2,1)S(1)}, u32[]{:S(2)}, u32[]{:S(2)}) collective-permute-start(bf16[8,6144]{1,0:T(8,128)(2,1)S(1)} %stacked.1.after_ref.refs_0_), channel_id=1, source_target_pairs={{0,1},{1,0},{2,3},{3,2},{4,5},{5,4},{6,7},{7,6},{8,9},{9,8},{10,11... | collective-permute-start | bytes 294920 | tf_op jit(solution)/shard_map/ppermute | solution.py:26
  14.1 3.4 %early.1.refs_9_ = bf16[2048,2048]{1,0:T(8,128)(2,1)S(1)} custom-call(bf16[8,6144]{1,0:T(8,128)(2,1)S(1)} %stacked.1.after_ref.refs_0_, bf16[6144,2048]{1,0:T(8,128)(2,1)} %refs_10_.1), custom_call_target="tpu_custom_call" | custom-call | bytes 8388608 | tf_op jit(solution)/shard_map/early/pallas_call | solution.py:142
  17.5 0.0 collective-permute-done.2.refs_1_
  17.5 0.0 collective-permute-done.3.refs_2_
  17.5 0.3 collective-permute-done.4.refs_3_
  17.8 0.7 %collective-permute-start.8 = (bf16[8,6144]{1,0:T(8,128)(2,1)S(1)}, bf16[8,6144]{1,0:T(8,128)(2,1)S(1)}, u32[]{:S(2)}, u32[]{:S(2)}) collective-permute-start(bf16[8,6144]{1,0:T(8,128)(2,1)S(1)} %collective-permute-done.4.refs_3_), channel_id=1, source_target_pairs={{0,1},{1,0},{2,3},{3,2},{4,5},{5,4},{6,7},{7,6},{8,9},{9,8},{10,11... | collective-permute-start | bytes 294920 | tf_op jit(solution)/shard_map/ppermute | solution.py:26
  18.5 0.0 collective-permute-start.7
  18.5 0.5 %collective-permute-start.6 = (bf16[8,6144]{1,0:T(8,128)(2,1)S(1)}, bf16[8,6144]{1,0:T(8,128)(2,1)S(1)}, u32[]{:S(2)}, u32[]{:S(2)}) collective-permute-start(bf16[8,6144]{1,0:T(8,128)(2,1)S(1)} %collective-permute-done.2.refs_1_), channel_id=1, source_target_pairs={{0,1},{1,0},{2,3},{3,2},{4,5},{5,4},{6,7},{7,6},{8,9},{9,8},{10,11... | collective-permute-start | bytes 294920 | tf_op jit(solution)/shard_map/ppermute | solution.py:26
  19.0 0.0 collective-permute-done.5.refs_4_
  19.0 0.4 collective-permute-done.8.refs_7_
  19.4 0.4 collective-permute-done.7.refs_6_
  19.8 0.2 collective-permute-done.6.refs_5_
  19.9 0.0 copy-done
  19.9 12.8 %ffn.1 = (bf16[64,2048]{1,0:T(8,128)(2,1)S(1)}, bf16[2048,2048]{1,0:T(8,128)(2,1)S(1)}, bf16[64,3072]{1,0:T(8,128)(2,1)S(1)}) custom-call(bf16[8,6144]{1,0:T(8,128)(2,1)S(1)} %stacked.1.after_ref.refs_0_, bf16[8,6144]{1,0:T(8,128)(2,1)S(1)} %collective-permute-done.2.refs_1_, bf16[8,6144]{1,0:T(8,128)(2,1)S(1)} %collective-permute-done.3.refs_2_, ...), custom_call_target="tpu_custom_call" | custom-call | flops 4026531840 | bytes 50331648 | tf_op jit(solution)/shard_map/ffn/pallas_call | solution.py:320
  32.7 0.4 collective-permute-start.9
  33.1 2.7 %kept_part.1.refs_0_ = f32[64,3072]{1,0:T(8,128)S(1)} custom-call(bf16[64,2048]{1,0:T(8,128)(2,1)S(1)} %get-tuple-element.28.hidden_ref, bf16[2048,2048]{1,0:T(8,128)(2,1)S(1)} %get-tuple-element.29.kept_ref, bf16[2048,6144]{1,0:T(8,128)(2,1)} %down_ref.1), custom_call_target="tpu_custom_call" | custom-call | flops 805306368 | bytes 12582912 | tf_op jit(solution)/shard_map/kept_part/pallas_call | solution.py:381
  35.9 0.0 collective-permute-done.9.refs_1_
  35.9 0.1 hid_sum.1
  36.0 1.1 %collective-permute-start.10 = (bf16[16,3072]{1,0:T(8,128)(2,1)S(1)}, bf16[16,3072]{1,0:T(8,128)(2,1)S(1)}, u32[]{:S(2)}, u32[]{:S(2)}) collective-permute-start(bf16[16,3072]{1,0:T(8,128)(2,1)S(1)} %get-tuple-element.32), channel_id=1, source_target_pairs={{0,8},{8,0},{16,24},{24,16},{1,9},{9,1},{17,25},{25,17},{2,10},{10... | collective-permute-start | bytes 294920 | tf_op jit(solution)/shard_map/ppermute | solution.py:26
  37.0 1.3 %collective-permute-start.11 = (bf16[16,3072]{1,0:T(8,128)(2,1)S(1)}, bf16[16,3072]{1,0:T(8,128)(2,1)S(1)}, u32[]{:S(2)}, u32[]{:S(2)}) collective-permute-start(bf16[16,3072]{1,0:T(8,128)(2,1)S(1)} %get-tuple-element.33), channel_id=1, source_target_pairs={{0,16},{8,24},{16,0},{24,8},{1,17},{9,25},{17,1},{25,9},{2,18},{10... | collective-permute-start | bytes 294920 | tf_op jit(solution)/shard_map/ppermute | solution.py:26
  38.3 1.2 %collective-permute-start.12 = (bf16[16,3072]{1,0:T(8,128)(2,1)S(1)}, bf16[16,3072]{1,0:T(8,128)(2,1)S(1)}, u32[]{:S(2)}, u32[]{:S(2)}) collective-permute-start(bf16[16,3072]{1,0:T(8,128)(2,1)S(1)} %get-tuple-element.34), channel_id=1, source_target_pairs={{0,24},{8,16},{16,8},{24,0},{1,25},{9,17},{17,9},{25,1},{2,26},{10... | collective-permute-start | bytes 294920 | tf_op jit(solution)/shard_map/ppermute | solution.py:26
  39.5 1.5 %collective-permute-done.10.refs_1_ = bf16[16,3072]{1,0:T(8,128)(2,1)S(1)} collective-permute-done((bf16[16,3072]{1,0:T(8,128)(2,1)S(1)}, bf16[16,3072]{1,0:T(8,128)(2,1)S(1)}, u32[]{:S(2)}, u32[]{:S(2)}) %collective-permute-start.10) | collective-permute-done | bytes 98336 | tf_op jit(solution)/shard_map/ppermute | solution.py:26
  41.1 1.7 %collective-permute-done.11.refs_2_ = bf16[16,3072]{1,0:T(8,128)(2,1)S(1)} collective-permute-done((bf16[16,3072]{1,0:T(8,128)(2,1)S(1)}, bf16[16,3072]{1,0:T(8,128)(2,1)S(1)}, u32[]{:S(2)}, u32[]{:S(2)}) %collective-permute-start.11) | collective-permute-done | bytes 98336 | tf_op jit(solution)/shard_map/ppermute | solution.py:26
  42.7 1.1 %collective-permute-done.12.refs_3_ = bf16[16,3072]{1,0:T(8,128)(2,1)S(1)} collective-permute-done((bf16[16,3072]{1,0:T(8,128)(2,1)S(1)}, bf16[16,3072]{1,0:T(8,128)(2,1)S(1)}, u32[]{:S(2)}, u32[]{:S(2)}) %collective-permute-start.12) | collective-permute-done | bytes 98336 | tf_op jit(solution)/shard_map/ppermute | solution.py:26
  43.8 0.8 %blk_sum.1 = bf16[16,3072]{1,0:T(8,128)(2,1)} custom-call(f32[16,3072]{1,0:T(8,128)S(1)} %get-tuple-element.31.refs_0_, bf16[16,3072]{1,0:T(8,128)(2,1)S(1)} %collective-permute-done.10.refs_1_, bf16[16,3072]{1,0:T(8,128)(2,1)S(1)} %collective-permute-done.11.refs_2_, bf16[16,3072]{1,0:T(8,128)(2,1)S(1)} %collective-permute-done.12.refs_3_), custom_call_target="tpu_custom_call" | custom-call | tf_op jit(solution)/shard_map/blk_sum/pallas_call | solution.py:449
  (1 shorter events, 0.0 us)
Async XLA Ops:
  0.0 19.9 %copy-start = (bf16[6144,2048]{1,0:T(8,128)(2,1)S(1)}, bf16[6144,2048]{1,0:T(8,128)(2,1)}, u32[]{:S(2)}) copy-start(bf16[6144,2048]{1,0:T(8,128)(2,1)} %refs_8_.1) | copy-start | bytes 75497472
  1.6 4.9 %collective-permute-start = (bf16[4,6144]{1,0:T(4,128)(2,1)S(1)}, bf16[4,6144]{1,0:T(4,128)(2,1)S(1)}, u32[]{:S(2)}, u32[]{:S(2)}) collective-permute-start(bf16[4,6144]{1,0:T(4,128)(2,1)S(1)} %get-tuple-element.20), channel_id=1, source_target_pairs={{0,0},{1,3},{2,2},{3,1},{4,4},{5,7},{6,6},{7,5},{8,8},{9,11},{10,1... | collective-permute-start | bytes 147464 | tf_op jit(solution)/shard_map/ppermute | solution.py:98
  2.4 6.3 %collective-permute-start.1 = (bf16[4,6144]{1,0:T(4,128)(2,1)S(1)}, bf16[4,6144]{1,0:T(4,128)(2,1)S(1)}, u32[]{:S(2)}, u32[]{:S(2)}) collective-permute-start(bf16[4,6144]{1,0:T(4,128)(2,1)S(1)} %get-tuple-element.21), channel_id=1, source_target_pairs={{0,4},{1,7},{2,6},{3,5},{4,0},{5,3},{6,2},{7,1},{8,12},{9,15},{10,... | collective-permute-start | bytes 147464 | tf_op jit(solution)/shard_map/ppermute | solution.py:98
  8.7 8.7 %collective-permute-start.2 = (bf16[8,6144]{1,0:T(8,128)(2,1)S(1)}, bf16[8,6144]{1,0:T(8,128)(2,1)S(1)}, u32[]{:S(2)}, u32[]{:S(2)}) collective-permute-start(bf16[8,6144]{1,0:T(8,128)(2,1)S(1)} %stacked.1.after_ref.refs_0_), channel_id=1, source_target_pairs={{0,8},{8,0},{16,24},{24,16},{1,9},{9,1},{17,25},{25,17},{2,10},{10... | collective-permute-start | bytes 294920 | tf_op jit(solution)/shard_map/ppermute | solution.py:26
  10.5 7.0 %collective-permute-start.3 = (bf16[8,6144]{1,0:T(8,128)(2,1)S(1)}, bf16[8,6144]{1,0:T(8,128)(2,1)S(1)}, u32[]{:S(2)}, u32[]{:S(2)}) collective-permute-start(bf16[8,6144]{1,0:T(8,128)(2,1)S(1)} %stacked.1.after_ref.refs_0_), channel_id=1, source_target_pairs={{0,16},{8,24},{16,0},{24,8},{1,17},{9,25},{17,1},{25,9},{2,18},{10... | collective-permute-start | bytes 294920 | tf_op jit(solution)/shard_map/ppermute | solution.py:26
  12.1 5.7 %collective-permute-start.4 = (bf16[8,6144]{1,0:T(8,128)(2,1)S(1)}, bf16[8,6144]{1,0:T(8,128)(2,1)S(1)}, u32[]{:S(2)}, u32[]{:S(2)}) collective-permute-start(bf16[8,6144]{1,0:T(8,128)(2,1)S(1)} %stacked.1.after_ref.refs_0_), channel_id=1, source_target_pairs={{0,24},{8,16},{16,8},{24,0},{1,25},{9,17},{17,9},{25,1},{2,26},{10... | collective-permute-start | bytes 294920 | tf_op jit(solution)/shard_map/ppermute | solution.py:26
  12.3 6.7 %collective-permute-start.5 = (bf16[8,6144]{1,0:T(8,128)(2,1)S(1)}, bf16[8,6144]{1,0:T(8,128)(2,1)S(1)}, u32[]{:S(2)}, u32[]{:S(2)}) collective-permute-start(bf16[8,6144]{1,0:T(8,128)(2,1)S(1)} %stacked.1.after_ref.refs_0_), channel_id=1, source_target_pairs={{0,1},{1,0},{2,3},{3,2},{4,5},{5,4},{6,7},{7,6},{8,9},{9,8},{10,11... | collective-permute-start | bytes 294920 | tf_op jit(solution)/shard_map/ppermute | solution.py:26
  17.8 1.6 %collective-permute-start.8 = (bf16[8,6144]{1,0:T(8,128)(2,1)S(1)}, bf16[8,6144]{1,0:T(8,128)(2,1)S(1)}, u32[]{:S(2)}, u32[]{:S(2)}) collective-permute-start(bf16[8,6144]{1,0:T(8,128)(2,1)S(1)} %collective-permute-done.4.refs_3_), channel_id=1, source_target_pairs={{0,1},{1,0},{2,3},{3,2},{4,5},{5,4},{6,7},{7,6},{8,9},{9,8},{10,11... | collective-permute-start | bytes 294920 | tf_op jit(solution)/shard_map/ppermute | solution.py:26
  18.5 1.3 %collective-permute-start.7 = (bf16[8,6144]{1,0:T(8,128)(2,1)S(1)}, bf16[8,6144]{1,0:T(8,128)(2,1)S(1)}, u32[]{:S(2)}, u32[]{:S(2)}) collective-permute-start(bf16[8,6144]{1,0:T(8,128)(2,1)S(1)} %collective-permute-done.3.refs_2_), channel_id=1, source_target_pairs={{0,1},{1,0},{2,3},{3,2},{4,5},{5,4},{6,7},{7,6},{8,9},{9,8},{10,11... | collective-permute-start | bytes 294920 | tf_op jit(solution)/shard_map/ppermute | solution.py:26
  18.5 1.5 %collective-permute-start.6 = (bf16[8,6144]{1,0:T(8,128)(2,1)S(1)}, bf16[8,6144]{1,0:T(8,128)(2,1)S(1)}, u32[]{:S(2)}, u32[]{:S(2)}) collective-permute-start(bf16[8,6144]{1,0:T(8,128)(2,1)S(1)} %collective-permute-done.2.refs_1_), channel_id=1, source_target_pairs={{0,1},{1,0},{2,3},{3,2},{4,5},{5,4},{6,7},{7,6},{8,9},{9,8},{10,11... | collective-permute-start | bytes 294920 | tf_op jit(solution)/shard_map/ppermute | solution.py:26
  32.7 3.2 %collective-permute-start.9 = (bf16[64,3072]{1,0:T(8,128)(2,1)S(1)}, bf16[64,3072]{1,0:T(8,128)(2,1)S(1)}, u32[]{:S(2)}, u32[]{:S(2)}) collective-permute-start(bf16[64,3072]{1,0:T(8,128)(2,1)S(1)} %get-tuple-element.30), channel_id=1, source_target_pairs={{0,1},{1,0},{2,3},{3,2},{4,5},{5,4},{6,7},{7,6},{8,9},{9,8},{10,11... | collective-permute-start | bytes 1179656 | tf_op jit(solution)/shard_map/ppermute | solution.py:26
  36.0 5.1 %collective-permute-start.10 = (bf16[16,3072]{1,0:T(8,128)(2,1)S(1)}, bf16[16,3072]{1,0:T(8,128)(2,1)S(1)}, u32[]{:S(2)}, u32[]{:S(2)}) collective-permute-start(bf16[16,3072]{1,0:T(8,128)(2,1)S(1)} %get-tuple-element.32), channel_id=1, source_target_pairs={{0,8},{8,0},{16,24},{24,16},{1,9},{9,1},{17,25},{25,17},{2,10},{10... | collective-permute-start | bytes 294920 | tf_op jit(solution)/shard_map/ppermute | solution.py:26
  37.0 5.7 %collective-permute-start.11 = (bf16[16,3072]{1,0:T(8,128)(2,1)S(1)}, bf16[16,3072]{1,0:T(8,128)(2,1)S(1)}, u32[]{:S(2)}, u32[]{:S(2)}) collective-permute-start(bf16[16,3072]{1,0:T(8,128)(2,1)S(1)} %get-tuple-element.33), channel_id=1, source_target_pairs={{0,16},{8,24},{16,0},{24,8},{1,17},{9,25},{17,1},{25,9},{2,18},{10... | collective-permute-start | bytes 294920 | tf_op jit(solution)/shard_map/ppermute | solution.py:26
  38.3 5.5 %collective-permute-start.12 = (bf16[16,3072]{1,0:T(8,128)(2,1)S(1)}, bf16[16,3072]{1,0:T(8,128)(2,1)S(1)}, u32[]{:S(2)}, u32[]{:S(2)}) collective-permute-start(bf16[16,3072]{1,0:T(8,128)(2,1)S(1)} %get-tuple-element.34), channel_id=1, source_target_pairs={{0,24},{8,16},{16,8},{24,0},{1,25},{9,17},{17,9},{25,1},{2,26},{10... | collective-permute-start | bytes 294920 | tf_op jit(solution)/shard_map/ppermute | solution.py:26

commit v7 on v6

--- a/solution.py
+++ b/solution.py
@@ -95,7 +95,8 @@
             for core in range(hids):
                 yield lane * hids + core, (lane ^ (t * hids + core)) * hids + core
 
-    return [lax.ppermute(piece, ("regroup", "hid"), list(pairs(t))) for t, piece in enumerate(pieces)]
+    far = {t: lax.ppermute(pieces[t], ("regroup", "hid"), list(pairs(t))) for t in reversed(range(count))}
+    return [far[t] for t in range(count)]
 
 
 def stack_kernel(*refs):
@@ -283,7 +284,7 @@
 
     for side in range(1, hids):
 
-        @pl.loop(0, wide)
+        @pl.loop(0, wide, unroll=wide)
         def _(c):
             total = None
             for k in range(deep):

time: 44.8 us -> 44.8 us (level)
  no operation moved by 1% of the time
where the time goes in v7:
time: 44.8 us; the launch traced here: 44.6 us
  Pallas kernels  21.4 us (48%)
  starting transfers between devices  15.4 us (34%)
  waiting for transfers between devices  7.72 us (17%)
    pallas_call x1, Pallas kernels, ffn(): pl.pallas_call(functools.partial(ffn_kernel, blocks, hids, (slots, part,...  12.7 us
    ppermute x11, starting transfers between devices, exchange(): return lax.ppermute(array, axis, [(i, i ^ step) for i in range(count)])  10.5 us
    ppermute x11, waiting for transfers between devices, exchange(): return lax.ppermute(array, axis, [(i, i ^ step) for i in range(count)])  5.57 us
    ppermute x2, starting transfers between devices, to_lanes(): lax.ppermute(pieces[t], ('regroup', 'hid'), list(pairs(t)))  4.9 us
    pallas_call x1, Pallas kernels, early(): pl.pallas_call(functools.partial(early_kernel, width), out_shape=pltpu.VM...  3.39 us
    pallas_call x1, Pallas kernels, kept_part(): pl.pallas_call(kept_kernel, out_shape=jax.ShapeDtypeStruct((rows, width),...  2.73 us
    ppermute x2, waiting for transfers between devices, to_lanes(): lax.ppermute(pieces[t], ('regroup', 'hid'), list(pairs(t)))  2.15 us
    pallas_call x1, Pallas kernels, norm(): pl.pallas_call(functools.partial(norm_kernel, lanes, hids), out_shape=(ja...  1.64 us
  transfers between devices with their start and end apart: 13, of which 8 were waited for; matrix products, arithmetic and copies ran while one was open for 0% of the time, Pallas kernels for 14%

profile of v7, /device:TPU:0, one launch (start us, length us, event | category | flops | bytes accessed | tf_op | source)
XLA Modules:
  0.0 44.6 jit_solution(12652797832713702387)
XLA Ops:
  0.0 0.0 copy-start
  0.0 1.6 %norm.1 = (bf16[4,6144]{1,0:T(4,128)(2,1)S(1)}, bf16[4,6144]{1,0:T(4,128)(2,1)S(1)}) custom-call(bf16[16,6144]{1,0:T(8,128)(2,1)} %refs_0_.1, s32[16]{0:T(128)} %refs_1_.1, s32[1,16]{1,0:T(1,128)} %refs_2_.1, f32[8,6144]{1,0:T(8,128)} %refs_3_.1), custom_call_target="tpu_custom_call" | custom-call | bytes 50331648 | tf_op jit(solution)/shard_map/norm/pallas_call | solution.py:69
  1.6 0.8 %collective-permute-start = (bf16[4,6144]{1,0:T(4,128)(2,1)S(1)}, bf16[4,6144]{1,0:T(4,128)(2,1)S(1)}, u32[]{:S(2)}, u32[]{:S(2)}) collective-permute-start(bf16[4,6144]{1,0:T(4,128)(2,1)S(1)} %get-tuple-element.20), channel_id=1, source_target_pairs={{0,0},{1,3},{2,2},{3,1},{4,4},{5,7},{6,6},{7,5},{8,8},{9,11},{10,1... | collective-permute-start | bytes 147464 | tf_op jit(solution)/shard_map/ppermute | solution.py:98
  2.4 4.1 %collective-permute-start.1 = (bf16[4,6144]{1,0:T(4,128)(2,1)S(1)}, bf16[4,6144]{1,0:T(4,128)(2,1)S(1)}, u32[]{:S(2)}, u32[]{:S(2)}) collective-permute-start(bf16[4,6144]{1,0:T(4,128)(2,1)S(1)} %get-tuple-element.21), channel_id=1, source_target_pairs={{0,4},{1,7},{2,6},{3,5},{4,0},{5,3},{6,2},{7,1},{8,12},{9,15},{10,... | collective-permute-start | bytes 147464 | tf_op jit(solution)/shard_map/ppermute | solution.py:98
  6.5 0.0 collective-permute-done.refs_0_
  6.6 2.2 %collective-permute-done.1.refs_1_ = bf16[4,6144]{1,0:T(4,128)(2,1)S(1)} collective-permute-done((bf16[4,6144]{1,0:T(4,128)(2,1)S(1)}, bf16[4,6144]{1,0:T(4,128)(2,1)S(1)}, u32[]{:S(2)}, u32[]{:S(2)}) %collective-permute-start.1) | collective-permute-done | bytes 49184 | tf_op jit(solution)/shard_map/ppermute | solution.py:98
  8.7 1.8 %collective-permute-start.2 = (bf16[8,6144]{1,0:T(8,128)(2,1)S(1)}, bf16[8,6144]{1,0:T(8,128)(2,1)S(1)}, u32[]{:S(2)}, u32[]{:S(2)}) collective-permute-start(bf16[8,6144]{1,0:T(8,128)(2,1)S(1)} %stacked.1.after_ref.refs_0_), channel_id=1, source_target_pairs={{0,8},{8,0},{16,24},{24,16},{1,9},{9,1},{17,25},{25,17},{2,10},{10... | collective-permute-start | bytes 294920 | tf_op jit(solution)/shard_map/ppermute | solution.py:26
  10.5 1.5 %collective-permute-start.3 = (bf16[8,6144]{1,0:T(8,128)(2,1)S(1)}, bf16[8,6144]{1,0:T(8,128)(2,1)S(1)}, u32[]{:S(2)}, u32[]{:S(2)}) collective-permute-start(bf16[8,6144]{1,0:T(8,128)(2,1)S(1)} %stacked.1.after_ref.refs_0_), channel_id=1, source_target_pairs={{0,16},{8,24},{16,0},{24,8},{1,17},{9,25},{17,1},{25,9},{2,18},{10... | collective-permute-start | bytes 294920 | tf_op jit(solution)/shard_map/ppermute | solution.py:26
  12.1 0.2 collective-permute-start.4
  12.3 1.8 %collective-permute-start.5 = (bf16[8,6144]{1,0:T(8,128)(2,1)S(1)}, bf16[8,6144]{1,0:T(8,128)(2,1)S(1)}, u32[]{:S(2)}, u32[]{:S(2)}) collective-permute-start(bf16[8,6144]{1,0:T(8,128)(2,1)S(1)} %stacked.1.after_ref.refs_0_), channel_id=1, source_target_pairs={{0,1},{1,0},{2,3},{3,2},{4,5},{5,4},{6,7},{7,6},{8,9},{9,8},{10,11... | collective-permute-start | bytes 294920 | tf_op jit(solution)/shard_map/ppermute | solution.py:26
  14.1 3.4 %early.1.refs_9_ = bf16[2048,2048]{1,0:T(8,128)(2,1)S(1)} custom-call(bf16[8,6144]{1,0:T(8,128)(2,1)S(1)} %stacked.1.after_ref.refs_0_, bf16[6144,2048]{1,0:T(8,128)(2,1)} %refs_10_.1), custom_call_target="tpu_custom_call" | custom-call | bytes 8388608 | tf_op jit(solution)/shard_map/early/pallas_call | solution.py:143
  17.5 0.0 collective-permute-done.2.refs_1_
  17.5 0.0 collective-permute-done.3.refs_2_
  17.5 0.3 collective-permute-done.4.refs_3_
  17.8 0.7 %collective-permute-start.8 = (bf16[8,6144]{1,0:T(8,128)(2,1)S(1)}, bf16[8,6144]{1,0:T(8,128)(2,1)S(1)}, u32[]{:S(2)}, u32[]{:S(2)}) collective-permute-start(bf16[8,6144]{1,0:T(8,128)(2,1)S(1)} %collective-permute-done.4.refs_3_), channel_id=1, source_target_pairs={{0,1},{1,0},{2,3},{3,2},{4,5},{5,4},{6,7},{7,6},{8,9},{9,8},{10,11... | collective-permute-start | bytes 294920 | tf_op jit(solution)/shard_map/ppermute | solution.py:26
  18.5 0.0 collective-permute-start.7
  18.5 0.5 %collective-permute-start.6 = (bf16[8,6144]{1,0:T(8,128)(2,1)S(1)}, bf16[8,6144]{1,0:T(8,128)(2,1)S(1)}, u32[]{:S(2)}, u32[]{:S(2)}) collective-permute-start(bf16[8,6144]{1,0:T(8,128)(2,1)S(1)} %collective-permute-done.2.refs_1_), channel_id=1, source_target_pairs={{0,1},{1,0},{2,3},{3,2},{4,5},{5,4},{6,7},{7,6},{8,9},{9,8},{10,11... | collective-permute-start | bytes 294920 | tf_op jit(solution)/shard_map/ppermute | solution.py:26
  19.0 0.0 collective-permute-done.5.refs_4_
  19.0 0.4 collective-permute-done.8.refs_7_
  19.4 0.4 collective-permute-done.7.refs_6_
  19.8 0.2 collective-permute-done.6.refs_5_
  19.9 0.0 copy-done
  19.9 12.7 %ffn.1 = (bf16[64,2048]{1,0:T(8,128)(2,1)S(1)}, bf16[2048,2048]{1,0:T(8,128)(2,1)S(1)}, bf16[64,3072]{1,0:T(8,128)(2,1)S(1)}) custom-call(bf16[8,6144]{1,0:T(8,128)(2,1)S(1)} %stacked.1.after_ref.refs_0_, bf16[8,6144]{1,0:T(8,128)(2,1)S(1)} %collective-permute-done.2.refs_1_, bf16[8,6144]{1,0:T(8,128)(2,1)S(1)} %collective-permute-done.3.refs_2_, ...), custom_call_target="tpu_custom_call" | custom-call | flops 4026531840 | bytes 50331648 | tf_op jit(solution)/shard_map/ffn/pallas_call | solution.py:321
  32.7 0.4 collective-permute-start.9
  33.1 2.7 %kept_part.1.refs_0_ = f32[64,3072]{1,0:T(8,128)S(1)} custom-call(bf16[64,2048]{1,0:T(8,128)(2,1)S(1)} %get-tuple-element.28.hidden_ref, bf16[2048,2048]{1,0:T(8,128)(2,1)S(1)} %get-tuple-element.29.kept_ref, bf16[2048,6144]{1,0:T(8,128)(2,1)} %down_ref.1), custom_call_target="tpu_custom_call" | custom-call | flops 805306368 | bytes 12582912 | tf_op jit(solution)/shard_map/kept_part/pallas_call | solution.py:382
  35.8 0.0 collective-permute-done.9.refs_1_
  35.8 0.1 hid_sum.1
  35.9 1.1 %collective-permute-start.10 = (bf16[16,3072]{1,0:T(8,128)(2,1)S(1)}, bf16[16,3072]{1,0:T(8,128)(2,1)S(1)}, u32[]{:S(2)}, u32[]{:S(2)}) collective-permute-start(bf16[16,3072]{1,0:T(8,128)(2,1)S(1)} %get-tuple-element.32), channel_id=1, source_target_pairs={{0,8},{8,0},{16,24},{24,16},{1,9},{9,1},{17,25},{25,17},{2,10},{10... | collective-permute-start | bytes 294920 | tf_op jit(solution)/shard_map/ppermute | solution.py:26
  37.0 1.3 %collective-permute-start.11 = (bf16[16,3072]{1,0:T(8,128)(2,1)S(1)}, bf16[16,3072]{1,0:T(8,128)(2,1)S(1)}, u32[]{:S(2)}, u32[]{:S(2)}) collective-permute-start(bf16[16,3072]{1,0:T(8,128)(2,1)S(1)} %get-tuple-element.33), channel_id=1, source_target_pairs={{0,16},{8,24},{16,0},{24,8},{1,17},{9,25},{17,1},{25,9},{2,18},{10... | collective-permute-start | bytes 294920 | tf_op jit(solution)/shard_map/ppermute | solution.py:26
  38.3 1.2 %collective-permute-start.12 = (bf16[16,3072]{1,0:T(8,128)(2,1)S(1)}, bf16[16,3072]{1,0:T(8,128)(2,1)S(1)}, u32[]{:S(2)}, u32[]{:S(2)}) collective-permute-start(bf16[16,3072]{1,0:T(8,128)(2,1)S(1)} %get-tuple-element.34), channel_id=1, source_target_pairs={{0,24},{8,16},{16,8},{24,0},{1,25},{9,17},{17,9},{25,1},{2,26},{10... | collective-permute-start | bytes 294920 | tf_op jit(solution)/shard_map/ppermute | solution.py:26
  39.5 1.5 %collective-permute-done.10.refs_1_ = bf16[16,3072]{1,0:T(8,128)(2,1)S(1)} collective-permute-done((bf16[16,3072]{1,0:T(8,128)(2,1)S(1)}, bf16[16,3072]{1,0:T(8,128)(2,1)S(1)}, u32[]{:S(2)}, u32[]{:S(2)}) %collective-permute-start.10) | collective-permute-done | bytes 98336 | tf_op jit(solution)/shard_map/ppermute | solution.py:26
  41.0 1.7 %collective-permute-done.11.refs_2_ = bf16[16,3072]{1,0:T(8,128)(2,1)S(1)} collective-permute-done((bf16[16,3072]{1,0:T(8,128)(2,1)S(1)}, bf16[16,3072]{1,0:T(8,128)(2,1)S(1)}, u32[]{:S(2)}, u32[]{:S(2)}) %collective-permute-start.11) | collective-permute-done | bytes 98336 | tf_op jit(solution)/shard_map/ppermute | solution.py:26
  42.7 1.1 %collective-permute-done.12.refs_3_ = bf16[16,3072]{1,0:T(8,128)(2,1)S(1)} collective-permute-done((bf16[16,3072]{1,0:T(8,128)(2,1)S(1)}, bf16[16,3072]{1,0:T(8,128)(2,1)S(1)}, u32[]{:S(2)}, u32[]{:S(2)}) %collective-permute-start.12) | collective-permute-done | bytes 98336 | tf_op jit(solution)/shard_map/ppermute | solution.py:26
  43.8 0.8 %blk_sum.1 = bf16[16,3072]{1,0:T(8,128)(2,1)} custom-call(f32[16,3072]{1,0:T(8,128)S(1)} %get-tuple-element.31.refs_0_, bf16[16,3072]{1,0:T(8,128)(2,1)S(1)} %collective-permute-done.10.refs_1_, bf16[16,3072]{1,0:T(8,128)(2,1)S(1)} %collective-permute-done.11.refs_2_, bf16[16,3072]{1,0:T(8,128)(2,1)S(1)} %collective-permute-done.12.refs_3_), custom_call_target="tpu_custom_call" | custom-call | tf_op jit(solution)/shard_map/blk_sum/pallas_call | solution.py:450
  (1 shorter events, 0.0 us)
Async XLA Ops:
  0.0 19.9 %copy-start = (bf16[6144,2048]{1,0:T(8,128)(2,1)S(1)}, bf16[6144,2048]{1,0:T(8,128)(2,1)}, u32[]{:S(2)}) copy-start(bf16[6144,2048]{1,0:T(8,128)(2,1)} %refs_8_.1) | copy-start | bytes 75497472
  1.6 4.9 %collective-permute-start = (bf16[4,6144]{1,0:T(4,128)(2,1)S(1)}, bf16[4,6144]{1,0:T(4,128)(2,1)S(1)}, u32[]{:S(2)}, u32[]{:S(2)}) collective-permute-start(bf16[4,6144]{1,0:T(4,128)(2,1)S(1)} %get-tuple-element.20), channel_id=1, source_target_pairs={{0,0},{1,3},{2,2},{3,1},{4,4},{5,7},{6,6},{7,5},{8,8},{9,11},{10,1... | collective-permute-start | bytes 147464 | tf_op jit(solution)/shard_map/ppermute | solution.py:98
  2.4 6.3 %collective-permute-start.1 = (bf16[4,6144]{1,0:T(4,128)(2,1)S(1)}, bf16[4,6144]{1,0:T(4,128)(2,1)S(1)}, u32[]{:S(2)}, u32[]{:S(2)}) collective-permute-start(bf16[4,6144]{1,0:T(4,128)(2,1)S(1)} %get-tuple-element.21), channel_id=1, source_target_pairs={{0,4},{1,7},{2,6},{3,5},{4,0},{5,3},{6,2},{7,1},{8,12},{9,15},{10,... | collective-permute-start | bytes 147464 | tf_op jit(solution)/shard_map/ppermute | solution.py:98
  8.7 8.7 %collective-permute-start.2 = (bf16[8,6144]{1,0:T(8,128)(2,1)S(1)}, bf16[8,6144]{1,0:T(8,128)(2,1)S(1)}, u32[]{:S(2)}, u32[]{:S(2)}) collective-permute-start(bf16[8,6144]{1,0:T(8,128)(2,1)S(1)} %stacked.1.after_ref.refs_0_), channel_id=1, source_target_pairs={{0,8},{8,0},{16,24},{24,16},{1,9},{9,1},{17,25},{25,17},{2,10},{10... | collective-permute-start | bytes 294920 | tf_op jit(solution)/shard_map/ppermute | solution.py:26
  10.5 7.0 %collective-permute-start.3 = (bf16[8,6144]{1,0:T(8,128)(2,1)S(1)}, bf16[8,6144]{1,0:T(8,128)(2,1)S(1)}, u32[]{:S(2)}, u32[]{:S(2)}) collective-permute-start(bf16[8,6144]{1,0:T(8,128)(2,1)S(1)} %stacked.1.after_ref.refs_0_), channel_id=1, source_target_pairs={{0,16},{8,24},{16,0},{24,8},{1,17},{9,25},{17,1},{25,9},{2,18},{10... | collective-permute-start | bytes 294920 | tf_op jit(solution)/shard_map/ppermute | solution.py:26
  12.1 5.7 %collective-permute-start.4 = (bf16[8,6144]{1,0:T(8,128)(2,1)S(1)}, bf16[8,6144]{1,0:T(8,128)(2,1)S(1)}, u32[]{:S(2)}, u32[]{:S(2)}) collective-permute-start(bf16[8,6144]{1,0:T(8,128)(2,1)S(1)} %stacked.1.after_ref.refs_0_), channel_id=1, source_target_pairs={{0,24},{8,16},{16,8},{24,0},{1,25},{9,17},{17,9},{25,1},{2,26},{10... | collective-permute-start | bytes 294920 | tf_op jit(solution)/shard_map/ppermute | solution.py:26
  12.3 6.7 %collective-permute-start.5 = (bf16[8,6144]{1,0:T(8,128)(2,1)S(1)}, bf16[8,6144]{1,0:T(8,128)(2,1)S(1)}, u32[]{:S(2)}, u32[]{:S(2)}) collective-permute-start(bf16[8,6144]{1,0:T(8,128)(2,1)S(1)} %stacked.1.after_ref.refs_0_), channel_id=1, source_target_pairs={{0,1},{1,0},{2,3},{3,2},{4,5},{5,4},{6,7},{7,6},{8,9},{9,8},{10,11... | collective-permute-start | bytes 294920 | tf_op jit(solution)/shard_map/ppermute | solution.py:26
  17.8 1.6 %collective-permute-start.8 = (bf16[8,6144]{1,0:T(8,128)(2,1)S(1)}, bf16[8,6144]{1,0:T(8,128)(2,1)S(1)}, u32[]{:S(2)}, u32[]{:S(2)}) collective-permute-start(bf16[8,6144]{1,0:T(8,128)(2,1)S(1)} %collective-permute-done.4.refs_3_), channel_id=1, source_target_pairs={{0,1},{1,0},{2,3},{3,2},{4,5},{5,4},{6,7},{7,6},{8,9},{9,8},{10,11... | collective-permute-start | bytes 294920 | tf_op jit(solution)/shard_map/ppermute | solution.py:26
  18.5 1.3 %collective-permute-start.7 = (bf16[8,6144]{1,0:T(8,128)(2,1)S(1)}, bf16[8,6144]{1,0:T(8,128)(2,1)S(1)}, u32[]{:S(2)}, u32[]{:S(2)}) collective-permute-start(bf16[8,6144]{1,0:T(8,128)(2,1)S(1)} %collective-permute-done.3.refs_2_), channel_id=1, source_target_pairs={{0,1},{1,0},{2,3},{3,2},{4,5},{5,4},{6,7},{7,6},{8,9},{9,8},{10,11... | collective-permute-start | bytes 294920 | tf_op jit(solution)/shard_map/ppermute | solution.py:26
  18.5 1.5 %collective-permute-start.6 = (bf16[8,6144]{1,0:T(8,128)(2,1)S(1)}, bf16[8,6144]{1,0:T(8,128)(2,1)S(1)}, u32[]{:S(2)}, u32[]{:S(2)}) collective-permute-start(bf16[8,6144]{1,0:T(8,128)(2,1)S(1)} %collective-permute-done.2.refs_1_), channel_id=1, source_target_pairs={{0,1},{1,0},{2,3},{3,2},{4,5},{5,4},{6,7},{7,6},{8,9},{9,8},{10,11... | collective-permute-start | bytes 294920 | tf_op jit(solution)/shard_map/ppermute | solution.py:26
  32.7 3.2 %collective-permute-start.9 = (bf16[64,3072]{1,0:T(8,128)(2,1)S(1)}, bf16[64,3072]{1,0:T(8,128)(2,1)S(1)}, u32[]{:S(2)}, u32[]{:S(2)}) collective-permute-start(bf16[64,3072]{1,0:T(8,128)(2,1)S(1)} %get-tuple-element.30), channel_id=1, source_target_pairs={{0,1},{1,0},{2,3},{3,2},{4,5},{5,4},{6,7},{7,6},{8,9},{9,8},{10,11... | collective-permute-start | bytes 1179656 | tf_op jit(solution)/shard_map/ppermute | solution.py:26
  35.9 5.1 %collective-permute-start.10 = (bf16[16,3072]{1,0:T(8,128)(2,1)S(1)}, bf16[16,3072]{1,0:T(8,128)(2,1)S(1)}, u32[]{:S(2)}, u32[]{:S(2)}) collective-permute-start(bf16[16,3072]{1,0:T(8,128)(2,1)S(1)} %get-tuple-element.32), channel_id=1, source_target_pairs={{0,8},{8,0},{16,24},{24,16},{1,9},{9,1},{17,25},{25,17},{2,10},{10... | collective-permute-start | bytes 294920 | tf_op jit(solution)/shard_map/ppermute | solution.py:26
  37.0 5.7 %collective-permute-start.11 = (bf16[16,3072]{1,0:T(8,128)(2,1)S(1)}, bf16[16,3072]{1,0:T(8,128)(2,1)S(1)}, u32[]{:S(2)}, u32[]{:S(2)}) collective-permute-start(bf16[16,3072]{1,0:T(8,128)(2,1)S(1)} %get-tuple-element.33), channel_id=1, source_target_pairs={{0,16},{8,24},{16,0},{24,8},{1,17},{9,25},{17,1},{25,9},{2,18},{10... | collective-permute-start | bytes 294920 | tf_op jit(solution)/shard_map/ppermute | solution.py:26
  38.3 5.5 %collective-permute-start.12 = (bf16[16,3072]{1,0:T(8,128)(2,1)S(1)}, bf16[16,3072]{1,0:T(8,128)(2,1)S(1)}, u32[]{:S(2)}, u32[]{:S(2)}) collective-permute-start(bf16[16,3072]{1,0:T(8,128)(2,1)S(1)} %get-tuple-element.34), channel_id=1, source_target_pairs={{0,24},{8,16},{16,8},{24,0},{1,25},{9,17},{17,9},{25,1},{2,26},{10... | collective-permute-start | bytes 294920 | tf_op jit(solution)/shard_map/ppermute | solution.py:26
